TPU v7x, 128 devices: a whole 4x4x4 slice. The times are simulated.
128 devices in a mesh: param: 8 (over y, core), ex: 16 (over z, x).
Axes of the slice: x: 4, y: 4, z: 4, core: 2. Of those that a mesh axis runs over, the one named last changes fastest.
Arguments:
- activations: bfloat16 [1024, 128, 8192], P('ex', None, 'param'), may hold values from -8 to 8
- cotangents: bfloat16 [1024, 128, 64], P('ex'), may hold values from -8 to 8
- token_ids: int32 [1024, 128], P('ex'), may hold values from 0 to 128255, as said below
- signs: int32 [64, 8192], P(None, 'param'), may hold values from -1 to 1, as said below
- select: int32 [32768], replicated, may hold values from 0 to 524287, as said below
Outputs:
- features: float32 [1024, 32768], P('ex', 'param')
- gram: float32 [1024, 1024], P('ex')
Inputs may be any that keep to these rules, and one draw needn't show every extreme that they name: `token_ids`: in each example the nonzero ids come first and zeros fill the rest; at least 32 positions of every example are nonzero. `signs`: every entry is 1 or -1. `select`: the 32768 entries are distinct.
All inputs are finite; a program needn't handle non-finite values.
Results may differ from a plain program's by a relative error of at most 0.0003.
Values sent between devices are 32-bit elements; how exact they have to be, the bound alone decides.
No kernel may reach another device: no remote copies, remote signals or barrier semaphores. Data moves between devices by JAX's collectives and lax.ppermute only.
A program may use at most 192 MiB of HBM per device.

v0:
```python
import math

import jax
import jax.numpy as jnp
from jax import lax
from jax.sharding import PartitionSpec as P

D = 8192
SLAB = 64
TOKS = 128
K = 32768


def walsh_table(table_order):
    row_index = lax.broadcasted_iota(jnp.int32, (table_order, table_order), 0)
    column_index = lax.broadcasted_iota(jnp.int32, (table_order, table_order), 1)
    common_bits = row_index & column_index
    parity = jnp.zeros((table_order, table_order), jnp.int32)
    for bit_index in range(table_order.bit_length() - 1):
        parity = parity ^ common_bits >> bit_index & 1
    return (1 - 2 * parity).astype(jnp.float32)


def body(activations, cotangents, token_ids, signs, select):
    highest = lax.Precision.HIGHEST
    count_ex = activations.shape[0]
    local_width = activations.shape[2]
    slab_rows = cotangents.shape[2]
    live_mask = token_ids != 0
    masked = jnp.where(live_mask[:, :, None], cotangents, jnp.zeros((), cotangents.dtype))
    gradient = jnp.einsum(
        "etr,etc->erc", masked, activations, preferred_element_type=jnp.float32
    ) * (1.0 / math.sqrt(TOKS))
    flipped = gradient * signs.astype(jnp.float32)[None, :, :]
    mixed = jnp.einsum("rs,esc->erc", walsh_table(slab_rows), flipped, precision=highest)
    local_values = jnp.einsum("erc,cd->erd", mixed, walsh_table(local_width), precision=highest)
    factor = 1.0 / math.sqrt(SLAB * D)
    my_index = lax.axis_index("param")
    section_count = lax.axis_size("param").bit_length() - 1
    column = select % D
    owner_block = column // local_width
    position = select // D * local_width + column % local_width
    shared = owner_block & my_index
    parity = jnp.zeros_like(shared)
    for bit_index in range(section_count):
        parity = parity ^ shared >> bit_index & 1
    weight = (1 - 2 * parity).astype(jnp.float32) * factor
    partial_term = jnp.take(local_values.reshape(count_ex, -1), position, axis=1) * weight[None, :]
    features = lax.psum_scatter(partial_term, "param", scatter_dimension=1, tiled=True)
    tile_block = jnp.einsum(
        "ek,fk->ef", features, lax.all_gather(features, "ex", axis=0, tiled=True), precision=highest
    )
    gram = lax.psum(tile_block, "param") / K
    return (features, gram)


def solution(mesh):
    return jax.shard_map(
        body,
        mesh=mesh,
        in_specs=(
            P("ex", None, "param"),
            P("ex", None, None),
            P("ex", None),
            P(None, "param"),
            P(),
        ),
        out_specs=(P("ex", "param"), P("ex", None)),
        check_vma=False,
    )
```

profile of v0, /device:TPU:1, one launch (start us, length us, event | category | flops | bytes accessed | tf_op | source)
XLA Modules:
  0.0 562.5 jit_solution(14893608860567406003)
XLA Ops:
  7.2 0.0 copy-start.2
  7.2 0.0 copy-start.4
  7.2 0.0 copy-start.3
  7.2 0.0 copy-start.1
  7.2 0.0 reduce-scatter.2.cloned.1.call-start
  7.3 4.5 fusion.116
  11.8 0.0 copy-done.2
  11.8 0.2 compare_and_fusion
  12.1 0.0 copy-done.4
  12.1 0.0 copy-done.3
  12.1 0.0 copy-done.1
  12.1 13.9 %fusion.51 = f32[64,64,1024]{2,1,0:T(8,128)} fusion(bf16[64,128,1024]{2,1,0:T(8,128)(2,1)} %param.5, bf16[64,128,64]{1,2,0:T(8,128)(2,1)S(1)} %copy-done.1, pred[64,128]{1,0:T(8,128)(4,1)S(1)} %broadcast_compare_fusion), kind=kOutput, calls=%fused_computation.53 | convolution fusion | flops 1074266112 | bytes 34611200 | tf_op jit(solution)/shard_map/etr,etc->erc/dot_general | solution.py:31
  26.0 25.6 %fusion.2 = f32[64,1024,64]{1,2,0:T(8,128)} fusion(f32[64,64,1024]{2,1,0:T(8,128)} %fusion.51, f32[64,1024]{1,0:T(8,128)S(1)} %convert_multiply_fusion), kind=kOutput, calls=%fused_computation.4 | convolution fusion | flops 3225505792 | bytes 33816576 | tf_op jit(solution)/shard_map/rs,esc->erc/dot_general | solution.py:35
  51.6 58.5 %fusion = f32[64,64,1024]{2,1,0:T(8,128)} fusion(f32[64,1024,64]{1,2,0:T(8,128)} %fusion.2, f32[1024,1024,1]{1,0,2:T(8,128)S(1)} %fusion.116), kind=kOutput, calls=%fused_computation.1 | convolution fusion | flops 51539607552 | bytes 37748736 | tf_op jit(solution)/shard_map/erc,cd->erd/dot_general | solution.py:36
  110.1 23.3 %copy.12 = f32[64,64,1024]{0,2,1:T(8,128)} copy(f32[64,64,1024]{2,1,0:T(8,128)} %fusion) | data formatting | bytes 33554432 | tf_op jit(solution)/shard_map/reshape | solution.py:48
  133.4 0.2 convert_multiply_fusion.1
  133.6 119.0 %gather_fusion = f32[32768,64]{1,0:T(8,128)} fusion(f32[64,65536]{0,1:T(8,128)} %bitcast.20, s32[32768]{0:T(1024)S(1)} %broadcast_clamp_fusion), kind=kCustom, calls=%fused_computation | custom fusion | bytes 16908288 | tf_op jit(solution)/shard_map/jit(_take)/gather | solution.py:48
  252.6 13.2 %multiply_bitcast_fusion = f32[64,32768]{0,1:T(8,128)} fusion(f32[32768,64]{1,0:T(8,128)} %gather_fusion, f32[32768]{0:T(1024)S(1)} %convert_multiply_fusion.1, pred[32768]{0:T(1024)(128)(4,1)S(1)} %get-tuple-element.6), kind=kLoop, calls=%fused_computation.3 | loop fusion | flops 4194304 | bytes 16941056 | tf_op jit(solution)/shard_map/mul | solution.py:48
  265.8 0.0 reduce-scatter.2.cloned.1.call-update
  265.8 0.0 all-gather.2.cloned.1.call-start
  265.9 94.5 %reduce-scatter.2.cloned.1.call-done = f32[64,4096]{0,1:T(8,128)} async-done(((f32[64,32768]{0,1:T(8,128)}), f32[64,4096]{0,1:T(8,128)}) %reduce-scatter.2.cloned.1.call-update) | async-done | bytes 1048592 | tf_op jit(solution)/shard_map/reduce_scatter | solution.py:49
  360.4 0.0 copy-start
  360.4 3.3 copy.11
  363.7 0.0 all-gather.2.cloned.1.call-update
  363.7 0.0 all-reduce.2.cloned.1.call-start
  363.8 111.7 %all-gather.2.cloned.1.call-done = f32[1024,4096]{1,0:T(8,128)} async-done(((f32[64,4096]{1,0:T(8,128)}), f32[1024,4096]{1,0:T(8,128)}) %all-gather.2.cloned.1.call-update) | async-done | bytes 16777232 | tf_op jit(solution)/shard_map/all_gather | solution.py:51
  475.5 0.0 copy-done
  475.5 20.8 %fusion.109 = f32[64,1024]{1,0:T(8,128)} fusion(f32[64,4096]{0,1:T(8,128)S(1)} %copy-done, f32[1024,4096]{1,0:T(8,128)} %all-gather.2.cloned.1.call-done), kind=kOutput, calls=%fused_computation.130 | convolution fusion | flops 3221225472 | bytes 18087936 | tf_op jit(solution)/shard_map/ek,fk->ef/dot_general | solution.py:50
  496.2 0.0 all-reduce.2.cloned.1.call-update
  496.2 57.6 %all-reduce.2.cloned.1.call-done = f32[64,1024]{1,0:T(8,128)} async-done(((f32[64,1024]{1,0:T(8,128)}), f32[64,1024]{1,0:T(8,128)}) %all-reduce.2.cloned.1.call-update) | async-done | bytes 262160 | tf_op jit(solution)/shard_map/psum | solution.py:53
  553.8 1.7 broadcast_multiply_fusion
  (3 shorter events, 0.1 us)
Async XLA Ops:
  7.2 4.6 copy-start.2
  7.2 4.9 copy-start.4
  7.2 4.9 copy-start.3
  7.2 4.9 copy-start.1
  7.2 353.2 %reduce-scatter.2.cloned.1.call-start = ((), (), s32[]{:S(2)}) async-start(), calls=%async_computation.1 | async-start | bytes 18874368 | tf_op jit(solution)/shard_map/reduce_scatter | solution.py:49
  265.8 209.6 %all-gather.2.cloned.1.call-start = ((), (), s32[]{:S(2)}) async-start(), calls=%async_computation.2 | async-start | bytes 17825792 | tf_op jit(solution)/shard_map/all_gather | solution.py:51
  360.4 115.1 %copy-start = (f32[64,4096]{0,1:T(8,128)S(1)}, f32[64,4096]{0,1:T(8,128)}, u32[]{:S(2)}) copy-start(f32[64,4096]{0,1:T(8,128)} %reduce-scatter.2.cloned.1.call-done) | copy-start | bytes 3145732
  363.7 190.1 %all-reduce.2.cloned.1.call-start = ((), (), s32[]{:S(2)}) async-start(), calls=%async_computation.3 | async-start | bytes 524288 | tf_op jit(solution)/shard_map/psum | solution.py:53
Sparse Core Ops, SparseCore 0:
  265.9 94.3 reduce-scatter.1
  363.8 111.5 all-gather.1
  496.4 57.4 all-reduce.1
where the time goes:
time: 570 us; the launch traced here: 562 us
  waiting for transfers between devices  264 us (46%)
  local copies, waits for them, and re-layouts  146 us (26%)
  matrix products  119 us (21%)
  other arithmetic  19.9 us (3%)
  between operations  14.3 us (3%)
    gather x1, local copies, waits for them, and re-layouts, body(): jnp.take(local_values.reshape(count_ex, -1), position, axis=1)  119 us
    all_gather x1, waiting for transfers between devices, body(): lax.all_gather(features, 'ex', axis=0, tiled=True)  112 us
    reduce_scatter x1, waiting for transfers between devices, body(): lax.psum_scatter(partial_term, 'param', scatter_dimension=1, tiled=True)  94.5 us
    dot_general x1, matrix products, body(): jnp.einsum('erc,cd->erd', mixed, walsh_table(local_width), precision=high...  58.5 us
    psum x1, waiting for transfers between devices, body(): gram = lax.psum(tile_block, 'param') / K  57.6 us
    dot_general x1, matrix products, body(): jnp.einsum('rs,esc->erc', walsh_table(slab_rows), flipped, precision=high...  25.6 us
    reshape x1, local copies, waits for them, and re-layouts, body(): local_values.reshape(count_ex, -1)  23.3 us
    dot_general x1, matrix products, body(): jnp.einsum('ek,fk->ef', features, lax.all_gather(features, 'ex', axis=0,...  20.8 us
  transfers between devices with their start and end apart: 3, of which 3 were waited for; matrix products, arithmetic and copies ran while one was open for 0% of the time, Pallas kernels for 0%

commit v1 on v0

v1 whole, which is shorter than its diff:
```python
import functools
import math

import jax
import jax.numpy as jnp
from jax import lax
from jax.experimental import pallas as pl
from jax.experimental.pallas import tpu as pltpu
from jax.sharding import PartitionSpec as P

D = 8192
SLAB = 64
TOKS = 128
K = 32768
LANES = 128
STEP_EX = 8
TAP = 256


def walsh_table(table_order):
    row_index = lax.broadcasted_iota(jnp.int32, (table_order, table_order), 0)
    column_index = lax.broadcasted_iota(jnp.int32, (table_order, table_order), 1)
    common_bits = row_index & column_index
    parity = jnp.zeros((table_order, table_order), jnp.int32)
    for bit_index in range(table_order.bit_length() - 1):
        parity = parity ^ common_bits >> bit_index & 1
    return (1 - 2 * parity).astype(jnp.float32)


def butterfly(parts):
    count = len(parts)
    half = 1
    while half < count:
        out = list(parts)
        for index in range(count):
            if not index & half:
                out[index] = parts[index] + parts[index | half]
                out[index | half] = parts[index] - parts[index | half]
        parts = out
        half *= 2
    return parts


def local_kernel(n_ex, width, n_feat, rows_ref, acts_ref, cots_ref, flip_ref, walsh_ref, half_ref, sign_ref,
                 out_ref, grad_ref, table_ref, buf_ref):
    step = pl.program_id(0)
    tiles = width // LANES
    rows = SLAB

    @pl.loop(0, STEP_EX)
    def _(i):
        e = step * STEP_EX + i
        g = jnp.dot(cots_ref[i], acts_ref[i], preferred_element_type=jnp.float32)
        g = g * flip_ref[...]
        for low in range(2):
            tile = [g[:, (2 * q + low) * LANES:(2 * q + low + 1) * LANES] for q in range(tiles // 2)]
            tile = butterfly(tile)
            for q in range(tiles // 2):
                parts = butterfly([tile[q][8 * s:8 * s + 8] for s in range(rows // 8)])
                for s in range(rows // 8):
                    grad_ref[2 * q + low, pl.ds(e * rows + 8 * s, 8), :] = parts[s]

    @pl.when(step == pl.num_programs(0) - 1)
    def _():
        lane = lax.broadcasted_iota(jnp.int32, (TAP, LANES), 1)
        low_half = jnp.where(lane < LANES // 2, 1.0, -1.0).astype(jnp.float32)

        @pl.loop(0, (rows // 8) * (tiles // 2))
        def _(index):
            s = index // (tiles // 2)
            q = index % (tiles // 2)
            high, low = [], []
            for r in range(8):
                pieces = [
                    grad_ref.at[2 * q + j][pl.ds(s * 8 + r, n_ex, stride=rows), :] for j in range(2)
                ]
                x = jnp.concatenate(pieces, axis=1)
                h = x.astype(jnp.bfloat16)
                high.append(h)
                low.append((x - h.astype(jnp.float32)).astype(jnp.bfloat16))
            nt = (((1,), (1,)), ((), ()))
            mixed = lax.dot_general(walsh_ref[...], jnp.concatenate(high, axis=0), nt, preferred_element_type=jnp.float32)
            mixed += lax.dot_general(walsh_ref[...], jnp.concatenate(low, axis=0), nt, preferred_element_type=jnp.float32)
            parts = butterfly([mixed[:, j * LANES:(j + 1) * LANES] for j in range(4)])
            for j in range(4):
                v = parts[j]
                v = v * low_half + pltpu.roll(v, LANES // 2, 1)
                table_ref[pl.ds((s * 4 + j) * width + q * TAP, TAP), :] = v

        @pl.loop(0, n_feat // LANES)
        def _(block):
            base = pl.multiple_of(block * LANES, LANES)
            for j in range(LANES):
                buf_ref[j:j + 1, :] = table_ref[pl.ds(rows_ref[base + j], 1), :]
            t = buf_ref[...].T
            here = pl.ds(base, LANES)
            picked = jnp.where(half_ref[:, here] > 0, t[LANES // 2:], t[:LANES // 2])
            out_ref[:, here] = picked * sign_ref[:, here]


def local_terms(activations, cots, flip, rows, half, sign):
    n_ex, toks, width = activations.shape
    slab = cots.shape[1]
    n_feat = rows.shape[0]
    walsh = walsh_table(TAP).astype(jnp.bfloat16)
    whole = lambda shape: pl.BlockSpec(shape, lambda i, *_: (0,) * len(shape))
    return pl.pallas_call(
        functools.partial(local_kernel, n_ex, width, n_feat),
        out_shape=jax.ShapeDtypeStruct((n_ex, n_feat), jnp.float32),
        grid_spec=pltpu.PrefetchScalarGridSpec(
            num_scalar_prefetch=1,
            grid=(n_ex // STEP_EX,),
            in_specs=[
                pl.BlockSpec((STEP_EX, toks, width), lambda i, *_: (i, 0, 0)),
                pl.BlockSpec((STEP_EX, slab, toks), lambda i, *_: (i, 0, 0)),
                whole((slab, width)),
                whole((TAP, TAP)),
                whole((1, n_feat)),
                whole((1, n_feat)),
            ],
            out_specs=whole((n_ex, n_feat)),
            scratch_shapes=[
                pltpu.VMEM((width // LANES, n_ex * slab, LANES), jnp.float32),
                pltpu.VMEM((slab // 2 * width, LANES), jnp.float32),
                pltpu.VMEM((LANES, LANES), jnp.float32),
            ],
        ),
        compiler_params=pltpu.CompilerParams(
            dimension_semantics=("arbitrary",), vmem_limit_bytes=60 * 1024 * 1024
        ),
        name="local_terms",
    )(rows, activations, cots, flip, walsh, half, sign)


def prepare(cotangents, token_ids, signs, select, my_index, width, section_bits):
    live = token_ids != 0
    cots = jnp.where(live[:, None, :], jnp.swapaxes(cotangents, 1, 2), jnp.zeros((), cotangents.dtype))
    factor = 1.0 / math.sqrt(TOKS) / math.sqrt(SLAB * D)
    flip = signs.astype(jnp.float32) * factor
    column = select % D
    row = select // D
    rows = (row >> 1) * width + column % width
    shared = (column // width) & my_index
    parity = jnp.zeros_like(shared)
    for bit_index in range(section_bits):
        parity = parity ^ shared >> bit_index & 1
    sign = (1 - 2 * parity).astype(jnp.float32)
    return cots, flip, rows, (row & 1)[None, :], sign[None, :]


def body(activations, cotangents, token_ids, signs, select):
    highest = lax.Precision.HIGHEST
    section_bits = lax.axis_size("param").bit_length() - 1
    cots, flip, rows, half, sign = prepare(
        cotangents, token_ids, signs, select, lax.axis_index("param"), activations.shape[2], section_bits
    )
    partial_term = local_terms(activations, cots, flip, rows, half, sign)
    features = lax.psum_scatter(partial_term, "param", scatter_dimension=1, tiled=True)
    tile_block = jnp.einsum(
        "ek,fk->ef", features, lax.all_gather(features, "ex", axis=0, tiled=True), precision=highest
    )
    gram = lax.psum(tile_block, "param") / K
    return (features, gram)


def solution(mesh):
    return jax.shard_map(
        body,
        mesh=mesh,
        in_specs=(
            P("ex", None, "param"),
            P("ex", None, None),
            P("ex", None),
            P(None, "param"),
            P(),
        ),
        out_specs=(P("ex", "param"), P("ex", None)),
        check_vma=False,
    )
```

time: 570 us -> 367 us (0.64); the launches traced: 562 us -> 365 us
  local copies, waits for them, and re-layouts: 146 us -> 0 us
  matrix products: 119 us -> 20.5 us
  Pallas kernels: 0 us -> 94.8 us
  waiting for transfers between devices: 264 us -> 227 us
  other arithmetic: 19.9 us -> 9.24 us
    gather x1 -> x0, local copies, waits for them, and re-layouts: 119 us -> none  [body(): jnp.take(local_values.reshape(count_ex, -1), position, axis=1)]
    dot_general x3 -> x0, matrix products: 97.9 us -> none  [the longest x1 58.5 us: body(): jnp.einsum('erc,cd->erd', mixed, walsh_table(local_width), precision=high...]
    pallas_call x0 -> x1, Pallas kernels: none -> 94.8 us  [local_terms(): pl.pallas_call(functools.partial(local_kernel, n_ex, width, n_feat), out_...]
    reduce_scatter x1, waiting for transfers between devices: 94.5 us -> 55.2 us  [body(): lax.psum_scatter(partial_term, 'param', scatter_dimension=1, tiled=True)]
    reshape x1 -> x0, local copies, waits for them, and re-layouts: 23.3 us -> none  [body(): local_values.reshape(count_ex, -1)]
    mul x3 -> x1, other arithmetic: 13.4 us -> 1.68 us  [prepare(): flip = signs.astype(jnp.float32) * factor]
where the time goes in v1:
time: 367 us; the launch traced here: 365 us
  waiting for transfers between devices  227 us (62%)
  Pallas kernels  94.8 us (26%)
  matrix products  20.5 us (6%)
  between operations  13.7 us (4%)
  other arithmetic  9.24 us (3%)
    all_gather x1, waiting for transfers between devices, body(): lax.all_gather(features, 'ex', axis=0, tiled=True)  114 us
    pallas_call x1, Pallas kernels, local_terms(): pl.pallas_call(functools.partial(local_kernel, n_ex, width, n_feat), out_...  94.8 us
    psum x1, waiting for transfers between devices, body(): gram = lax.psum(tile_block, 'param') / K  57.6 us
    reduce_scatter x1, waiting for transfers between devices, body(): lax.psum_scatter(partial_term, 'param', scatter_dimension=1, tiled=True)  55.2 us
    dot_general x1, matrix products, body(): jnp.einsum('ek,fk->ef', features, lax.all_gather(features, 'ex', axis=0,...  20.5 us
  transfers between devices with their start and end apart: 3, of which 3 were waited for; matrix products, arithmetic and copies ran while one was open for 0% of the time, Pallas kernels for 0%

profile of v1, /device:TPU:1, one launch (start us, length us, event | category | flops | bytes accessed | tf_op | source)
XLA Modules:
  0.0 365.4 jit_solution(1002523077169653138)
XLA Ops:
  7.2 0.0 reduce-scatter.2.cloned.1.call-start
  7.2 0.9 convert_convert_fusion.walsh_ref
  8.1 0.8 broadcast_compare_fusion
  8.9 1.7 convert_multiply_fusion.flip_ref
  10.6 1.9 subtract_convert_fusion
  12.5 2.3 select_bitcast_fusion.cots_ref
  14.8 94.8 %local_terms.1 = f32[64,32768]{1,0:T(8,128)} custom-call(s32[32768]{0:T(1024)} %get-tuple-element.3.rows_ref, bf16[64,128,1024]{2,1,0:T(8,128)(2,1)} %acts_ref.1, bf16[64,64,128]{2,1,0:T(8,128)(2,1)} %select_bitcast_fusion.cots_ref, f32[64,1024]{1,0:T(8,128)} %convert_multiply_fusion.flip_ref, bf16[256,256]{1,0:T(8,128)(2,1)} %convert_convert_fusion.walsh_ref, ...), custom_call_target="tpu_custom_call" | custom-call | tf_op jit(solution)/shard_map/local_terms/pallas_call | solution.py:107
  109.6 0.0 reduce-scatter.2.cloned.1.call-update
  109.6 0.0 all-gather.2.cloned.1.call-start
  109.6 55.2 %reduce-scatter.2.cloned.1.call-done = f32[64,4096]{1,0:T(8,128)} async-done(((f32[64,32768]{1,0:T(8,128)}), f32[64,4096]{1,0:T(8,128)}) %reduce-scatter.2.cloned.1.call-update) | async-done | bytes 1048592 | tf_op jit(solution)/shard_map/reduce_scatter | solution.py:158
  164.8 0.0 all-gather.2.cloned.1.call-update
  164.8 0.0 all-reduce.2.cloned.1.call-start
  164.9 114.3 %all-gather.2.cloned.1.call-done = f32[1024,4096]{1,0:T(8,128)} async-done(((f32[64,4096]{1,0:T(8,128)}), f32[1024,4096]{1,0:T(8,128)}) %all-gather.2.cloned.1.call-update) | async-done | bytes 16777232 | tf_op jit(solution)/shard_map/all_gather | solution.py:160
  279.1 20.5 %fusion.6 = f32[64,1024]{1,0:T(8,128)} fusion(f32[64,4096]{1,0:T(8,128)} %reduce-scatter.2.cloned.1.call-done, f32[1024,4096]{1,0:T(8,128)} %all-gather.2.cloned.1.call-done), kind=kOutput, calls=%fused_computation.25 | convolution fusion | flops 3221225472 | bytes 18087936 | tf_op jit(solution)/shard_map/ek,fk->ef/dot_general | solution.py:159
  299.6 0.0 all-reduce.2.cloned.1.call-update
  299.6 57.6 %all-reduce.2.cloned.1.call-done = f32[64,1024]{1,0:T(8,128)} async-done(((f32[64,1024]{1,0:T(8,128)}), f32[64,1024]{1,0:T(8,128)}) %all-reduce.2.cloned.1.call-update) | async-done | bytes 262160 | tf_op jit(solution)/shard_map/psum | solution.py:162
  357.2 1.7 broadcast_multiply_fusion
Async XLA Ops:
  7.2 157.7 %reduce-scatter.2.cloned.1.call-start = ((), (), s32[]{:S(2)}) async-start(), calls=%async_computation.1 | async-start | bytes 9437184 | tf_op jit(solution)/shard_map/reduce_scatter | solution.py:158
  109.6 169.6 %all-gather.2.cloned.1.call-start = ((), (), s32[]{:S(2)}) async-start(), calls=%async_computation.2 | async-start | bytes 17825792 | tf_op jit(solution)/shard_map/all_gather | solution.py:160
  164.8 192.3 %all-reduce.2.cloned.1.call-start = ((), (), s32[]{:S(2)}) async-start(), calls=%async_computation.3 | async-start | bytes 524288 | tf_op jit(solution)/shard_map/psum | solution.py:162
Sparse Core Ops, SparseCore 0:
  109.7 55.0 reduce-scatter.1
  167.5 111.5 all-gather.1
  299.7 57.4 all-reduce.1

commit v2 on v1

--- a/solution.py
+++ b/solution.py
@@ -15,6 +15,7 @@
 LANES = 128
 STEP_EX = 8
 TAP = 256
+CHUNKS = 2
 
 
 def walsh_table(table_order):
@@ -41,8 +42,7 @@
     return parts
 
 
-def local_kernel(n_ex, width, n_feat, rows_ref, acts_ref, cots_ref, flip_ref, walsh_ref, half_ref, sign_ref,
-                 out_ref, grad_ref, table_ref, buf_ref):
+def table_kernel(n_ex, width, acts_ref, cots_ref, flip_ref, walsh_ref, table_ref, grad_ref):
     step = pl.program_id(0)
     tiles = width // LANES
     rows = SLAB
@@ -87,49 +87,62 @@
                 v = v * low_half + pltpu.roll(v, LANES // 2, 1)
                 table_ref[pl.ds((s * 4 + j) * width + q * TAP, TAP), :] = v
 
-        @pl.loop(0, n_feat // LANES)
-        def _(block):
-            base = pl.multiple_of(block * LANES, LANES)
-            for j in range(LANES):
-                buf_ref[j:j + 1, :] = table_ref[pl.ds(rows_ref[base + j], 1), :]
-            t = buf_ref[...].T
-            here = pl.ds(base, LANES)
-            picked = jnp.where(half_ref[:, here] > 0, t[LANES // 2:], t[:LANES // 2])
-            out_ref[:, here] = picked * sign_ref[:, here]
-
-
-def local_terms(activations, cots, flip, rows, half, sign):
+
+def gather_kernel(n_block, rows_ref, table_ref, half_ref, sign_ref, out_ref, buf_ref):
+    @pl.loop(0, n_block)
+    def _(block):
+        base = pl.multiple_of(block * LANES, LANES)
+        for j in range(LANES):
+            buf_ref[j:j + 1, :] = table_ref[pl.ds(rows_ref[base + j], 1), :]
+        t = buf_ref[...].T
+        here = pl.ds(block, 1)
+        picked = jnp.where(half_ref[here, :] > 0, t[LANES // 2:], t[:LANES // 2])
+        out_ref[block] = picked * sign_ref[here, :]
+
+
+def whole(shape):
+    return pl.BlockSpec(shape, lambda i, *_: (0,) * len(shape))
+
+
+def make_table(activations, cots, flip):
     n_ex, toks, width = activations.shape
     slab = cots.shape[1]
-    n_feat = rows.shape[0]
     walsh = walsh_table(TAP).astype(jnp.bfloat16)
-    whole = lambda shape: pl.BlockSpec(shape, lambda i, *_: (0,) * len(shape))
-    return pl.pallas_call(
-        functools.partial(local_kernel, n_ex, width, n_feat),
-        out_shape=jax.ShapeDtypeStruct((n_ex, n_feat), jnp.float32),
-        grid_spec=pltpu.PrefetchScalarGridSpec(
-            num_scalar_prefetch=1,
-            grid=(n_ex // STEP_EX,),
-            in_specs=[
-                pl.BlockSpec((STEP_EX, toks, width), lambda i, *_: (i, 0, 0)),
-                pl.BlockSpec((STEP_EX, slab, toks), lambda i, *_: (i, 0, 0)),
-                whole((slab, width)),
-                whole((TAP, TAP)),
-                whole((1, n_feat)),
-                whole((1, n_feat)),
-            ],
-            out_specs=whole((n_ex, n_feat)),
-            scratch_shapes=[
-                pltpu.VMEM((width // LANES, n_ex * slab, LANES), jnp.float32),
-                pltpu.VMEM((slab // 2 * width, LANES), jnp.float32),
-                pltpu.VMEM((LANES, LANES), jnp.float32),
-            ],
+    return pl.pallas_call(
+        functools.partial(table_kernel, n_ex, width),
+        out_shape=pltpu.VMEM((slab // 2 * width, LANES), jnp.float32),
+        grid=(n_ex // STEP_EX,),
+        in_specs=[
+            pl.BlockSpec((STEP_EX, toks, width), lambda i: (i, 0, 0)),
+            pl.BlockSpec((STEP_EX, slab, toks), lambda i: (i, 0, 0)),
+            whole((slab, width)),
+            whole((TAP, TAP)),
+        ],
+        out_specs=pl.BlockSpec(memory_space=pltpu.VMEM),
+        scratch_shapes=[pltpu.VMEM((width // LANES, n_ex * slab, LANES), jnp.float32)],
+        compiler_params=pltpu.CompilerParams(
+            dimension_semantics=("arbitrary",), vmem_limit_bytes=30 * 1024 * 1024
         ),
-        compiler_params=pltpu.CompilerParams(
-            dimension_semantics=("arbitrary",), vmem_limit_bytes=60 * 1024 * 1024
-        ),
-        name="local_terms",
-    )(rows, activations, cots, flip, walsh, half, sign)
+        name="make_table",
+    )(activations, cots, flip, walsh)
+
+
+def gather_rows(table, rows, half, sign):
+    n_block = half.shape[0]
+    return pl.pallas_call(
+        functools.partial(gather_kernel, n_block),
+        out_shape=jax.ShapeDtypeStruct((n_block, LANES // 2, LANES), jnp.float32),
+        in_specs=[
+            pl.BlockSpec(memory_space=pltpu.SMEM),
+            pl.BlockSpec(memory_space=pltpu.VMEM),
+            pl.BlockSpec(memory_space=pltpu.VMEM),
+            pl.BlockSpec(memory_space=pltpu.VMEM),
+        ],
+        out_specs=pl.BlockSpec(memory_space=pltpu.VMEM),
+        scratch_shapes=[pltpu.VMEM((LANES, LANES), jnp.float32)],
+        compiler_params=pltpu.CompilerParams(vmem_limit_bytes=16 * 1024 * 1024),
+        name="gather_rows",
+    )(rows.reshape(-1), table, half, sign)
 
 
 def prepare(cotangents, token_ids, signs, select, my_index, width, section_bits):
@@ -145,22 +158,164 @@
     for bit_index in range(section_bits):
         parity = parity ^ shared >> bit_index & 1
     sign = (1 - 2 * parity).astype(jnp.float32)
-    return cots, flip, rows, (row & 1)[None, :], sign[None, :]
+    return cots, flip, rows, row & 1, sign
+
+
+def test_local(a, c, t, s, sel, my):
+    cots, flip, rows, half, sign = prepare(c, t, s, sel, my, a.shape[2], 3)
+    table = make_table(a, cots, flip)
+    out = gather_rows(table, rows, half.reshape(-1, LANES), sign.reshape(-1, LANES))
+    return jnp.swapaxes(out, 0, 1).reshape(64, -1)
+
+
+def gram_kernel(n_ex, *refs):
+    x_refs, out_ref, high_ref, low_ref = refs[:-3], refs[-3], refs[-2], refs[-1]
+    blocks = x_refs[0].shape[0]
+    width = sum(r.shape[2] for r in x_refs)
+    for b in range(blocks):
+        x = jnp.concatenate([r[b] for r in x_refs], axis=1)
+        h = x.astype(jnp.bfloat16)
+        low = (x - h.astype(jnp.float32)).astype(jnp.bfloat16)
+        for at in ((b, b + blocks) if b < 10 else (b,)):
+            high_ref[at * n_ex:(at + 1) * n_ex, :] = h
+            low_ref[at * n_ex:(at + 1) * n_ex, :] = low
+    half = LANES // 2
+    left = lax.broadcasted_iota(jnp.int32, (n_ex // 2, LANES), 1) < half
+    nt = (((1,), (1,)), ((), ()))
+
+    @pl.loop(0, blocks)
+    def _(b):
+        first = pl.multiple_of(b * n_ex, n_ex)
+        mine = pl.ds(first, n_ex)
+        near = pl.ds(first, 10 * n_ex)
+        t = lax.dot_general(high_ref[mine, :], high_ref[near, :], nt, preferred_element_type=jnp.float32)
+        t += lax.dot_general(high_ref[mine, :], low_ref[near, :], nt, preferred_element_type=jnp.float32)
+        t += lax.dot_general(low_ref[mine, :], high_ref[near, :], nt, preferred_element_type=jnp.float32)
+        for p in range(8):
+            q = (p + 1) // 2
+            top = t[:n_ex // 2, q * LANES:(q + 1) * LANES]
+            low = t[n_ex // 2:, q * LANES:(q + 1) * LANES]
+            if p % 2:
+                low = pltpu.roll(low, half, 1)
+            else:
+                top = pltpu.roll(top, half, 1)
+            out_ref[p, b, :n_ex // 2, :] = jnp.where(left, top, low)
+            out_ref[p, b, n_ex // 2:, :] = t[8 * p:8 * p + 8, :LANES]
+
+
+def partial_gram(parts):
+    blocks, n_ex, _ = parts[0].shape
+    width = sum(x.shape[2] for x in parts)
+    vmem = pl.BlockSpec(memory_space=pltpu.VMEM)
+    return pl.pallas_call(
+        functools.partial(gram_kernel, n_ex),
+        out_shape=jax.ShapeDtypeStruct((8, blocks, n_ex // 2 + 8, LANES), jnp.float32),
+        in_specs=[vmem] * len(parts),
+        out_specs=vmem,
+        scratch_shapes=[pltpu.VMEM(((blocks + 10) * n_ex, width), jnp.bfloat16)] * 2,
+        compiler_params=pltpu.CompilerParams(vmem_limit_bytes=16 * 1024 * 1024),
+        name="partial_gram",
+    )(*parts)
+
+
+def sum_kernel(scale, x_ref, tile_ref, strip_ref):
+    half = LANES // 2
+    total = jnp.sum(x_ref[...], axis=0) * scale
+    pair = total[:half // 2]
+    tile = jnp.concatenate([pair[:, :half], pair[:, half:]], axis=0)
+    tile_ref[0] = tile
+    tile_ref[1] = tile.T
+    strip_ref[...] = total[half // 2:]
+
+
+def sum_tiles(received):
+    vmem = pl.BlockSpec(memory_space=pltpu.VMEM)
+    return pl.pallas_call(
+        functools.partial(sum_kernel, 1.0 / K),
+        out_shape=(
+            jax.ShapeDtypeStruct((2, LANES // 2, LANES // 2), jnp.float32),
+            jax.ShapeDtypeStruct((8, LANES), jnp.float32),
+        ),
+        in_specs=[vmem],
+        out_specs=(vmem, vmem),
+        compiler_params=pltpu.CompilerParams(vmem_limit_bytes=16 * 1024 * 1024),
+        name="sum_tiles",
+    )(received)
+
+
+def place_kernel(me_ref, x_ref, out_ref):
+    half = LANES // 2
+    count = out_ref.shape[1] // half
+    columns = [None] * count
+    columns[0] = jnp.concatenate([x_ref[p, half:, :half] for p in range(8)], axis=0)
+    for p in range(8):
+        columns[p + 1] = x_ref[p, :half, :half]
+        if count - 1 - p > p + 1:
+            columns[count - 1 - p] = x_ref[p, :half, half:]
+    row = jnp.concatenate(columns, axis=1)
+    out_ref[...] = pltpu.roll(row, me_ref[0] * half, 1)
+
+
+def place_tiles(tiles, me, n_ex, count):
+    vmem = pl.BlockSpec(memory_space=pltpu.VMEM)
+    return pl.pallas_call(
+        place_kernel,
+        out_shape=jax.ShapeDtypeStruct((n_ex, count * n_ex), jnp.float32),
+        in_specs=[pl.BlockSpec(memory_space=pltpu.SMEM), vmem],
+        out_specs=vmem,
+        name="place_tiles",
+    )(me.reshape(1), tiles)
 
 
 def body(activations, cotangents, token_ids, signs, select):
-    highest = lax.Precision.HIGHEST
-    section_bits = lax.axis_size("param").bit_length() - 1
-    cots, flip, rows, half, sign = prepare(
-        cotangents, token_ids, signs, select, lax.axis_index("param"), activations.shape[2], section_bits
+    n_param, n_group = lax.axis_size("param"), lax.axis_size("ex")
+    n_ex, _, width = activations.shape
+    me = lax.axis_index("param")
+    section_bits = n_param.bit_length() - 1
+    cots, flip, rows, half, sign = prepare(cotangents, token_ids, signs, select, me, width, section_bits)
+    table = make_table(activations, cots, flip)
+
+    n_y = n_param // 2
+    other_first = me % 2 == 0
+
+    def arrange(x):
+        x = x.reshape(n_y, 2, CHUNKS, n_group, -1)
+        even, odd = x[:, 0], x[:, 1]
+        x = jnp.stack([jnp.where(other_first, odd, even), jnp.where(other_first, even, odd)])
+        return jnp.moveaxis(x, 2, 0).reshape(CHUNKS, 2, n_y * n_group * x.shape[-1] // LANES, LANES)
+
+    rows, half, sign = arrange(rows), arrange(half), arrange(sign)
+    swap = [(i, i ^ 1) for i in range(n_param)]
+    ring = [[2 * y + core for y in range(n_y)] for core in range(2)]
+    features, shares = [], []
+    for chunk in range(CHUNKS):
+        sent = gather_rows(table, rows[chunk, 0], half[chunk, 0], sign[chunk, 0])
+        arrived = lax.ppermute(sent, "param", swap)
+        kept = gather_rows(table, rows[chunk, 1], half[chunk, 1], sign[chunk, 1])
+        pair = (kept + arrived).reshape(n_y, -1, n_ex, LANES)
+        parts = lax.all_to_all(pair, "param", split_axis=0, concat_axis=0, axis_index_groups=ring)
+        block = parts[0] + parts[1] + parts[2] + parts[3]
+        features.append(block)
+        shares.append(lax.all_to_all(block, "ex", split_axis=0, concat_axis=0))
+    whole_features = jnp.swapaxes(jnp.concatenate(features, axis=0), 0, 1).reshape(n_ex, -1)
+
+    partial = partial_gram(shares)
+    rows_out = partial.shape[2]
+    everyone = ("param", "ex")
+    received = lax.all_to_all(
+        partial.reshape(n_param * n_group, rows_out, LANES), everyone, split_axis=0, concat_axis=0
     )
-    partial_term = local_terms(activations, cots, flip, rows, half, sign)
-    features = lax.psum_scatter(partial_term, "param", scatter_dimension=1, tiled=True)
-    tile_block = jnp.einsum(
-        "ek,fk->ef", features, lax.all_gather(features, "ex", axis=0, tiled=True), precision=highest
+    tile, strip = sum_tiles(received)
+    onward = [
+        (p * n_group + e, p * n_group + (e + p + 1) % n_group) for p in range(n_param) for e in range(n_group)
+    ]
+    turned = lax.ppermute(tile[1], everyone, onward)
+    message = jnp.concatenate([jnp.concatenate([tile[0], turned], axis=1), strip], axis=0)
+    spread = lax.all_to_all(
+        jnp.broadcast_to(message[None], (n_param,) + message.shape), "param", split_axis=0, concat_axis=0
     )
-    gram = lax.psum(tile_block, "param") / K
-    return (features, gram)
+    gram = place_tiles(spread, lax.axis_index("ex"), n_ex, n_group)
+    return (whole_features, gram)
 
 
 def solution(mesh):

time: 367 us -> 247 us (0.67)
  waiting for transfers between devices: 227 us -> 43.8 us
  blocking collectives: 0 us -> 54.5 us
  starting transfers between devices: 0.12 us -> 24.8 us
  matrix products: 20.5 us -> 0 us
  between operations: 13.7 us -> 0.94 us
  Pallas kernels: 94.8 us -> 103 us
  local copies, waits for them, and re-layouts: 0 us -> 7.31 us
    all_gather x1 -> x0, waiting for transfers between devices: 114 us -> none  [body(): lax.all_gather(features, 'ex', axis=0, tiled=True)]
    psum x1 -> x0, waiting for transfers between devices: 57.6 us -> none  [body(): gram = lax.psum(tile_block, 'param') / K]
    reduce_scatter x1 -> x0, waiting for transfers between devices: 55.2 us -> none  [body(): lax.psum_scatter(partial_term, 'param', scatter_dimension=1, tiled=True)]
    all_to_all x0 -> x2, blocking collectives: none -> 54.5 us  [the longest x1 42.6 us: body(): lax.all_to_all(partial.reshape(n_param * n_group, rows_out, LANES), every...]
    all_to_all x0 -> x4, waiting for transfers between devices: none -> 39.3 us  [the longest x2 25.4 us: body(): lax.all_to_all(pair, 'param', split_axis=0, concat_axis=0, axis_index_gro...]
    all_to_all x0 -> x4, starting transfers between devices: none -> 20.9 us  [the longest x2 8.08 us: body(): lax.all_to_all(pair, 'param', split_axis=0, concat_axis=0, axis_index_gro...]
    dot_general x1 -> x0, matrix products: 20.5 us -> none  [body(): jnp.einsum('ek,fk->ef', features, lax.all_gather(features, 'ex', axis=0,...]
    pallas_call x1 -> x8, Pallas kernels: 94.8 us -> 103 us  [the longest x4 55.2 us: gather_rows(): pl.pallas_call(functools.partial(gather_kernel, n_block), out_shape=jax.S...]
  transfers between devices with their start and end apart: 3 -> 7, of which waited for: 3 -> 5; matrix products, arithmetic and copies ran while one was open for 0% -> 4% of each run, Pallas kernels for 0% -> 17%
where the time goes in v2:
time: 247 us; the launch traced here: 246 us
  Pallas kernels  103 us (42%)
  blocking collectives  54.5 us (22%)
  waiting for transfers between devices  43.8 us (18%)
  starting transfers between devices  24.8 us (10%)
  other arithmetic  11.6 us (5%)
  local copies, waits for them, and re-layouts  7.31 us (3%)
    pallas_call x4, Pallas kernels, gather_rows(): pl.pallas_call(functools.partial(gather_kernel, n_block), out_shape=jax.S...  55.2 us
    all_to_all x1, blocking collectives, body(): lax.all_to_all(partial.reshape(n_param * n_group, rows_out, LANES), every...  42.6 us
    pallas_call x1, Pallas kernels, make_table(): pl.pallas_call(functools.partial(table_kernel, n_ex, width), out_shape=pl...  37.7 us
    all_to_all x2, waiting for transfers between devices, body(): lax.all_to_all(pair, 'param', split_axis=0, concat_axis=0, axis_index_gro...  25.4 us
    all_to_all x1, blocking collectives, body(): shares.append(lax.all_to_all(block, 'ex', split_axis=0, concat_axis=0))  11.9 us
    all_to_all x1, waiting for transfers between devices, body(): shares.append(lax.all_to_all(block, 'ex', split_axis=0, concat_axis=0))  9.13 us
    pallas_call x1, Pallas kernels, partial_gram(): pl.pallas_call(functools.partial(gram_kernel, n_ex), out_shape=jax.ShapeD...  8.14 us
    all_to_all x2, starting transfers between devices, body(): lax.all_to_all(pair, 'param', split_axis=0, concat_axis=0, axis_index_gro...  8.08 us
  transfers between devices with their start and end apart: 7, of which 5 were waited for; matrix products, arithmetic and copies ran while one was open for 4% of the time, Pallas kernels for 17%

profile of v2, /device:TPU:1, one launch (start us, length us, event | category | flops | bytes accessed | tf_op | source)
XLA Modules:
  0.0 246.0 jit_solution(17114938513101134187)
XLA Ops:
  0.6 0.0 copy-start.5
  0.6 0.0 copy-start.4
  0.7 0.2 convert_convert_fusion.walsh_ref
  0.9 0.0 copy-start.3
  0.9 1.3 subtract_convert_fusion
  2.5 0.0 copy-done.5
  2.5 0.0 copy-done.4
  2.5 0.0 copy-done.3
  2.5 0.1 select_bitcast_fusion.cots_ref
  2.6 37.7 %make_table.1.table_ref = f32[32768,128]{1,0:T(8,128)S(1)} custom-call(bf16[64,128,1024]{2,1,0:T(8,128)(2,1)} %acts_ref.1, bf16[64,64,128]{2,1,0:T(8,128)(2,1)S(1)} %select_bitcast_fusion.cots_ref, f32[64,1024]{1,0:T(8,128)S(1)} %convert_multiply_fusion.flip_ref, bf16[256,256]{1,0:T(8,128)(2,1)S(1)} %convert_convert_fusion.walsh_ref), custom_call_target="tpu_custom_call" | custom-call | tf_op jit(solution)/shard_map/make_table/pallas_call | solution.py:111
  40.3 0.0 copy-start
  40.3 13.8 %gather_rows.5 = f32[64,64,128]{2,1,0:T(8,128)S(1)} custom-call(s32[8192]{0:T(1024)S(1)} %get-tuple-element.14.rows_ref, f32[32768,128]{1,0:T(8,128)S(1)} %make_table.1.table_ref, s32[64,128]{1,0:T(8,128)S(1)} %get-tuple-element.10.half_ref, f32[64,128]{1,0:T(8,128)S(1)} %get-tuple-element.6.sign_ref), custom_call_target="tpu_custom_call" | custom-call | tf_op jit(solution)/shard_map/gather_rows/pallas_call | solution.py:132
  54.1 1.5 collective-permute-start
  55.6 13.8 %gather_rows.7 = f32[64,64,128]{2,1,0:T(8,128)S(1)} custom-call(s32[8192]{0:T(1024)S(1)} %get-tuple-element.15.rows_ref, f32[32768,128]{1,0:T(8,128)S(1)} %make_table.1.table_ref, s32[64,128]{1,0:T(8,128)S(1)} %get-tuple-element.11.half_ref, f32[64,128]{1,0:T(8,128)S(1)} %get-tuple-element.7.sign_ref), custom_call_target="tpu_custom_call" | custom-call | tf_op jit(solution)/shard_map/gather_rows/pallas_call | solution.py:132
  69.4 0.1 collective-permute-start.1
  69.5 0.0 copy-done
  69.5 13.8 %gather_rows.4 = f32[64,64,128]{2,1,0:T(8,128)S(1)} custom-call(s32[8192]{0:T(1024)S(1)} %get-tuple-element.17.rows_ref, f32[32768,128]{1,0:T(8,128)S(1)} %make_table.1.table_ref, s32[64,128]{1,0:T(8,128)S(1)} %get-tuple-element.13.half_ref, f32[64,128]{1,0:T(8,128)S(1)} %get-tuple-element.9.sign_ref), custom_call_target="tpu_custom_call" | custom-call | tf_op jit(solution)/shard_map/gather_rows/pallas_call | solution.py:132
  83.3 0.0 collective-permute-done
  83.3 1.7 add.57
  85.1 4.5 %all-to-all-start = ((f32[4,16,64,128]{3,2,1,0:T(8,128)}), f32[4,16,64,128]{3,2,1,0:T(8,128)}, u32[]{:S(2)}, u32[]{:S(2)}) async-start(f32[4,16,64,128]{3,2,1,0:T(8,128)} %bitcast.103), calls=%async_computation | async-start | bytes 4194304 | tf_op jit(solution)/shard_map/all_to_all | solution.py:296
  89.5 0.0 copy-start.1
  89.6 5.8 %copy-done.1 = f32[32768,128]{1,0:T(8,128)S(1)} copy-done((f32[32768,128]{1,0:T(8,128)S(1)}, f32[32768,128]{1,0:T(8,128)}, u32[]{:S(2)}) %copy-start.1) | copy-done | bytes 16777240
  95.3 13.8 %gather_rows.6 = f32[64,64,128]{2,1,0:T(8,128)S(1)} custom-call(s32[8192]{0:T(1024)S(1)} %get-tuple-element.16.rows_ref, f32[32768,128]{1,0:T(8,128)S(1)} %copy-done.1, s32[64,128]{1,0:T(8,128)S(1)} %get-tuple-element.12.half_ref, f32[64,128]{1,0:T(8,128)S(1)} %get-tuple-element.8.sign_ref), custom_call_target="tpu_custom_call" | custom-call | tf_op jit(solution)/shard_map/gather_rows/pallas_call | solution.py:132
  109.1 0.0 collective-permute-done.1
  109.1 3.3 %add.62 = f32[64,64,128]{2,1,0:T(8,128)} add(f32[64,64,128]{2,1,0:T(8,128)S(1)} %gather_rows.6, f32[64,64,128]{2,1,0:T(8,128)} %collective-permute-done.1) | non-fusion elementwise | flops 524288 | bytes 6291456 | tf_op jit(solution)/shard_map/add | solution.py:295
  112.5 3.0 %all-to-all-done = f32[4,16,64,128]{3,2,1,0:T(8,128)} async-done(((f32[4,16,64,128]{3,2,1,0:T(8,128)}), f32[4,16,64,128]{3,2,1,0:T(8,128)}, u32[]{:S(2)}, u32[]{:S(2)}) %all-to-all-start) | async-done | bytes 2097184 | tf_op jit(solution)/shard_map/all_to_all | solution.py:296
  115.5 3.6 %all-to-all-start.1 = ((f32[4,16,64,128]{3,2,1,0:T(8,128)}), f32[4,16,64,128]{3,2,1,0:T(8,128)S(1)}, u32[]{:S(2)}, u32[]{:S(2)}) async-start(f32[4,16,64,128]{3,2,1,0:T(8,128)} %bitcast.33), calls=%async_computation.1 | async-start | bytes 4194304 | tf_op jit(solution)/shard_map/all_to_all | solution.py:296
  119.1 2.5 %fusion.1 = f32[16,64,128]{2,1,0:T(8,128)} fusion(f32[4,16,64,128]{3,2,1,0:T(8,128)} %all-to-all-done), kind=kLoop, calls=%fused_computation.8 | loop fusion | flops 393216 | bytes 2621440 | tf_op jit(solution)/shard_map/add | solution.py:297
  121.6 22.4 %all-to-all-done.1 = f32[4,16,64,128]{3,2,1,0:T(8,128)S(1)} async-done(((f32[4,16,64,128]{3,2,1,0:T(8,128)}), f32[4,16,64,128]{3,2,1,0:T(8,128)S(1)}, u32[]{:S(2)}, u32[]{:S(2)}) %all-to-all-start.1) | async-done | bytes 2097184 | tf_op jit(solution)/shard_map/all_to_all | solution.py:296
  144.0 7.9 %all-to-all-start.2 = ((f32[16,64,128]{2,1,0:T(8,128)}), f32[16,64,128]{2,1,0:T(8,128)S(1)}, u32[]{:S(2)}, u32[]{:S(2)}) async-start(f32[16,64,128]{2,1,0:T(8,128)} %fusion.1), calls=%async_computation.2 | async-start | bytes 1048576 | tf_op jit(solution)/shard_map/all_to_all | solution.py:299
  151.8 0.2 fusion
  152.0 9.1 %all-to-all-done.2.refs_0_ = f32[16,64,128]{2,1,0:T(8,128)S(1)} async-done(((f32[16,64,128]{2,1,0:T(8,128)}), f32[16,64,128]{2,1,0:T(8,128)S(1)}, u32[]{:S(2)}, u32[]{:S(2)}) %all-to-all-start.2) | async-done | bytes 524320 | tf_op jit(solution)/shard_map/all_to_all | solution.py:299
  161.1 11.9 %all_to_all.30.refs_1_ = f32[16,64,128]{2,1,0:T(8,128)S(1)} all-to-all(f32[16,64,128]{2,1,0:T(8,128)S(1)} %fusion), channel_id=1, replica_groups=mesh['param'=8,'ex'=16] {'ex'}, dimensions={0} | all-to-all | bytes 1048576 | tf_op jit(solution)/shard_map/all_to_all | solution.py:299
  173.0 8.1 %partial_gram.1 = f32[8,16,40,128]{3,2,1,0:T(8,128)S(1)} custom-call(f32[16,64,128]{2,1,0:T(8,128)S(1)} %all-to-all-done.2.refs_0_, f32[16,64,128]{2,1,0:T(8,128)S(1)} %all_to_all.30.refs_1_), custom_call_target="tpu_custom_call" | custom-call | tf_op jit(solution)/shard_map/partial_gram/pallas_call | solution.py:210
  181.1 42.6 %all_to_all.31.x_ref = f32[128,40,128]{2,1,0:T(8,128)S(1)} all-to-all(f32[128,40,128]{2,1,0:T(8,128)S(1)} %bitcast.102), channel_id=1, replica_groups=mesh['param'=8,'ex'=16] {'param','ex'}, dimensions={0} | all-to-all | bytes 5242880 | tf_op jit(solution)/shard_map/all_to_all | solution.py:305
  223.7 0.3 sum_tiles.1
  224.1 2.2 collective-permute-start.2
  226.3 4.5 %collective-permute-done.2 = f32[64,64]{1,0:T(8,128)S(1)} collective-permute-done((f32[64,64]{1,0:T(8,128)S(1)}, f32[64,64]{1,0:T(8,128)S(1)}, u32[]{:S(2)}, u32[]{:S(2)}) %collective-permute-start.2) | collective-permute-done | bytes 16416 | tf_op jit(solution)/shard_map/ppermute | solution.py:312
  230.8 0.1 pad_maximum_fusion
  230.9 0.7 broadcast_in_dim.21
  231.6 5.0 %all-to-all-start.5 = ((f32[8,72,128]{2,1,0:T(8,128)}), f32[8,72,128]{2,1,0:T(8,128)S(1)}, u32[]{:S(2)}, u32[]{:S(2)}) async-start(f32[8,72,128]{2,1,0:T(8,128)} %broadcast_in_dim.21), calls=%async_computation.5 | async-start | bytes 589824 | tf_op jit(solution)/shard_map/all_to_all | solution.py:314
  236.6 2.1 copy_bitcast_fusion
  238.7 4.8 %all-to-all-done.5.x_ref = f32[8,72,128]{2,1,0:T(8,128)S(1)} async-done(((f32[8,72,128]{2,1,0:T(8,128)}), f32[8,72,128]{2,1,0:T(8,128)S(1)}, u32[]{:S(2)}, u32[]{:S(2)}) %all-to-all-start.5) | async-done | bytes 294944 | tf_op jit(solution)/shard_map/all_to_all | solution.py:314
  243.4 0.0 copy-start.2
  243.4 0.7 copy-done.2
  244.1 1.9 place_tiles.1
  (15 shorter events, 0.2 us)
Async XLA Ops:
  0.6 1.8 copy-start.5
  0.6 1.8 copy-start.4
  0.9 1.6 copy-start.3
  40.3 29.2 %copy-start = (f32[32768,128]{1,0:T(8,128)}, f32[32768,128]{1,0:T(8,128)S(1)}, u32[]{:S(2)}) copy-start(f32[32768,128]{1,0:T(8,128)S(1)} %make_table.1.table_ref) | copy-start | bytes 50331652
  54.1 29.2 %collective-permute-start = (f32[64,64,128]{2,1,0:T(8,128)S(1)}, f32[64,64,128]{2,1,0:T(8,128)S(1)}, u32[]{:S(2)}, u32[]{:S(2)}) collective-permute-start(f32[64,64,128]{2,1,0:T(8,128)S(1)} %gather_rows.5), channel_id=1, source_target_pairs={{0,16},{16,0},{32,48},{48,32},{64,80},{80,64},{96,112},{112,96},{1... | collective-permute-start | bytes 6291464 | tf_op jit(solution)/shard_map/ppermute | solution.py:293
  69.4 39.7 %collective-permute-start.1 = (f32[64,64,128]{2,1,0:T(8,128)S(1)}, f32[64,64,128]{2,1,0:T(8,128)}, u32[]{:S(2)}, u32[]{:S(2)}) collective-permute-start(f32[64,64,128]{2,1,0:T(8,128)S(1)} %gather_rows.7), channel_id=1, source_target_pairs={{0,16},{16,0},{32,48},{48,32},{64,80},{80,64},{96,112},{112,96},{1... | collective-permute-start | bytes 6291464 | tf_op jit(solution)/shard_map/ppermute | solution.py:293
  85.1 30.4 %all-to-all-start = ((f32[4,16,64,128]{3,2,1,0:T(8,128)}), f32[4,16,64,128]{3,2,1,0:T(8,128)}, u32[]{:S(2)}, u32[]{:S(2)}) async-start(f32[4,16,64,128]{3,2,1,0:T(8,128)} %bitcast.103), calls=%async_computation | async-start | bytes 4194304 | tf_op jit(solution)/shard_map/all_to_all | solution.py:296
  89.5 5.8 %copy-start.1 = (f32[32768,128]{1,0:T(8,128)S(1)}, f32[32768,128]{1,0:T(8,128)}, u32[]{:S(2)}) copy-start(f32[32768,128]{1,0:T(8,128)} %copy-done) | copy-start | bytes 50331652
  115.5 28.5 %all-to-all-start.1 = ((f32[4,16,64,128]{3,2,1,0:T(8,128)}), f32[4,16,64,128]{3,2,1,0:T(8,128)S(1)}, u32[]{:S(2)}, u32[]{:S(2)}) async-start(f32[4,16,64,128]{3,2,1,0:T(8,128)} %bitcast.33), calls=%async_computation.1 | async-start | bytes 4194304 | tf_op jit(solution)/shard_map/all_to_all | solution.py:296
  144.0 17.2 %all-to-all-start.2 = ((f32[16,64,128]{2,1,0:T(8,128)}), f32[16,64,128]{2,1,0:T(8,128)S(1)}, u32[]{:S(2)}, u32[]{:S(2)}) async-start(f32[16,64,128]{2,1,0:T(8,128)} %fusion.1), calls=%async_computation.2 | async-start | bytes 1048576 | tf_op jit(solution)/shard_map/all_to_all | solution.py:299
  224.1 6.7 %collective-permute-start.2 = (f32[64,64]{1,0:T(8,128)S(1)}, f32[64,64]{1,0:T(8,128)S(1)}, u32[]{:S(2)}, u32[]{:S(2)}) collective-permute-start(f32[64,64]{1,0:T(8,128)S(1)} %get-tuple-element.26), channel_id=1, source_target_pairs={{0,1},{1,2},{2,3},{3,4},{4,5},{5,6},{6,7},{7,8},{8,9},{9,10},{10,1... | collective-permute-start | bytes 49160 | tf_op jit(solution)/shard_map/ppermute | solution.py:312
  231.6 11.8 %all-to-all-start.5 = ((f32[8,72,128]{2,1,0:T(8,128)}), f32[8,72,128]{2,1,0:T(8,128)S(1)}, u32[]{:S(2)}, u32[]{:S(2)}) async-start(f32[8,72,128]{2,1,0:T(8,128)} %broadcast_in_dim.21), calls=%async_computation.5 | async-start | bytes 589824 | tf_op jit(solution)/shard_map/all_to_all | solution.py:314
  243.4 0.7 copy-start.2

commit v3 on v2

--- a/solution.py
+++ b/solution.py
@@ -3,6 +3,8 @@
 
 import jax
 import jax.numpy as jnp
+import ml_dtypes
+import numpy as np
 from jax import lax
 from jax.experimental import pallas as pl
 from jax.experimental.pallas import tpu as pltpu
@@ -13,19 +15,16 @@
 TOKS = 128
 K = 32768
 LANES = 128
+ROW_COST = 10_000_000
 STEP_EX = 8
 TAP = 256
-CHUNKS = 2
-
-
-def walsh_table(table_order):
-    row_index = lax.broadcasted_iota(jnp.int32, (table_order, table_order), 0)
-    column_index = lax.broadcasted_iota(jnp.int32, (table_order, table_order), 1)
-    common_bits = row_index & column_index
-    parity = jnp.zeros((table_order, table_order), jnp.int32)
-    for bit_index in range(table_order.bit_length() - 1):
-        parity = parity ^ common_bits >> bit_index & 1
-    return (1 - 2 * parity).astype(jnp.float32)
+
+
+def walsh_table(order):
+    table = np.ones((1, 1), np.float32)
+    while table.shape[0] < order:
+        table = np.block([[table, table], [table, -table]])
+    return table.astype(ml_dtypes.bfloat16)
 
 
 def butterfly(parts):
@@ -42,15 +41,21 @@
     return parts
 
 
-def table_kernel(n_ex, width, acts_ref, cots_ref, flip_ref, walsh_ref, table_ref, grad_ref):
+def table_kernel(n_ex, width, acts_ref, cots_ref, ids_ref, signs_ref, walsh_ref, table_ref, grad_ref, flip_ref):
     step = pl.program_id(0)
     tiles = width // LANES
     rows = SLAB
 
+    @pl.when(step == 0)
+    def _():
+        factor = 1.0 / math.sqrt(TOKS) / math.sqrt(SLAB * D)
+        flip_ref[...] = signs_ref[...].astype(jnp.float32) * factor
+
     @pl.loop(0, STEP_EX)
     def _(i):
         e = step * STEP_EX + i
-        g = jnp.dot(cots_ref[i], acts_ref[i], preferred_element_type=jnp.float32)
+        live = (ids_ref[pl.ds(i, 1), :] != 0).astype(jnp.bfloat16)
+        g = jnp.dot(cots_ref[i] * live, acts_ref[i], preferred_element_type=jnp.float32)
         g = g * flip_ref[...]
         for low in range(2):
             tile = [g[:, (2 * q + low) * LANES:(2 * q + low + 1) * LANES] for q in range(tiles // 2)]
@@ -88,26 +93,41 @@
                 table_ref[pl.ds((s * 4 + j) * width + q * TAP, TAP), :] = v
 
 
-def gather_kernel(n_block, rows_ref, table_ref, half_ref, sign_ref, out_ref, buf_ref):
-    @pl.loop(0, n_block)
-    def _(block):
+def gather_kernel(segments, start, rows_ref, table_ref, half_ref, sign_ref, *refs):
+    n_extra = sum(extra is not None for _, _, extra in segments)
+    extras, out_ref, bufs = refs[:n_extra], refs[-3], refs[-2:]
+    n_block = segments[-1][1]
+
+    def fetch(block, slot):
         base = pl.multiple_of(block * LANES, LANES)
         for j in range(LANES):
-            buf_ref[j:j + 1, :] = table_ref[pl.ds(rows_ref[base + j], 1), :]
-        t = buf_ref[...].T
-        here = pl.ds(block, 1)
-        picked = jnp.where(half_ref[here, :] > 0, t[LANES // 2:], t[:LANES // 2])
-        out_ref[block] = picked * sign_ref[here, :]
+            bufs[slot][j:j + 1, :] = table_ref[pl.ds(rows_ref[base + j], 1), :]
+
+    def finish(block, t, extra, first):
+        here = pl.ds(start + block, 1)
+        picked = jnp.where(half_ref[here, :] > 0, t[LANES // 2:], t[:LANES // 2]) * sign_ref[here, :]
+        out_ref[block] = picked if extra is None else picked + extras[extra][block - first]
+
+    fetch(0, 0)
+    for first, last, extra in segments:
+
+        @pl.loop(first // 2, last // 2)
+        def _(i):
+            t = bufs[0][...].T
+            fetch(2 * i + 1, 1)
+            finish(2 * i, t, extra, first)
+            t = bufs[1][...].T
+            fetch(jnp.minimum(2 * i + 2, n_block - 1), 0)
+            finish(2 * i + 1, t, extra, first)
 
 
 def whole(shape):
     return pl.BlockSpec(shape, lambda i, *_: (0,) * len(shape))
 
 
-def make_table(activations, cots, flip):
+def make_table(activations, cotangents, token_ids, signs):
     n_ex, toks, width = activations.shape
-    slab = cots.shape[1]
-    walsh = walsh_table(TAP).astype(jnp.bfloat16)
+    slab = cotangents.shape[2]
     return pl.pallas_call(
         functools.partial(table_kernel, n_ex, width),
         out_shape=pltpu.VMEM((slab // 2 * width, LANES), jnp.float32),
@@ -115,65 +135,100 @@
         in_specs=[
             pl.BlockSpec((STEP_EX, toks, width), lambda i: (i, 0, 0)),
             pl.BlockSpec((STEP_EX, slab, toks), lambda i: (i, 0, 0)),
+            pl.BlockSpec((STEP_EX, toks), lambda i: (i, 0)),
             whole((slab, width)),
             whole((TAP, TAP)),
         ],
         out_specs=pl.BlockSpec(memory_space=pltpu.VMEM),
-        scratch_shapes=[pltpu.VMEM((width // LANES, n_ex * slab, LANES), jnp.float32)],
+        scratch_shapes=[
+            pltpu.VMEM((width // LANES, n_ex * slab, LANES), jnp.float32),
+            pltpu.VMEM((slab, width), jnp.float32),
+        ],
         compiler_params=pltpu.CompilerParams(
             dimension_semantics=("arbitrary",), vmem_limit_bytes=30 * 1024 * 1024
         ),
         name="make_table",
-    )(activations, cots, flip, walsh)
-
-
-def gather_rows(table, rows, half, sign):
-    n_block = half.shape[0]
-    return pl.pallas_call(
-        functools.partial(gather_kernel, n_block),
+    )(activations, jnp.swapaxes(cotangents, 1, 2), token_ids, signs, jnp.asarray(walsh_table(TAP)))
+
+
+def gather_rows(table, index, core, first, count, after=(), add=()):
+    half, sign = index[:2]
+    rows = index[2 + core * 3 + max(first - 1, 0)]
+    unit = half.shape[0] // 8
+    n_block = count * unit
+    start = (core * 4 + first) * unit
+    segments, at = [], 0
+    for number, (low, high, _) in enumerate(add):
+        if at < low:
+            segments.append((at, low, None))
+        segments.append((low, high, number))
+        at = high
+    if at < n_block:
+        segments.append((at, n_block, None))
+    vmem = pl.BlockSpec(memory_space=pltpu.VMEM)
+    n_add = len(add)
+
+    def kernel(*refs):
+        gather_kernel(segments, start, *refs[:4 + n_add], *refs[4 + n_add + len(after):])
+
+    return pl.pallas_call(
+        kernel,
         out_shape=jax.ShapeDtypeStruct((n_block, LANES // 2, LANES), jnp.float32),
-        in_specs=[
-            pl.BlockSpec(memory_space=pltpu.SMEM),
-            pl.BlockSpec(memory_space=pltpu.VMEM),
-            pl.BlockSpec(memory_space=pltpu.VMEM),
-            pl.BlockSpec(memory_space=pltpu.VMEM),
-        ],
-        out_specs=pl.BlockSpec(memory_space=pltpu.VMEM),
-        scratch_shapes=[pltpu.VMEM((LANES, LANES), jnp.float32)],
-        compiler_params=pltpu.CompilerParams(vmem_limit_bytes=16 * 1024 * 1024),
+        in_specs=[pl.BlockSpec(memory_space=pltpu.SMEM)] + [vmem] * (3 + n_add) + [pl.BlockSpec(memory_space=pl.ANY)] * len(after),
+        out_specs=vmem,
+        scratch_shapes=[pltpu.VMEM((LANES, LANES), jnp.float32)] * 2,
+        compiler_params=pltpu.CompilerParams(vmem_limit_bytes=4 * 1024 * 1024),
+        cost_estimate=pl.CostEstimate(
+            flops=n_block * LANES * ROW_COST, bytes_accessed=n_block * LANES * 4096, transcendentals=0
+        ),
         name="gather_rows",
-    )(rows.reshape(-1), table, half, sign)
-
-
-def prepare(cotangents, token_ids, signs, select, my_index, width, section_bits):
-    live = token_ids != 0
-    cots = jnp.where(live[:, None, :], jnp.swapaxes(cotangents, 1, 2), jnp.zeros((), cotangents.dtype))
-    factor = 1.0 / math.sqrt(TOKS) / math.sqrt(SLAB * D)
-    flip = signs.astype(jnp.float32) * factor
-    column = select % D
-    row = select // D
-    rows = (row >> 1) * width + column % width
-    shared = (column // width) & my_index
-    parity = jnp.zeros_like(shared)
-    for bit_index in range(section_bits):
-        parity = parity ^ shared >> bit_index & 1
-    sign = (1 - 2 * parity).astype(jnp.float32)
-    return cots, flip, rows, row & 1, sign
-
-
-def test_local(a, c, t, s, sel, my):
-    cots, flip, rows, half, sign = prepare(c, t, s, sel, my, a.shape[2], 3)
-    table = make_table(a, cots, flip)
-    out = gather_rows(table, rows, half.reshape(-1, LANES), sign.reshape(-1, LANES))
-    return jnp.swapaxes(out, 0, 1).reshape(64, -1)
+    )(rows.reshape(-1), table, half, sign, *[x for _, _, x in add], *after)
+
+
+STEPS = (1, 3, 2, 0)
+
+
+def index_kernel(width, bits, me_ref, select_ref, half_ref, sign_ref, *rows_refs):
+    me = me_ref[0]
+    n_y, _, n_block, _ = select_ref.shape
+    col_bits, width_bits = D.bit_length() - 1, width.bit_length() - 1
+    for core in range(2):
+        owner_core = (me & 1) ^ (1 - core)
+        for place, step in enumerate(STEPS):
+            chosen = select_ref[((me >> 1) + step) & (n_y - 1), owner_core]
+            row = chosen >> col_bits
+            column = chosen & (D - 1)
+            shared = (column >> width_bits) & me
+            parity = jnp.zeros_like(shared)
+            for bit in range(bits):
+                parity = parity ^ (shared >> bit & 1)
+            here = pl.ds((core * n_y + place) * n_block, n_block)
+            rows_ref, first = rows_refs[core * 3 + max(place - 1, 0)], (place == 1) * n_block
+            rows_ref[first:first + n_block, :] = (row >> 1) * width + (column & (width - 1))
+            half_ref[here, :] = row & 1
+            sign_ref[here, :] = (1 - 2 * parity).astype(jnp.float32)
+
+
+def make_index(select, me, n_param, width):
+    n_block = select.shape[0] // LANES
+    vmem = pl.BlockSpec(memory_space=pltpu.VMEM)
+    return pl.pallas_call(
+        functools.partial(index_kernel, width, n_param.bit_length() - 1),
+        out_shape=(
+            jax.ShapeDtypeStruct((n_block, LANES), jnp.int32),
+            jax.ShapeDtypeStruct((n_block, LANES), jnp.float32),
+        ) + tuple(jax.ShapeDtypeStruct((n * n_block // n_param, LANES), jnp.int32) for n in (2, 1, 1)) * 2,
+        in_specs=[pl.BlockSpec(memory_space=pltpu.SMEM), vmem],
+        out_specs=(vmem,) * 8,
+        name="make_index",
+    )(me.reshape(1), select.reshape(n_param // 2, 2, n_block // n_param, LANES))
 
 
 def gram_kernel(n_ex, *refs):
-    x_refs, out_ref, high_ref, low_ref = refs[:-3], refs[-3], refs[-2], refs[-1]
-    blocks = x_refs[0].shape[0]
-    width = sum(r.shape[2] for r in x_refs)
+    x_ref, out_ref, high_ref, low_ref = refs
+    blocks = x_ref.shape[0]
     for b in range(blocks):
-        x = jnp.concatenate([r[b] for r in x_refs], axis=1)
+        x = jnp.concatenate([x_ref[b, j] for j in range(x_ref.shape[1])], axis=1)
         h = x.astype(jnp.bfloat16)
         low = (x - h.astype(jnp.float32)).astype(jnp.bfloat16)
         for at in ((b, b + blocks) if b < 10 else (b,)):
@@ -203,19 +258,19 @@
             out_ref[p, b, n_ex // 2:, :] = t[8 * p:8 * p + 8, :LANES]
 
 
-def partial_gram(parts):
-    blocks, n_ex, _ = parts[0].shape
-    width = sum(x.shape[2] for x in parts)
+def partial_gram(share):
+    blocks, lane_tiles, n_ex, _ = share.shape
+    width = lane_tiles * LANES
     vmem = pl.BlockSpec(memory_space=pltpu.VMEM)
     return pl.pallas_call(
         functools.partial(gram_kernel, n_ex),
         out_shape=jax.ShapeDtypeStruct((8, blocks, n_ex // 2 + 8, LANES), jnp.float32),
-        in_specs=[vmem] * len(parts),
+        in_specs=[vmem],
         out_specs=vmem,
         scratch_shapes=[pltpu.VMEM(((blocks + 10) * n_ex, width), jnp.bfloat16)] * 2,
         compiler_params=pltpu.CompilerParams(vmem_limit_bytes=16 * 1024 * 1024),
         name="partial_gram",
-    )(*parts)
+    )(share)
 
 
 def sum_kernel(scale, x_ref, tile_ref, strip_ref):
@@ -271,35 +326,39 @@
     n_param, n_group = lax.axis_size("param"), lax.axis_size("ex")
     n_ex, _, width = activations.shape
     me = lax.axis_index("param")
-    section_bits = n_param.bit_length() - 1
-    cots, flip, rows, half, sign = prepare(cotangents, token_ids, signs, select, me, width, section_bits)
-    table = make_table(activations, cots, flip)
-
-    n_y = n_param // 2
-    other_first = me % 2 == 0
-
-    def arrange(x):
-        x = x.reshape(n_y, 2, CHUNKS, n_group, -1)
-        even, odd = x[:, 0], x[:, 1]
-        x = jnp.stack([jnp.where(other_first, odd, even), jnp.where(other_first, even, odd)])
-        return jnp.moveaxis(x, 2, 0).reshape(CHUNKS, 2, n_y * n_group * x.shape[-1] // LANES, LANES)
-
-    rows, half, sign = arrange(rows), arrange(half), arrange(sign)
+    table = make_table(activations, cotangents, token_ids, signs)
+    index = make_index(select, me, n_param, width)
+    n_block = select.shape[0] // n_param // LANES
     swap = [(i, i ^ 1) for i in range(n_param)]
-    ring = [[2 * y + core for y in range(n_y)] for core in range(2)]
-    features, shares = [], []
-    for chunk in range(CHUNKS):
-        sent = gather_rows(table, rows[chunk, 0], half[chunk, 0], sign[chunk, 0])
-        arrived = lax.ppermute(sent, "param", swap)
-        kept = gather_rows(table, rows[chunk, 1], half[chunk, 1], sign[chunk, 1])
-        pair = (kept + arrived).reshape(n_y, -1, n_ex, LANES)
-        parts = lax.all_to_all(pair, "param", split_axis=0, concat_axis=0, axis_index_groups=ring)
-        block = parts[0] + parts[1] + parts[2] + parts[3]
-        features.append(block)
-        shares.append(lax.all_to_all(block, "ex", split_axis=0, concat_axis=0))
-    whole_features = jnp.swapaxes(jnp.concatenate(features, axis=0), 0, 1).reshape(n_ex, -1)
-
-    partial = partial_gram(shares)
+
+    def along(step):
+        return [(i, (i + 2 * step) % n_param) for i in range(n_param)]
+
+    mid = n_block // 2
+    sent = gather_rows(table, index, 0, 2, 1)
+    arrived = lax.ppermute(sent, "param", swap)
+    far = gather_rows(table, index, 1, 2, 1, after=(sent,)) + arrived
+    up = lax.ppermute(far[:mid], "param", along(1))
+    down = lax.ppermute(far[mid:], "param", along(-1))
+    sent = gather_rows(table, index, 0, 0, 2, after=(far,))
+    arrived = lax.ppermute(sent, "param", swap)
+    near = gather_rows(
+        table, index, 1, 0, 2, after=(sent,), add=((0, mid, up), (n_block + mid, 2 * n_block, down))
+    )
+    outward = near[:n_block] + arrived[:n_block]
+    from_below = lax.ppermute(outward, "param", along(1))
+    inward = near[n_block:] + arrived[n_block:]
+    from_above = lax.ppermute(inward, "param", along(-1))
+    sent = gather_rows(table, index, 0, 3, 1, after=(outward, inward))
+    arrived = lax.ppermute(sent, "param", swap)
+    own = gather_rows(table, index, 1, 3, 1, after=(sent,))
+    features = own + arrived + from_below + from_above
+    share = lax.all_to_all(
+        features.reshape(n_group, n_block // n_group, n_ex, LANES), "ex", split_axis=0, concat_axis=0
+    )
+    whole_features = jnp.swapaxes(features, 0, 1).reshape(n_ex, -1)
+
+    partial = partial_gram(share)
     rows_out = partial.shape[2]
     everyone = ("param", "ex")
     received = lax.all_to_all(

time: 247 us -> 203 us (0.82)
  Pallas kernels: 103 us -> 85.5 us
  waiting for transfers between devices: 43.8 us -> 26.7 us
  blocking collectives: 54.5 us -> 65 us
  other arithmetic: 11.6 us -> 1.21 us
  starting transfers between devices: 24.8 us -> 16.5 us
    all_to_all x3 -> x0, waiting for transfers between devices: 34.5 us -> none  [the longest x2 25.4 us: body(): lax.all_to_all(pair, 'param', split_axis=0, concat_axis=0, axis_index_gro...]
    pallas_call x4 -> x7, Pallas kernels: 55.2 us -> 37.5 us  [the longest x6 35.8 us: gather_rows(): pl.pallas_call(kernel, out_shape=jax.ShapeDtypeStruct((n_block, LANES //...]
    ppermute x0 -> x4, waiting for transfers between devices: none -> 16.4 us  [the longest x1 11 us: body(): from_below = lax.ppermute(outward, 'param', along(1))]
    all_to_all x3 -> x0, starting transfers between devices: 15.9 us -> none  [the longest x2 8.08 us: body(): lax.all_to_all(pair, 'param', split_axis=0, concat_axis=0, axis_index_gro...]
    all_to_all x1, blocking collectives: 11.9 us -> 23 us  [body(): lax.all_to_all(features.reshape(n_group, n_block // n_group, n_ex, LANES)...]
    add x4 -> x3, other arithmetic: 7.68 us -> 1.14 us  [the longest x1 0.55 us: body(): outward = near[:n_block] + arrived[:n_block]]
    ppermute x0 -> x4, starting transfers between devices: none -> 5.61 us  [the longest x1 2.87 us: body(): down = lax.ppermute(far[mid:], 'param', along(-1))]
    unnamed x12 -> x26, local copies, waits for them, and re-layouts: 6.49 us -> 4.57 us
  transfers between devices with their start and end apart: 7 -> 9, of which waited for: 5 -> 5; matrix products, arithmetic and copies ran while one was open for 4% -> 1% of each run, Pallas kernels for 17% -> 15%
where the time goes in v3:
time: 203 us; the launch traced here: 202 us
  Pallas kernels  85.5 us (42%)
  blocking collectives  65 us (32%)
  waiting for transfers between devices  26.7 us (13%)
  starting transfers between devices  16.5 us (8%)
  local copies, waits for them, and re-layouts  6.42 us (3%)
    all_to_all x1, blocking collectives, body(): lax.all_to_all(partial.reshape(n_param * n_group, rows_out, LANES), every...  42 us
    pallas_call x1, Pallas kernels, make_table(): pl.pallas_call(functools.partial(table_kernel, n_ex, width), out_shape=pl...  37.7 us
    pallas_call x6, Pallas kernels, gather_rows(): pl.pallas_call(kernel, out_shape=jax.ShapeDtypeStruct((n_block, LANES //...  35.8 us
    all_to_all x1, blocking collectives, body(): lax.all_to_all(features.reshape(n_group, n_block // n_group, n_ex, LANES)...  23 us
    ppermute x1, waiting for transfers between devices, body(): from_below = lax.ppermute(outward, 'param', along(1))  11 us
    pallas_call x1, Pallas kernels, partial_gram(): pl.pallas_call(functools.partial(gram_kernel, n_ex), out_shape=jax.ShapeD...  8.14 us
    all_to_all x1, waiting for transfers between devices, body(): lax.all_to_all(jnp.broadcast_to(message[None], (n_param,) + message.shape...  5.79 us
    all_to_all x1, starting transfers between devices, body(): lax.all_to_all(jnp.broadcast_to(message[None], (n_param,) + message.shape...  5.01 us
  transfers between devices with their start and end apart: 9, of which 5 were waited for; matrix products, arithmetic and copies ran while one was open for 1% of the time, Pallas kernels for 15%

profile of v3, /device:TPU:1, one launch (start us, length us, event | category | flops | bytes accessed | tf_op | source)
XLA Modules:
  0.0 202.2 jit_solution(4360142697781094718)
XLA Ops:
  0.6 1.7 make_index.1
  2.3 0.0 copy-start
  2.3 1.2 copy-done
  3.6 0.0 copy-start.1
  3.6 0.9 copy-done.1
  4.5 0.0 copy-start.2
  4.5 0.9 copy-done.2
  5.4 0.0 copy-start.3
  5.4 0.8 copy-done.3
  6.2 0.0 copy-start.4
  6.2 0.0 copy-start.5
  6.2 0.0 copy-start.11
  6.2 37.7 %make_table.1.refs_1_ = f32[32768,128]{1,0:T(8,128)S(1)} custom-call(bf16[64,128,1024]{2,1,0:T(8,128)(2,1)} %acts_ref.1, bf16[64,64,128]{2,1,0:T(8,128)(2,1)S(1)} %bitcast.23, s32[64,128]{1,0:T(8,128)S(1)} %copy-done.3, s32[64,1024]{1,0:T(8,128)S(1)} %copy-done.1, bf16[256,256]{1,0:T(8,128)(2,1)S(1)} %copy-done.2), custom_call_target="tpu_custom_call" | custom-call | tf_op jit(solution)/shard_map/make_table/pallas_call | solution.py:131
  43.9 0.0 copy-done.4
  43.9 0.0 copy-done.5
  43.9 0.0 copy-done.11
  44.0 0.0 copy-start.10
  44.0 4.6 %gather_rows.6.refs_4_ = f32[32,64,128]{2,1,0:T(8,128)S(1)} custom-call(s32[4096]{0:T(1024)S(1)} %bitcast.29, f32[32768,128]{1,0:T(8,128)S(1)} %make_table.1.refs_1_, s32[256,128]{1,0:T(8,128)S(1)} %copy-done.4, f32[256,128]{1,0:T(8,128)S(1)} %copy-done.5), custom_call_target="tpu_custom_call" | custom-call | flops 40960000000 | bytes 16777216 | tf_op jit(solution)/shard_map/gather_rows/pallas_call | solution.py:174
  48.6 1.5 collective-permute-start
  50.1 0.0 copy-done.10
  50.1 4.6 %gather_rows.7 = f32[32,64,128]{2,1,0:T(8,128)S(1)} custom-call(s32[4096]{0:T(1024)S(1)} %bitcast.28, f32[32768,128]{1,0:T(8,128)S(1)} %make_table.1.refs_1_, s32[256,128]{1,0:T(8,128)S(1)} %copy-done.4, f32[256,128]{1,0:T(8,128)S(1)} %copy-done.5, f32[32,64,128]{2,1,0:T(8,128)S(1)} %gather_rows.6.refs_4_), custom_call_target="tpu_custom_call" | custom-call | flops 40960000000 | bytes 16777216 | tf_op jit(solution)/shard_map/gather_rows/pallas_call | solution.py:174
  54.7 0.0 copy-start.7
  54.7 0.0 collective-permute-done
  54.7 0.2 add.18.refs_4_
  54.9 0.1 fusion
  55.0 2.9 %collective-permute-start.2 = (f32[16,64,128]{2,1,0:T(8,128)S(1)}, f32[16,64,128]{2,1,0:T(8,128)S(1)}, u32[]{:S(2)}, u32[]{:S(2)}) collective-permute-start(f32[16,64,128]{2,1,0:T(8,128)S(1)} %get-tuple-element.24), channel_id=1, source_target_pairs={{0,96},{16,112},{32,0},{48,16},{64,32},{80,48},{96,64},{112,80},{1... | collective-permute-start | bytes 1572872 | tf_op jit(solution)/shard_map/ppermute | solution.py:342
  57.9 0.0 collective-permute-start.1
  57.9 0.0 copy-done.7
  57.9 0.0 copy-start.6
  57.9 8.6 %gather_rows.8.refs_6_ = f32[64,64,128]{2,1,0:T(8,128)S(1)} custom-call(s32[8192]{0:T(1024)S(1)} %bitcast.25, f32[32768,128]{1,0:T(8,128)S(1)} %make_table.1.refs_1_, s32[256,128]{1,0:T(8,128)S(1)} %copy-done.4, f32[256,128]{1,0:T(8,128)S(1)} %copy-done.5, f32[32,64,128]{2,1,0:T(8,128)S(1)} %add.18.refs_4_), custom_call_target="tpu_custom_call" | custom-call | flops 81920000000 | bytes 33554432 | tf_op jit(solution)/shard_map/gather_rows/pallas_call | solution.py:174
  66.5 0.4 collective-permute-start.3
  66.9 2.3 %collective-permute-done.2.refs_5_ = f32[16,64,128]{2,1,0:T(8,128)S(1)} collective-permute-done((f32[16,64,128]{2,1,0:T(8,128)S(1)}, f32[16,64,128]{2,1,0:T(8,128)S(1)}, u32[]{:S(2)}, u32[]{:S(2)}) %collective-permute-start.2) | collective-permute-done | bytes 524320 | tf_op jit(solution)/shard_map/ppermute | solution.py:342
  69.2 3.1 %collective-permute-done.1.refs_4_ = f32[16,64,128]{2,1,0:T(8,128)S(1)} collective-permute-done((f32[16,64,128]{2,1,0:T(8,128)S(1)}, f32[16,64,128]{2,1,0:T(8,128)S(1)}, u32[]{:S(2)}, u32[]{:S(2)}) %collective-permute-start.1) | collective-permute-done | bytes 524320 | tf_op jit(solution)/shard_map/ppermute | solution.py:341
  72.3 0.0 copy-done.6
  72.3 8.7 %gather_rows.9 = f32[64,64,128]{2,1,0:T(8,128)S(1)} custom-call(s32[8192]{0:T(1024)S(1)} %bitcast.24, f32[32768,128]{1,0:T(8,128)S(1)} %make_table.1.refs_1_, s32[256,128]{1,0:T(8,128)S(1)} %copy-done.4, f32[256,128]{1,0:T(8,128)S(1)} %copy-done.5, f32[16,64,128]{2,1,0:T(8,128)S(1)} %collective-permute-done.1.refs_4_, ...), custom_call_target="tpu_custom_call" | custom-call | flops 81920000000 | bytes 33554432 | tf_op jit(solution)/shard_map/gather_rows/pallas_call | solution.py:174
  81.0 0.0 copy-start.9
  81.0 0.0 collective-permute-done.3
  81.0 0.6 slice_add_fusion.1
  81.6 0.1 collective-permute-start.5
  81.7 2.7 %collective-permute-start.6 = (f32[32,64,128]{2,1,0:T(8,128)S(1)}, f32[32,64,128]{2,1,0:T(8,128)S(1)}, u32[]{:S(2)}, u32[]{:S(2)}) collective-permute-start(f32[32,64,128]{2,1,0:T(8,128)S(1)} %get-tuple-element.23.refs_5_), channel_id=1, source_target_pairs={{0,96},{16,112},{32,0},{48,16},{64,32},{80,48},{96,64},{112,80},{1... | collective-permute-start | bytes 3145736 | tf_op jit(solution)/shard_map/ppermute | solution.py:351
  84.3 0.0 copy-done.9
  84.3 0.0 copy-start.8
  84.3 4.6 %gather_rows.10.refs_4_ = f32[32,64,128]{2,1,0:T(8,128)S(1)} custom-call(s32[4096]{0:T(1024)S(1)} %bitcast.27, f32[32768,128]{1,0:T(8,128)S(1)} %make_table.1.refs_1_, s32[256,128]{1,0:T(8,128)S(1)} %copy-done.4, f32[256,128]{1,0:T(8,128)S(1)} %copy-done.5, f32[32,64,128]{2,1,0:T(8,128)S(1)} %get-tuple-element.22.refs_4_, ...), custom_call_target="tpu_custom_call" | custom-call | flops 40960000000 | bytes 16777216 | tf_op jit(solution)/shard_map/gather_rows/pallas_call | solution.py:174
  88.9 1.8 collective-permute-start.4
  90.7 0.0 copy-done.8
  90.7 4.6 %gather_rows.11 = f32[32,64,128]{2,1,0:T(8,128)S(1)} custom-call(s32[4096]{0:T(1024)S(1)} %bitcast.26, f32[32768,128]{1,0:T(8,128)S(1)} %make_table.1.refs_1_, s32[256,128]{1,0:T(8,128)S(1)} %copy-done.4, f32[256,128]{1,0:T(8,128)S(1)} %copy-done.5, f32[32,64,128]{2,1,0:T(8,128)S(1)} %gather_rows.10.refs_4_), custom_call_target="tpu_custom_call" | custom-call | flops 40960000000 | bytes 16777216 | tf_op jit(solution)/shard_map/gather_rows/pallas_call | solution.py:174
  95.3 0.0 collective-permute-done.4
  95.3 11.0 %collective-permute-done.5 = f32[32,64,128]{2,1,0:T(8,128)S(1)} collective-permute-done((f32[32,64,128]{2,1,0:T(8,128)S(1)}, f32[32,64,128]{2,1,0:T(8,128)S(1)}, u32[]{:S(2)}, u32[]{:S(2)}) %collective-permute-start.5) | collective-permute-done | bytes 1048608 | tf_op jit(solution)/shard_map/ppermute | solution.py:349
  106.4 0.0 collective-permute-done.6
  106.4 0.4 add_add_fusion
  106.8 23.0 %all_to_all.15.refs_0_ = f32[16,2,64,128]{3,2,1,0:T(8,128)S(1)} all-to-all(f32[16,2,64,128]{3,2,1,0:T(8,128)S(1)} %bitcast.30), channel_id=1, replica_groups=mesh['param'=8,'ex'=16] {'ex'}, dimensions={0} | all-to-all | bytes 2097152 | tf_op jit(solution)/shard_map/all_to_all | solution.py:356
  129.8 8.1 %partial_gram.1 = f32[8,16,40,128]{3,2,1,0:T(8,128)S(1)} custom-call(f32[16,2,64,128]{3,2,1,0:T(8,128)S(1)} %all_to_all.15.refs_0_), custom_call_target="tpu_custom_call" | custom-call | tf_op jit(solution)/shard_map/partial_gram/pallas_call | solution.py:265
  137.9 42.0 %all_to_all.16.x_ref = f32[128,40,128]{2,1,0:T(8,128)S(1)} all-to-all(f32[128,40,128]{2,1,0:T(8,128)S(1)} %bitcast.22), channel_id=1, replica_groups=mesh['param'=8,'ex'=16] {'param','ex'}, dimensions={0} | all-to-all | bytes 5242880 | tf_op jit(solution)/shard_map/all_to_all | solution.py:364
  180.0 0.3 sum_tiles.1
  180.3 2.2 %collective-permute-start.7 = (f32[64,64]{1,0:T(8,128)S(1)}, f32[64,64]{1,0:T(8,128)S(1)}, u32[]{:S(2)}, u32[]{:S(2)}) collective-permute-start(f32[64,64]{1,0:T(8,128)S(1)} %get-tuple-element.27), channel_id=1, source_target_pairs={{0,1},{1,2},{2,3},{3,4},{4,5},{5,6},{6,7},{7,8},{8,9},{9,10},{10,1... | collective-permute-start | bytes 49160 | tf_op jit(solution)/shard_map/ppermute | solution.py:371
  182.5 4.5 %collective-permute-done.7 = f32[64,64]{1,0:T(8,128)S(1)} collective-permute-done((f32[64,64]{1,0:T(8,128)S(1)}, f32[64,64]{1,0:T(8,128)S(1)}, u32[]{:S(2)}, u32[]{:S(2)}) %collective-permute-start.7) | collective-permute-done | bytes 16416 | tf_op jit(solution)/shard_map/ppermute | solution.py:371
  187.0 0.1 pad_maximum_fusion
  187.1 0.7 broadcast_in_dim.2
  187.8 5.0 %all-to-all-start.2 = ((f32[8,72,128]{2,1,0:T(8,128)}), f32[8,72,128]{2,1,0:T(8,128)S(1)}, u32[]{:S(2)}, u32[]{:S(2)}) async-start(f32[8,72,128]{2,1,0:T(8,128)} %broadcast_in_dim.2), calls=%async_computation.2 | async-start | bytes 589824 | tf_op jit(solution)/shard_map/all_to_all | solution.py:373
  192.8 1.0 copy_bitcast_fusion
  193.9 5.8 %all-to-all-done.2.x_ref = f32[8,72,128]{2,1,0:T(8,128)S(1)} async-done(((f32[8,72,128]{2,1,0:T(8,128)}), f32[8,72,128]{2,1,0:T(8,128)S(1)}, u32[]{:S(2)}, u32[]{:S(2)}) %all-to-all-start.2) | async-done | bytes 294944 | tf_op jit(solution)/shard_map/all_to_all | solution.py:373
  199.7 0.0 copy-start.12
  199.7 0.7 copy-done.12
  200.4 1.9 place_tiles.1
  (1 shorter events, 0.0 us)
Async XLA Ops:
  2.3 1.2 copy-start
  3.6 0.9 copy-start.1
  4.5 0.9 copy-start.2
  5.4 0.8 copy-start.3
  6.2 37.7 %copy-start.4 = (s32[256,128]{1,0:T(8,128)S(1)}, s32[256,128]{1,0:T(8,128)}, u32[]{:S(2)}) copy-start(s32[256,128]{1,0:T(8,128)} %get-tuple-element.13.refs_2_) | copy-start | bytes 393220
  6.2 37.8 %copy-start.5 = (f32[256,128]{1,0:T(8,128)S(1)}, f32[256,128]{1,0:T(8,128)}, u32[]{:S(2)}) copy-start(f32[256,128]{1,0:T(8,128)} %get-tuple-element.14.refs_3_) | copy-start | bytes 393220
  6.2 37.8 %copy-start.11 = (s32[32,128]{1,0:T(8,128)S(1)}, s32[32,128]{1,0:T(8,128)}, u32[]{:S(2)}) copy-start(s32[32,128]{1,0:T(8,128)} %get-tuple-element.18) | copy-start | bytes 49156
  44.0 6.1 %copy-start.10 = (s32[32,128]{1,0:T(8,128)S(1)}, s32[32,128]{1,0:T(8,128)}, u32[]{:S(2)}) copy-start(s32[32,128]{1,0:T(8,128)} %get-tuple-element.17) | copy-start | bytes 49156
  48.6 6.1 %collective-permute-start = (f32[32,64,128]{2,1,0:T(8,128)S(1)}, f32[32,64,128]{2,1,0:T(8,128)S(1)}, u32[]{:S(2)}, u32[]{:S(2)}) collective-permute-start(f32[32,64,128]{2,1,0:T(8,128)S(1)} %gather_rows.6.refs_4_), channel_id=1, source_target_pairs={{0,16},{16,0},{32,48},{48,32},{64,80},{80,64},{96,112},{112,96},{1... | collective-permute-start | bytes 3145736 | tf_op jit(solution)/shard_map/ppermute | solution.py:339
  54.7 3.2 %copy-start.7 = (s32[64,128]{1,0:T(8,128)S(1)}, s32[64,128]{1,0:T(8,128)}, u32[]{:S(2)}) copy-start(s32[64,128]{1,0:T(8,128)} %get-tuple-element.19) | copy-start | bytes 98308
  55.0 14.2 %collective-permute-start.2 = (f32[16,64,128]{2,1,0:T(8,128)S(1)}, f32[16,64,128]{2,1,0:T(8,128)S(1)}, u32[]{:S(2)}, u32[]{:S(2)}) collective-permute-start(f32[16,64,128]{2,1,0:T(8,128)S(1)} %get-tuple-element.24), channel_id=1, source_target_pairs={{0,96},{16,112},{32,0},{48,16},{64,32},{80,48},{96,64},{112,80},{1... | collective-permute-start | bytes 1572872 | tf_op jit(solution)/shard_map/ppermute | solution.py:342
  57.9 14.4 %collective-permute-start.1 = (f32[16,64,128]{2,1,0:T(8,128)S(1)}, f32[16,64,128]{2,1,0:T(8,128)S(1)}, u32[]{:S(2)}, u32[]{:S(2)}) collective-permute-start(f32[16,64,128]{2,1,0:T(8,128)S(1)} %get-tuple-element.25), channel_id=1, source_target_pairs={{0,32},{16,48},{32,64},{48,80},{64,96},{80,112},{96,0},{112,16},{1... | collective-permute-start | bytes 1572872 | tf_op jit(solution)/shard_map/ppermute | solution.py:341
  57.9 14.4 %copy-start.6 = (s32[64,128]{1,0:T(8,128)S(1)}, s32[64,128]{1,0:T(8,128)}, u32[]{:S(2)}) copy-start(s32[64,128]{1,0:T(8,128)} %get-tuple-element.16) | copy-start | bytes 98308
  66.5 14.5 %collective-permute-start.3 = (f32[64,64,128]{2,1,0:T(8,128)S(1)}, f32[64,64,128]{2,1,0:T(8,128)S(1)}, u32[]{:S(2)}, u32[]{:S(2)}) collective-permute-start(f32[64,64,128]{2,1,0:T(8,128)S(1)} %gather_rows.8.refs_6_), channel_id=1, source_target_pairs={{0,16},{16,0},{32,48},{48,32},{64,80},{80,64},{96,112},{112,96},{1... | collective-permute-start | bytes 6291464 | tf_op jit(solution)/shard_map/ppermute | solution.py:344
  81.0 3.3 %copy-start.9 = (s32[32,128]{1,0:T(8,128)S(1)}, s32[32,128]{1,0:T(8,128)}, u32[]{:S(2)}) copy-start(s32[32,128]{1,0:T(8,128)} %get-tuple-element.15) | copy-start | bytes 49156
  81.6 24.8 %collective-permute-start.5 = (f32[32,64,128]{2,1,0:T(8,128)S(1)}, f32[32,64,128]{2,1,0:T(8,128)S(1)}, u32[]{:S(2)}, u32[]{:S(2)}) collective-permute-start(f32[32,64,128]{2,1,0:T(8,128)S(1)} %get-tuple-element.22.refs_4_), channel_id=1, source_target_pairs={{0,32},{16,48},{32,64},{48,80},{64,96},{80,112},{96,0},{112,16},{1... | collective-permute-start | bytes 3145736 | tf_op jit(solution)/shard_map/ppermute | solution.py:349
  81.7 24.7 %collective-permute-start.6 = (f32[32,64,128]{2,1,0:T(8,128)S(1)}, f32[32,64,128]{2,1,0:T(8,128)S(1)}, u32[]{:S(2)}, u32[]{:S(2)}) collective-permute-start(f32[32,64,128]{2,1,0:T(8,128)S(1)} %get-tuple-element.23.refs_5_), channel_id=1, source_target_pairs={{0,96},{16,112},{32,0},{48,16},{64,32},{80,48},{96,64},{112,80},{1... | collective-permute-start | bytes 3145736 | tf_op jit(solution)/shard_map/ppermute | solution.py:351
  84.3 6.4 %copy-start.8 = (s32[32,128]{1,0:T(8,128)S(1)}, s32[32,128]{1,0:T(8,128)}, u32[]{:S(2)}) copy-start(s32[32,128]{1,0:T(8,128)} %get-tuple-element.12) | copy-start | bytes 49156
  88.9 6.4 %collective-permute-start.4 = (f32[32,64,128]{2,1,0:T(8,128)S(1)}, f32[32,64,128]{2,1,0:T(8,128)S(1)}, u32[]{:S(2)}, u32[]{:S(2)}) collective-permute-start(f32[32,64,128]{2,1,0:T(8,128)S(1)} %gather_rows.10.refs_4_), channel_id=1, source_target_pairs={{0,16},{16,0},{32,48},{48,32},{64,80},{80,64},{96,112},{112,96},{1... | collective-permute-start | bytes 3145736 | tf_op jit(solution)/shard_map/ppermute | solution.py:353
  180.3 6.7 %collective-permute-start.7 = (f32[64,64]{1,0:T(8,128)S(1)}, f32[64,64]{1,0:T(8,128)S(1)}, u32[]{:S(2)}, u32[]{:S(2)}) collective-permute-start(f32[64,64]{1,0:T(8,128)S(1)} %get-tuple-element.27), channel_id=1, source_target_pairs={{0,1},{1,2},{2,3},{3,4},{4,5},{5,6},{6,7},{7,8},{8,9},{9,10},{10,1... | collective-permute-start | bytes 49160 | tf_op jit(solution)/shard_map/ppermute | solution.py:371
  187.8 11.8 %all-to-all-start.2 = ((f32[8,72,128]{2,1,0:T(8,128)}), f32[8,72,128]{2,1,0:T(8,128)S(1)}, u32[]{:S(2)}, u32[]{:S(2)}) async-start(f32[8,72,128]{2,1,0:T(8,128)} %broadcast_in_dim.2), calls=%async_computation.2 | async-start | bytes 589824 | tf_op jit(solution)/shard_map/all_to_all | solution.py:373
  199.7 0.7 copy-start.12

commit v4 on v3

--- a/solution.py
+++ b/solution.py
@@ -15,7 +15,7 @@
 TOKS = 128
 K = 32768
 LANES = 128
-ROW_COST = 10_000_000
+ROW_COST = 1_000_000_000
 STEP_EX = 8
 TAP = 256
 
@@ -145,18 +145,17 @@
             pltpu.VMEM((slab, width), jnp.float32),
         ],
         compiler_params=pltpu.CompilerParams(
-            dimension_semantics=("arbitrary",), vmem_limit_bytes=30 * 1024 * 1024
+            dimension_semantics=("arbitrary",), vmem_limit_bytes=46 * 1024 * 1024
         ),
         name="make_table",
     )(activations, jnp.swapaxes(cotangents, 1, 2), token_ids, signs, jnp.asarray(walsh_table(TAP)))
 
 
-def gather_rows(table, index, core, first, count, after=(), add=()):
+def gather_rows(table, index, core, group, after=(), add=()):
     half, sign = index[:2]
-    rows = index[2 + core * 3 + max(first - 1, 0)]
-    unit = half.shape[0] // 8
-    n_block = count * unit
-    start = (core * 4 + first) * unit
+    rows = index[2 + core * len(GROUPS) + group]
+    n_block = rows.shape[0]
+    start = (core * len(GROUPS) + group) * n_block
     segments, at = [], 0
     for number, (low, high, _) in enumerate(add):
         if at < low:
@@ -185,28 +184,31 @@
     )(rows.reshape(-1), table, half, sign, *[x for _, _, x in add], *after)
 
 
-STEPS = (1, 3, 2, 0)
+GROUPS = (((2, 0), (2, 1)), ((1, 0), (3, 0)), ((1, 1), (3, 1)), ((0, 0), (0, 1)))
+FAR, FIRST, SECOND, OWN = range(4)
 
 
 def index_kernel(width, bits, me_ref, select_ref, half_ref, sign_ref, *rows_refs):
     me = me_ref[0]
     n_y, _, n_block, _ = select_ref.shape
+    mid = n_block // 2
     col_bits, width_bits = D.bit_length() - 1, width.bit_length() - 1
     for core in range(2):
         owner_core = (me & 1) ^ (1 - core)
-        for place, step in enumerate(STEPS):
-            chosen = select_ref[((me >> 1) + step) & (n_y - 1), owner_core]
-            row = chosen >> col_bits
-            column = chosen & (D - 1)
-            shared = (column >> width_bits) & me
-            parity = jnp.zeros_like(shared)
-            for bit in range(bits):
-                parity = parity ^ (shared >> bit & 1)
-            here = pl.ds((core * n_y + place) * n_block, n_block)
-            rows_ref, first = rows_refs[core * 3 + max(place - 1, 0)], (place == 1) * n_block
-            rows_ref[first:first + n_block, :] = (row >> 1) * width + (column & (width - 1))
-            half_ref[here, :] = row & 1
-            sign_ref[here, :] = (1 - 2 * parity).astype(jnp.float32)
+        for group, pieces in enumerate(GROUPS):
+            for place, (step, part) in enumerate(pieces):
+                chosen = select_ref[((me >> 1) + step) & (n_y - 1), owner_core, part * mid:(part + 1) * mid, :]
+                row = chosen >> col_bits
+                column = chosen & (D - 1)
+                shared = (column >> width_bits) & me
+                parity = jnp.zeros_like(shared)
+                for bit in range(bits):
+                    parity = parity ^ (shared >> bit & 1)
+                here = pl.ds((core * len(GROUPS) + group) * n_block + place * mid, mid)
+                rows = (row >> 1) * width + (column & (width - 1))
+                rows_refs[core * len(GROUPS) + group][place * mid:(place + 1) * mid, :] = rows
+                half_ref[here, :] = row & 1
+                sign_ref[here, :] = (1 - 2 * parity).astype(jnp.float32)
 
 
 def make_index(select, me, n_param, width):
@@ -217,60 +219,68 @@
         out_shape=(
             jax.ShapeDtypeStruct((n_block, LANES), jnp.int32),
             jax.ShapeDtypeStruct((n_block, LANES), jnp.float32),
-        ) + tuple(jax.ShapeDtypeStruct((n * n_block // n_param, LANES), jnp.int32) for n in (2, 1, 1)) * 2,
+        ) + (jax.ShapeDtypeStruct((n_block // n_param, LANES), jnp.int32),) * n_param,
         in_specs=[pl.BlockSpec(memory_space=pltpu.SMEM), vmem],
-        out_specs=(vmem,) * 8,
+        out_specs=(vmem,) * (2 + n_param),
         name="make_index",
     )(me.reshape(1), select.reshape(n_param // 2, 2, n_block // n_param, LANES))
 
 
-def gram_kernel(n_ex, *refs):
-    x_ref, out_ref, high_ref, low_ref = refs
-    blocks = x_ref.shape[0]
+def gram_kernel(n_ex, core_ref, *refs):
+    x_refs, out_ref, high_ref, low_ref, part_ref = refs[:-4], refs[-4], refs[-3], refs[-2], refs[-1]
+    core = core_ref[0]
+    blocks = x_refs[0].shape[0]
+    half = LANES // 2
     for b in range(blocks):
-        x = jnp.concatenate([x_ref[b, j] for j in range(x_ref.shape[1])], axis=1)
+        x = jnp.concatenate([r[b] for r in x_refs], axis=1)
         h = x.astype(jnp.bfloat16)
         low = (x - h.astype(jnp.float32)).astype(jnp.bfloat16)
-        for at in ((b, b + blocks) if b < 10 else (b,)):
+        for at in ((b + 8, b - 8) if b >= 8 else (b + 8,)):
             high_ref[at * n_ex:(at + 1) * n_ex, :] = h
             low_ref[at * n_ex:(at + 1) * n_ex, :] = low
-    half = LANES // 2
     left = lax.broadcasted_iota(jnp.int32, (n_ex // 2, LANES), 1) < half
     nt = (((1,), (1,)), ((), ()))
 
-    @pl.loop(0, blocks)
-    def _(b):
-        first = pl.multiple_of(b * n_ex, n_ex)
-        mine = pl.ds(first, n_ex)
-        near = pl.ds(first, 10 * n_ex)
-        t = lax.dot_general(high_ref[mine, :], high_ref[near, :], nt, preferred_element_type=jnp.float32)
-        t += lax.dot_general(high_ref[mine, :], low_ref[near, :], nt, preferred_element_type=jnp.float32)
-        t += lax.dot_general(low_ref[mine, :], high_ref[near, :], nt, preferred_element_type=jnp.float32)
-        for p in range(8):
-            q = (p + 1) // 2
-            top = t[:n_ex // 2, q * LANES:(q + 1) * LANES]
-            low = t[n_ex // 2:, q * LANES:(q + 1) * LANES]
-            if p % 2:
-                low = pltpu.roll(low, half, 1)
-            else:
-                top = pltpu.roll(top, half, 1)
-            out_ref[p, b, :n_ex // 2, :] = jnp.where(left, top, low)
-            out_ref[p, b, n_ex // 2:, :] = t[8 * p:8 * p + 8, :LANES]
-
-
-def partial_gram(share):
-    blocks, lane_tiles, n_ex, _ = share.shape
-    width = lane_tiles * LANES
+    @pl.loop(0, blocks // 4)
+    def _(quad):
+        rows = pl.ds(pl.multiple_of(quad * 4 * n_ex, 4 * n_ex), 12 * n_ex)
+        columns = pl.ds(pl.multiple_of((quad * 4 + 8) * n_ex, 4 * n_ex), 4 * n_ex)
+        t = lax.dot_general(high_ref[rows, :], high_ref[columns, :], nt, preferred_element_type=jnp.float32)
+        t += lax.dot_general(high_ref[rows, :], low_ref[columns, :], nt, preferred_element_type=jnp.float32)
+        t += lax.dot_general(low_ref[rows, :], high_ref[columns, :], nt, preferred_element_type=jnp.float32)
+        part_ref[...] = t
+        for v in range(4):
+            lanes = slice(v // 2 * LANES, (v // 2 + 1) * LANES)
+            for m in range(4):
+                offset = 2 * m + core + 1
+                first = pl.multiple_of((8 + v - offset) * n_ex, n_ex)
+                top = part_ref[pl.ds(first, n_ex // 2), lanes]
+                low = part_ref[pl.ds(first + n_ex // 2, n_ex // 2), lanes]
+                strip = part_ref[pl.ds(pl.multiple_of((8 + v) * n_ex + 8 * (offset - 1), 8), 8), lanes]
+                if v % 2:
+                    top = pltpu.roll(top, half, 1)
+                    strip = pltpu.roll(strip, half, 1)
+                else:
+                    low = pltpu.roll(low, half, 1)
+                row_block = (quad * 4 + v + blocks - offset) & (blocks - 1)
+                out_ref[m, row_block, :n_ex // 2, :] = jnp.where(left, top, low)
+                out_ref[m, quad * 4 + v, n_ex // 2:, :] = strip
+
+
+def partial_gram(shares, core):
+    blocks, n_ex, _ = shares[0].shape
+    width = len(shares) * LANES
     vmem = pl.BlockSpec(memory_space=pltpu.VMEM)
     return pl.pallas_call(
         functools.partial(gram_kernel, n_ex),
-        out_shape=jax.ShapeDtypeStruct((8, blocks, n_ex // 2 + 8, LANES), jnp.float32),
-        in_specs=[vmem],
+        out_shape=jax.ShapeDtypeStruct((4, blocks, n_ex // 2 + 8, LANES), jnp.float32),
+        in_specs=[pl.BlockSpec(memory_space=pltpu.SMEM)] + [vmem] * len(shares),
         out_specs=vmem,
-        scratch_shapes=[pltpu.VMEM(((blocks + 10) * n_ex, width), jnp.bfloat16)] * 2,
+        scratch_shapes=[pltpu.VMEM(((blocks + 8) * n_ex, width), jnp.bfloat16)] * 2
+        + [pltpu.VMEM((12 * n_ex, 4 * n_ex), jnp.float32)],
         compiler_params=pltpu.CompilerParams(vmem_limit_bytes=16 * 1024 * 1024),
         name="partial_gram",
-    )(share)
+    )(core.reshape(1), *shares)
 
 
 def sum_kernel(scale, x_ref, tile_ref, strip_ref):
@@ -329,40 +339,51 @@
     table = make_table(activations, cotangents, token_ids, signs)
     index = make_index(select, me, n_param, width)
     n_block = select.shape[0] // n_param // LANES
+    n_y = n_param // 2
     swap = [(i, i ^ 1) for i in range(n_param)]
 
     def along(step):
         return [(i, (i + 2 * step) % n_param) for i in range(n_param)]
 
     mid = n_block // 2
-    sent = gather_rows(table, index, 0, 2, 1)
+    sent = gather_rows(table, index, 0, FAR)
     arrived = lax.ppermute(sent, "param", swap)
-    far = gather_rows(table, index, 1, 2, 1, after=(sent,)) + arrived
-    up = lax.ppermute(far[:mid], "param", along(1))
-    down = lax.ppermute(far[mid:], "param", along(-1))
-    sent = gather_rows(table, index, 0, 0, 2, after=(far,))
+    far = gather_rows(table, index, 1, FAR, after=(sent,))
+    outward = (far[:mid] + arrived[:mid], far[mid:] + arrived[mid:])
+    up, down = lax.ppermute(outward[0], "param", along(1)), lax.ppermute(outward[1], "param", along(-1))
+    sent_first = gather_rows(table, index, 0, FIRST, after=outward)
+    arrived_first = lax.ppermute(sent_first, "param", swap)
+    sent_second = gather_rows(table, index, 0, SECOND, after=(sent_first,))
+    arrived_second = lax.ppermute(sent_second, "param", swap)
+    first = gather_rows(table, index, 1, FIRST, after=(sent_second,), add=((0, mid, up),))
+    outward = (first[:mid] + arrived_first[:mid], first[mid:] + arrived_first[mid:])
+    first = lax.ppermute(outward[0], "param", along(1)), lax.ppermute(outward[1], "param", along(-1))
+    second = gather_rows(table, index, 1, SECOND, after=outward, add=((mid, n_block, down),))
+    outward = (second[:mid] + arrived_second[:mid], second[mid:] + arrived_second[mid:])
+    second = lax.ppermute(outward[0], "param", along(1)), lax.ppermute(outward[1], "param", along(-1))
+    sent = gather_rows(table, index, 0, OWN, after=outward)
     arrived = lax.ppermute(sent, "param", swap)
-    near = gather_rows(
-        table, index, 1, 0, 2, after=(sent,), add=((0, mid, up), (n_block + mid, 2 * n_block, down))
-    )
-    outward = near[:n_block] + arrived[:n_block]
-    from_below = lax.ppermute(outward, "param", along(1))
-    inward = near[n_block:] + arrived[n_block:]
-    from_above = lax.ppermute(inward, "param", along(-1))
-    sent = gather_rows(table, index, 0, 3, 1, after=(outward, inward))
-    arrived = lax.ppermute(sent, "param", swap)
-    own = gather_rows(table, index, 1, 3, 1, after=(sent,))
-    features = own + arrived + from_below + from_above
-    share = lax.all_to_all(
-        features.reshape(n_group, n_block // n_group, n_ex, LANES), "ex", split_axis=0, concat_axis=0
-    )
-    whole_features = jnp.swapaxes(features, 0, 1).reshape(n_ex, -1)
-
-    partial = partial_gram(share)
+    own = gather_rows(table, index, 1, OWN, after=(sent,))
+    front = own[:mid] + arrived[:mid] + first[0] + first[1]
+    own, arrived, front = lax.optimization_barrier((own, arrived, front))
+    back = own[mid:] + arrived[mid:] + second[0] + second[1]
+    features = (front, back)
+    shares = [lax.all_to_all(x, "ex", split_axis=0, concat_axis=0) for x in features]
+    shares += [lax.ppermute(x, "param", swap) for x in shares]
+    whole_features = jnp.swapaxes(jnp.concatenate(features, axis=0), 0, 1).reshape(n_ex, -1)
+
+    partial = partial_gram(shares, me % 2)
     rows_out = partial.shape[2]
     everyone = ("param", "ex")
+    alike = [
+        [(2 * y + core) * n_group + e for y in range(n_y) for e in range(n_group)] for core in range(2)
+    ]
     received = lax.all_to_all(
-        partial.reshape(n_param * n_group, rows_out, LANES), everyone, split_axis=0, concat_axis=0
+        partial.reshape(n_y * n_group, rows_out, LANES),
+        everyone,
+        split_axis=0,
+        concat_axis=0,
+        axis_index_groups=alike,
     )
     tile, strip = sum_tiles(received)
     onward = [

time: 203 us -> 194 us (0.956)
  blocking collectives: 65 us -> 25 us
  starting transfers between devices: 16.5 us -> 33 us
  other arithmetic: 1.21 us -> 14 us
  waiting for transfers between devices: 26.7 us -> 31.9 us
  local copies, waits for them, and re-layouts: 6.42 us -> 1.49 us
    all_to_all x2 -> x1, blocking collectives: 65 us -> 25 us  [body(): lax.all_to_all(partial.reshape(n_y * n_group, rows_out, LANES), everyone,...]
    all_to_all x0 -> x2, waiting for transfers between devices: none -> 17.5 us  [body(): lax.all_to_all(x, 'ex', split_axis=0, concat_axis=0)]
    ppermute x4 -> x10, waiting for transfers between devices: 16.4 us -> 4.63 us  [the longest x3 3.08 us: body(): lax.ppermute(outward[0], 'param', along(1))]
    all_to_all x0 -> x2, starting transfers between devices: none -> 11.2 us  [body(): lax.all_to_all(x, 'ex', split_axis=0, concat_axis=0)]
    add x3 -> x5, other arithmetic: 1.14 us -> 11.7 us  [the longest x1 2.37 us: body(): first[mid:] + arrived_first[mid:]]
    ppermute x4 -> x10, starting transfers between devices: 5.61 us -> 11.2 us  [the longest x3 5.49 us: body(): lax.ppermute(outward[1], 'param', along(-1))]
    pallas_call x6 -> x8, Pallas kernels: 35.8 us -> 41.4 us  [gather_rows(): pl.pallas_call(kernel, out_shape=jax.ShapeDtypeStruct((n_block, LANES //...]
    pallas_call x1, Pallas kernels: 8.14 us -> 4.06 us  [partial_gram(): pl.pallas_call(functools.partial(gram_kernel, n_ex), out_shape=jax.ShapeD...]
  transfers between devices with their start and end apart: 9 -> 16, of which waited for: 5 -> 6; matrix products, arithmetic and copies ran while one was open for 1% -> 6% of each run, Pallas kernels for 15% -> 19%
where the time goes in v4:
time: 194 us; the launch traced here: 193 us
  Pallas kernels  87.2 us (45%)
  starting transfers between devices  33 us (17%)
  waiting for transfers between devices  31.9 us (16%)
  blocking collectives  25 us (13%)
  other arithmetic  14 us (7%)
    pallas_call x8, Pallas kernels, gather_rows(): pl.pallas_call(kernel, out_shape=jax.ShapeDtypeStruct((n_block, LANES //...  41.4 us
    pallas_call x1, Pallas kernels, make_table(): pl.pallas_call(functools.partial(table_kernel, n_ex, width), out_shape=pl...  38 us
    all_to_all x1, blocking collectives, body(): lax.all_to_all(partial.reshape(n_y * n_group, rows_out, LANES), everyone,...  25 us
    all_to_all x2, waiting for transfers between devices, body(): lax.all_to_all(x, 'ex', split_axis=0, concat_axis=0)  17.5 us
    all_to_all x2, starting transfers between devices, body(): lax.all_to_all(x, 'ex', split_axis=0, concat_axis=0)  11.2 us
    all_to_all x1, starting transfers between devices, body(): lax.all_to_all(jnp.broadcast_to(message[None], (n_param,) + message.shape...  5.67 us
    ppermute x3, starting transfers between devices, body(): lax.ppermute(outward[1], 'param', along(-1))  5.49 us
    ppermute x1, waiting for transfers between devices, body(): turned = lax.ppermute(tile[1], everyone, onward)  5.2 us
  transfers between devices with their start and end apart: 16, of which 6 were waited for; matrix products, arithmetic and copies ran while one was open for 6% of the time, Pallas kernels for 19%

profile of v4, /device:TPU:1, one launch (start us, length us, event | category | flops | bytes accessed | tf_op | source)
XLA Modules:
  0.0 193.4 jit_solution(16814561054876696914)
XLA Ops:
  0.6 1.7 make_index.1
  2.3 0.0 copy-start
  2.4 0.0 copy-start.1
  2.4 38.0 %make_table.1.refs_1_ = f32[32768,128]{1,0:T(8,128)S(1)} custom-call(bf16[64,128,1024]{2,1,0:T(8,128)(2,1)} %acts_ref.1, bf16[64,64,128]{2,1,0:T(8,128)(2,1)} %bitcast.33, s32[64,128]{1,0:T(8,128)} %ids_ref.1, s32[64,1024]{1,0:T(8,128)} %signs_ref.1, bf16[256,256]{1,0:T(8,128)(2,1)} %constant.24.clone.walsh_ref), custom_call_target="tpu_custom_call" | custom-call | tf_op jit(solution)/shard_map/make_table/pallas_call | solution.py:131
  40.4 0.0 copy-done
  40.4 0.0 copy-done.1
  40.4 0.0 copy-done.9
  40.4 0.0 copy-start.8
  40.4 5.6 %gather_rows.8.refs_4_ = f32[32,64,128]{2,1,0:T(8,128)} custom-call(s32[4096]{0:T(1024)S(1)} %bitcast.32, f32[32768,128]{1,0:T(8,128)S(1)} %make_table.1.refs_1_, s32[256,128]{1,0:T(8,128)S(1)} %copy-done, f32[256,128]{1,0:T(8,128)S(1)} %copy-done.1), custom_call_target="tpu_custom_call" | custom-call | flops 4096000000000 | bytes 16777216 | tf_op jit(solution)/shard_map/gather_rows/pallas_call | solution.py:173
  46.0 1.4 collective-permute-start
  47.4 0.0 copy-done.8
  47.4 4.6 %gather_rows.9 = f32[32,64,128]{2,1,0:T(8,128)S(1)} custom-call(s32[4096]{0:T(1024)S(1)} %bitcast.31, f32[32768,128]{1,0:T(8,128)S(1)} %make_table.1.refs_1_, s32[256,128]{1,0:T(8,128)S(1)} %copy-done, f32[256,128]{1,0:T(8,128)S(1)} %copy-done.1, f32[32,64,128]{2,1,0:T(8,128)} %gather_rows.8.refs_4_), custom_call_target="tpu_custom_call" | custom-call | flops 4096000000000 | bytes 16777216 | tf_op jit(solution)/shard_map/gather_rows/pallas_call | solution.py:173
  52.0 0.0 collective-permute-done
  52.0 2.3 %slice_add_fusion.6 = (f32[16,64,128]{2,1,0:T(8,128)}, f32[16,64,128]{2,1,0:T(8,128)}) fusion(f32[32,64,128]{2,1,0:T(8,128)} %collective-permute-done, f32[32,64,128]{2,1,0:T(8,128)S(1)} %gather_rows.9), kind=kLoop, calls=%fused_computation.10 | loop fusion | flops 262144 | bytes 3145728 | tf_op jit(solution)/shard_map/add | solution.py:352
  54.4 2.8 %collective-permute-start.1 = (f32[16,64,128]{2,1,0:T(8,128)}, f32[16,64,128]{2,1,0:T(8,128)}, u32[]{:S(2)}, u32[]{:S(2)}) collective-permute-start(f32[16,64,128]{2,1,0:T(8,128)} %get-tuple-element.36.refs_5_), channel_id=1, source_target_pairs={{0,96},{16,112},{32,0},{48,16},{64,32},{80,48},{96,64},{112,80},{1... | collective-permute-start | bytes 1572872 | tf_op jit(solution)/shard_map/ppermute | solution.py:353
  57.2 0.0 collective-permute-start.2
  57.2 5.6 %gather_rows.10.refs_4_ = f32[32,64,128]{2,1,0:T(8,128)} custom-call(s32[4096]{0:T(1024)S(1)} %bitcast.30, f32[32768,128]{1,0:T(8,128)S(1)} %make_table.1.refs_1_, s32[256,128]{1,0:T(8,128)S(1)} %copy-done, f32[256,128]{1,0:T(8,128)S(1)} %copy-done.1, f32[16,64,128]{2,1,0:T(8,128)} %get-tuple-element.37.refs_4_, f32[16,64,128]{2,1,0:T(8,128)} %get-tuple-element.36.refs_5_), custom_call_target="tpu_custom_call" | custom-call | flops 4096000000000 | bytes 16777216 | tf_op jit(solution)/shard_map/gather_rows/pallas_call | solution.py:173
  62.8 0.3 collective-permute-start.3
  63.1 0.0 copy-done.6
  63.1 5.6 %gather_rows.11.refs_5_ = f32[32,64,128]{2,1,0:T(8,128)} custom-call(s32[4096]{0:T(1024)S(1)} %bitcast.29, f32[32768,128]{1,0:T(8,128)S(1)} %make_table.1.refs_1_, s32[256,128]{1,0:T(8,128)S(1)} %copy-done, f32[256,128]{1,0:T(8,128)S(1)} %copy-done.1, f32[32,64,128]{2,1,0:T(8,128)} %gather_rows.10.refs_4_), custom_call_target="tpu_custom_call" | custom-call | flops 4096000000000 | bytes 16777216 | tf_op jit(solution)/shard_map/gather_rows/pallas_call | solution.py:173
  68.7 0.2 collective-permute-start.4
  68.9 3.1 %collective-permute-done.2.refs_4_ = f32[16,64,128]{2,1,0:T(8,128)} collective-permute-done((f32[16,64,128]{2,1,0:T(8,128)}, f32[16,64,128]{2,1,0:T(8,128)}, u32[]{:S(2)}, u32[]{:S(2)}) %collective-permute-start.2) | collective-permute-done | bytes 524320 | tf_op jit(solution)/shard_map/ppermute | solution.py:353
  72.0 4.9 %gather_rows.12 = f32[32,64,128]{2,1,0:T(8,128)S(1)} custom-call(s32[4096]{0:T(1024)S(1)} %bitcast.28, f32[32768,128]{1,0:T(8,128)S(1)} %make_table.1.refs_1_, s32[256,128]{1,0:T(8,128)S(1)} %copy-done, f32[256,128]{1,0:T(8,128)S(1)} %copy-done.1, f32[16,64,128]{2,1,0:T(8,128)} %collective-permute-done.2.refs_4_, f32[32,64,128]{2,1,0:T(8,128)} %gather_rows.11.refs_5_), custom_call_target="tpu_custom_call" | custom-call | flops 4096000000000 | bytes 16777216 | tf_op jit(solution)/shard_map/gather_rows/pallas_call | solution.py:173
  76.9 0.0 collective-permute-done.3
  76.9 2.4 %slice_add_fusion.3 = (f32[16,64,128]{2,1,0:T(8,128)}, f32[16,64,128]{2,1,0:T(8,128)}) fusion(f32[32,64,128]{2,1,0:T(8,128)} %collective-permute-done.3, f32[32,64,128]{2,1,0:T(8,128)S(1)} %gather_rows.12), kind=kLoop, calls=%fused_computation.7 | loop fusion | flops 262144 | bytes 3145728 | tf_op jit(solution)/shard_map/add | solution.py:359
  79.3 0.0 collective-permute-start.7
  79.3 1.5 collective-permute-start.6
  80.7 0.0 collective-permute-done.1.refs_4_
  80.7 4.9 %gather_rows.13 = f32[32,64,128]{2,1,0:T(8,128)S(1)} custom-call(s32[4096]{0:T(1024)S(1)} %bitcast.27, f32[32768,128]{1,0:T(8,128)S(1)} %make_table.1.refs_1_, s32[256,128]{1,0:T(8,128)S(1)} %copy-done, f32[256,128]{1,0:T(8,128)S(1)} %copy-done.1, f32[16,64,128]{2,1,0:T(8,128)} %collective-permute-done.1.refs_4_, f32[16,64,128]{2,1,0:T(8,128)} %get-tuple-element.35.refs_5_, ...), custom_call_target="tpu_custom_call" | custom-call | flops 4096000000000 | bytes 16777216 | tf_op jit(solution)/shard_map/gather_rows/pallas_call | solution.py:173
  85.7 0.0 collective-permute-done.4
  85.7 2.3 %slice_add_fusion.2 = (f32[16,64,128]{2,1,0:T(8,128)}, f32[16,64,128]{2,1,0:T(8,128)}) fusion(f32[32,64,128]{2,1,0:T(8,128)} %collective-permute-done.4, f32[32,64,128]{2,1,0:T(8,128)S(1)} %gather_rows.13), kind=kLoop, calls=%fused_computation.6 | loop fusion | flops 262144 | bytes 3145728 | tf_op jit(solution)/shard_map/add | solution.py:362
  88.0 0.0 collective-permute-start.8
  88.0 2.7 %collective-permute-start.9 = (f32[16,64,128]{2,1,0:T(8,128)}, f32[16,64,128]{2,1,0:T(8,128)}, u32[]{:S(2)}, u32[]{:S(2)}) collective-permute-start(f32[16,64,128]{2,1,0:T(8,128)} %get-tuple-element.33.refs_5_), channel_id=1, source_target_pairs={{0,96},{16,112},{32,0},{48,16},{64,32},{80,48},{96,64},{112,80},{1... | collective-permute-start | bytes 1572872 | tf_op jit(solution)/shard_map/ppermute | solution.py:363
  90.6 0.0 copy-done.3
  90.6 5.6 %gather_rows.14.refs_4_ = f32[32,64,128]{2,1,0:T(8,128)} custom-call(s32[4096]{0:T(1024)S(1)} %bitcast.26, f32[32768,128]{1,0:T(8,128)S(1)} %make_table.1.refs_1_, s32[256,128]{1,0:T(8,128)S(1)} %copy-done, f32[256,128]{1,0:T(8,128)S(1)} %copy-done.1, f32[16,64,128]{2,1,0:T(8,128)} %get-tuple-element.32.refs_4_, f32[16,64,128]{2,1,0:T(8,128)} %get-tuple-element.33.refs_5_), custom_call_target="tpu_custom_call" | custom-call | flops 4096000000000 | bytes 16777216 | tf_op jit(solution)/shard_map/gather_rows/pallas_call | solution.py:173
  96.2 2.2 %collective-permute-start.5 = (f32[32,64,128]{2,1,0:T(8,128)}, f32[32,64,128]{2,1,0:T(8,128)}, u32[]{:S(2)}, u32[]{:S(2)}) collective-permute-start(f32[32,64,128]{2,1,0:T(8,128)} %gather_rows.14.refs_4_), channel_id=1, source_target_pairs={{0,16},{16,0},{32,48},{48,32},{64,80},{80,64},{96,112},{112,96},{1... | collective-permute-start | bytes 3145736 | tf_op jit(solution)/shard_map/ppermute | solution.py:365
  98.4 4.6 %gather_rows.15 = f32[32,64,128]{2,1,0:T(8,128)S(1)} custom-call(s32[4096]{0:T(1024)S(1)} %bitcast.25, f32[32768,128]{1,0:T(8,128)S(1)} %make_table.1.refs_1_, s32[256,128]{1,0:T(8,128)S(1)} %copy-done, f32[256,128]{1,0:T(8,128)S(1)} %copy-done.1, f32[32,64,128]{2,1,0:T(8,128)} %gather_rows.14.refs_4_), custom_call_target="tpu_custom_call" | custom-call | flops 4096000000000 | bytes 16777216 | tf_op jit(solution)/shard_map/gather_rows/pallas_call | solution.py:173
  103.1 0.0 collective-permute-done.7
  103.1 0.0 collective-permute-done.6
  103.1 0.0 collective-permute-done.5
  103.1 2.3 %fusion.1 = f32[16,64,128]{2,1,0:T(8,128)} fusion(f32[16,64,128]{2,1,0:T(8,128)} %collective-permute-done.7, f32[16,64,128]{2,1,0:T(8,128)} %collective-permute-done.6, f32[32,64,128]{2,1,0:T(8,128)} %collective-permute-done.5, f32[32,64,128]{2,1,0:T(8,128)S(1)} %gather_rows.15), kind=kLoop, calls=%fused_computation.4 | loop fusion | flops 393216 | bytes 2621440 | tf_op jit(solution)/shard_map/add | solution.py:367
  105.4 7.6 %all-to-all-start = ((f32[16,64,128]{2,1,0:T(8,128)}), f32[16,64,128]{2,1,0:T(8,128)S(1)}, u32[]{:S(2)}, u32[]{:S(2)}) async-start(f32[16,64,128]{2,1,0:T(8,128)} %fusion.1), calls=%async_computation | async-start | bytes 1048576 | tf_op jit(solution)/shard_map/all_to_all | solution.py:371
  113.0 0.0 collective-permute-done.8
  113.0 0.0 collective-permute-done.9
  113.1 2.3 %add_add_fusion = f32[16,64,128]{2,1,0:T(8,128)} fusion(f32[16,64,128]{2,1,0:T(8,128)} %collective-permute-done.9, f32[16,64,128]{2,1,0:T(8,128)} %collective-permute-done.8, f32[32,64,128]{2,1,0:T(8,128)} %collective-permute-done.5, f32[32,64,128]{2,1,0:T(8,128)S(1)} %gather_rows.15), kind=kLoop, calls=%fused_computation.11 | loop fusion | flops 393216 | bytes 2621440 | tf_op jit(solution)/shard_map/add | solution.py:369
  115.4 8.8 %all-to-all-done.refs_0_ = f32[16,64,128]{2,1,0:T(8,128)S(1)} async-done(((f32[16,64,128]{2,1,0:T(8,128)}), f32[16,64,128]{2,1,0:T(8,128)S(1)}, u32[]{:S(2)}, u32[]{:S(2)}) %all-to-all-start) | async-done | bytes 524320 | tf_op jit(solution)/shard_map/all_to_all | solution.py:371
  124.1 3.6 %all-to-all-start.1 = ((f32[16,64,128]{2,1,0:T(8,128)}), f32[16,64,128]{2,1,0:T(8,128)S(1)}, u32[]{:S(2)}, u32[]{:S(2)}) async-start(f32[16,64,128]{2,1,0:T(8,128)} %add_add_fusion), calls=%async_computation.1 | async-start | bytes 1048576 | tf_op jit(solution)/shard_map/all_to_all | solution.py:371
  127.7 1.5 collective-permute-start.10
  129.2 8.7 %all-to-all-done.1.refs_1_ = f32[16,64,128]{2,1,0:T(8,128)S(1)} async-done(((f32[16,64,128]{2,1,0:T(8,128)}), f32[16,64,128]{2,1,0:T(8,128)S(1)}, u32[]{:S(2)}, u32[]{:S(2)}) %all-to-all-start.1) | async-done | bytes 524320 | tf_op jit(solution)/shard_map/all_to_all | solution.py:371
  137.9 2.3 %collective-permute-start.11 = (f32[16,64,128]{2,1,0:T(8,128)S(1)}, f32[16,64,128]{2,1,0:T(8,128)S(1)}, u32[]{:S(2)}, u32[]{:S(2)}) collective-permute-start(f32[16,64,128]{2,1,0:T(8,128)S(1)} %all-to-all-done.1.refs_1_), channel_id=1, source_target_pairs={{0,16},{16,0},{32,48},{48,32},{64,80},{80,64},{96,112},{112,96},{1... | collective-permute-start | bytes 1572872 | tf_op jit(solution)/shard_map/ppermute | solution.py:372
  140.2 0.0 collective-permute-done.10.refs_2_
  140.2 1.5 collective-permute-done.11.refs_3_
  141.7 4.1 %partial_gram.1 = f32[4,16,40,128]{3,2,1,0:T(8,128)S(1)} custom-call(s32[1]{0:T(128)} %bitcast.13.core_ref, f32[16,64,128]{2,1,0:T(8,128)S(1)} %all-to-all-done.refs_0_, f32[16,64,128]{2,1,0:T(8,128)S(1)} %all-to-all-done.1.refs_1_, f32[16,64,128]{2,1,0:T(8,128)S(1)} %collective-permute-done.10.refs_2_, f32[16,64,128]{2,1,0:T(8,128)S(1)} %collective-permute-done.11.refs_3_), custom_call_target="tpu_custom_call" | custom-call | tf_op jit(solution)/shard_map/partial_gram/pallas_call | solution.py:274
  145.8 25.0 %all_to_all.20.x_ref = f32[64,40,128]{2,1,0:T(8,128)S(1)} all-to-all(f32[64,40,128]{2,1,0:T(8,128)S(1)} %bitcast.24), channel_id=1, replica_groups={{0,1,2,3,4,5,6,7,8,9,10,11,12,13,14,15,32,33,34,35,36,37,38,39,40,41,42..., dimensions={0} | all-to-all | bytes 2621440 | tf_op jit(solution)/shard_map/all_to_all | solution.py:381
  170.8 0.2 sum_tiles.1
  171.0 1.3 collective-permute-start.12
  172.3 5.2 %collective-permute-done.12 = f32[64,64]{1,0:T(8,128)S(1)} collective-permute-done((f32[64,64]{1,0:T(8,128)S(1)}, f32[64,64]{1,0:T(8,128)S(1)}, u32[]{:S(2)}, u32[]{:S(2)}) %collective-permute-start.12) | collective-permute-done | bytes 16416 | tf_op jit(solution)/shard_map/ppermute | solution.py:392
  177.5 0.1 pad_maximum_fusion
  177.6 0.7 broadcast_in_dim.2
  178.3 5.7 %all-to-all-start.3 = ((f32[8,72,128]{2,1,0:T(8,128)}), f32[8,72,128]{2,1,0:T(8,128)S(1)}, u32[]{:S(2)}, u32[]{:S(2)}) async-start(f32[8,72,128]{2,1,0:T(8,128)} %broadcast_in_dim.2), calls=%async_computation.3 | async-start | bytes 589824 | tf_op jit(solution)/shard_map/all_to_all | solution.py:394
  184.0 2.2 %copy_bitcast_fusion = f32[64,4096]{1,0:T(8,128)} fusion(f32[16,64,128]{2,1,0:T(8,128)} %add_add_fusion, f32[16,64,128]{2,1,0:T(8,128)} %fusion.1), kind=kLoop, calls=%fused_computation | loop fusion | flops 262144 | bytes 2097152 | tf_op jit(solution)/shard_map/reshape | solution.py:373
  186.2 4.6 %all-to-all-done.3.x_ref = f32[8,72,128]{2,1,0:T(8,128)S(1)} async-done(((f32[8,72,128]{2,1,0:T(8,128)}), f32[8,72,128]{2,1,0:T(8,128)S(1)}, u32[]{:S(2)}, u32[]{:S(2)}) %all-to-all-start.3) | async-done | bytes 294944 | tf_op jit(solution)/shard_map/all_to_all | solution.py:394
  190.8 0.7 copy-done.10
  191.5 1.9 place_tiles.1
  (13 shorter events, 0.0 us)
Async XLA Ops:
  2.3 38.0 %copy-start = (s32[256,128]{1,0:T(8,128)S(1)}, s32[256,128]{1,0:T(8,128)}, u32[]{:S(2)}) copy-start(s32[256,128]{1,0:T(8,128)} %get-tuple-element.18.refs_2_) | copy-start | bytes 393220
  2.4 38.0 %copy-start.1 = (f32[256,128]{1,0:T(8,128)S(1)}, f32[256,128]{1,0:T(8,128)}, u32[]{:S(2)}) copy-start(f32[256,128]{1,0:T(8,128)} %get-tuple-element.19.refs_3_) | copy-start | bytes 393220
  2.4 38.0 %copy-start.9 = (s32[32,128]{1,0:T(8,128)S(1)}, s32[32,128]{1,0:T(8,128)}, u32[]{:S(2)}) copy-start(s32[32,128]{1,0:T(8,128)} %get-tuple-element.23) | copy-start | bytes 49156
  40.4 7.0 %copy-start.8 = (s32[32,128]{1,0:T(8,128)S(1)}, s32[32,128]{1,0:T(8,128)}, u32[]{:S(2)}) copy-start(s32[32,128]{1,0:T(8,128)} %get-tuple-element.22) | copy-start | bytes 49156
  46.0 6.1 %collective-permute-start = (f32[32,64,128]{2,1,0:T(8,128)}, f32[32,64,128]{2,1,0:T(8,128)}, u32[]{:S(2)}, u32[]{:S(2)}) collective-permute-start(f32[32,64,128]{2,1,0:T(8,128)} %gather_rows.8.refs_4_), channel_id=1, source_target_pairs={{0,16},{16,0},{32,48},{48,32},{64,80},{80,64},{96,112},{112,96},{1... | collective-permute-start | bytes 3145736 | tf_op jit(solution)/shard_map/ppermute | solution.py:350
  47.4 9.8 %copy-start.7 = (s32[32,128]{1,0:T(8,128)S(1)}, s32[32,128]{1,0:T(8,128)}, u32[]{:S(2)}) copy-start(s32[32,128]{1,0:T(8,128)} %get-tuple-element.26) | copy-start | bytes 49156
  54.4 26.3 %collective-permute-start.1 = (f32[16,64,128]{2,1,0:T(8,128)}, f32[16,64,128]{2,1,0:T(8,128)}, u32[]{:S(2)}, u32[]{:S(2)}) collective-permute-start(f32[16,64,128]{2,1,0:T(8,128)} %get-tuple-element.36.refs_5_), channel_id=1, source_target_pairs={{0,96},{16,112},{32,0},{48,16},{64,32},{80,48},{96,64},{112,80},{1... | collective-permute-start | bytes 1572872 | tf_op jit(solution)/shard_map/ppermute | solution.py:353
  57.2 14.8 %collective-permute-start.2 = (f32[16,64,128]{2,1,0:T(8,128)}, f32[16,64,128]{2,1,0:T(8,128)}, u32[]{:S(2)}, u32[]{:S(2)}) collective-permute-start(f32[16,64,128]{2,1,0:T(8,128)} %get-tuple-element.37.refs_4_), channel_id=1, source_target_pairs={{0,32},{16,48},{32,64},{48,80},{64,96},{80,112},{96,0},{112,16},{1... | collective-permute-start | bytes 1572872 | tf_op jit(solution)/shard_map/ppermute | solution.py:353
  57.2 5.9 %copy-start.6 = (s32[32,128]{1,0:T(8,128)S(1)}, s32[32,128]{1,0:T(8,128)}, u32[]{:S(2)}) copy-start(s32[32,128]{1,0:T(8,128)} %get-tuple-element.25) | copy-start | bytes 49156
  62.8 14.1 %collective-permute-start.3 = (f32[32,64,128]{2,1,0:T(8,128)}, f32[32,64,128]{2,1,0:T(8,128)}, u32[]{:S(2)}, u32[]{:S(2)}) collective-permute-start(f32[32,64,128]{2,1,0:T(8,128)} %gather_rows.10.refs_4_), channel_id=1, source_target_pairs={{0,16},{16,0},{32,48},{48,32},{64,80},{80,64},{96,112},{112,96},{1... | collective-permute-start | bytes 3145736 | tf_op jit(solution)/shard_map/ppermute | solution.py:355
  63.1 8.9 %copy-start.5 = (s32[32,128]{1,0:T(8,128)S(1)}, s32[32,128]{1,0:T(8,128)}, u32[]{:S(2)}) copy-start(s32[32,128]{1,0:T(8,128)} %get-tuple-element.24) | copy-start | bytes 49156
  68.7 17.0 %collective-permute-start.4 = (f32[32,64,128]{2,1,0:T(8,128)}, f32[32,64,128]{2,1,0:T(8,128)}, u32[]{:S(2)}, u32[]{:S(2)}) collective-permute-start(f32[32,64,128]{2,1,0:T(8,128)} %gather_rows.11.refs_5_), channel_id=1, source_target_pairs={{0,16},{16,0},{32,48},{48,32},{64,80},{80,64},{96,112},{112,96},{1... | collective-permute-start | bytes 3145736 | tf_op jit(solution)/shard_map/ppermute | solution.py:357
  72.0 8.8 %copy-start.4 = (s32[32,128]{1,0:T(8,128)S(1)}, s32[32,128]{1,0:T(8,128)}, u32[]{:S(2)}) copy-start(s32[32,128]{1,0:T(8,128)} %get-tuple-element.21) | copy-start | bytes 49156
  79.3 23.8 %collective-permute-start.7 = (f32[16,64,128]{2,1,0:T(8,128)}, f32[16,64,128]{2,1,0:T(8,128)}, u32[]{:S(2)}, u32[]{:S(2)}) collective-permute-start(f32[16,64,128]{2,1,0:T(8,128)} %get-tuple-element.34.refs_6_), channel_id=1, source_target_pairs={{0,96},{16,112},{32,0},{48,16},{64,32},{80,48},{96,64},{112,80},{1... | collective-permute-start | bytes 1572872 | tf_op jit(solution)/shard_map/ppermute | solution.py:360
  79.3 23.8 %collective-permute-start.6 = (f32[16,64,128]{2,1,0:T(8,128)}, f32[16,64,128]{2,1,0:T(8,128)}, u32[]{:S(2)}, u32[]{:S(2)}) collective-permute-start(f32[16,64,128]{2,1,0:T(8,128)} %get-tuple-element.35.refs_5_), channel_id=1, source_target_pairs={{0,32},{16,48},{32,64},{48,80},{64,96},{80,112},{96,0},{112,16},{1... | collective-permute-start | bytes 1572872 | tf_op jit(solution)/shard_map/ppermute | solution.py:360
  80.7 9.9 %copy-start.3 = (s32[32,128]{1,0:T(8,128)S(1)}, s32[32,128]{1,0:T(8,128)}, u32[]{:S(2)}) copy-start(s32[32,128]{1,0:T(8,128)} %get-tuple-element.20) | copy-start | bytes 49156
  88.0 25.1 %collective-permute-start.8 = (f32[16,64,128]{2,1,0:T(8,128)}, f32[16,64,128]{2,1,0:T(8,128)}, u32[]{:S(2)}, u32[]{:S(2)}) collective-permute-start(f32[16,64,128]{2,1,0:T(8,128)} %get-tuple-element.32.refs_4_), channel_id=1, source_target_pairs={{0,32},{16,48},{32,64},{48,80},{64,96},{80,112},{96,0},{112,16},{1... | collective-permute-start | bytes 1572872 | tf_op jit(solution)/shard_map/ppermute | solution.py:363
  88.0 25.1 %collective-permute-start.9 = (f32[16,64,128]{2,1,0:T(8,128)}, f32[16,64,128]{2,1,0:T(8,128)}, u32[]{:S(2)}, u32[]{:S(2)}) collective-permute-start(f32[16,64,128]{2,1,0:T(8,128)} %get-tuple-element.33.refs_5_), channel_id=1, source_target_pairs={{0,96},{16,112},{32,0},{48,16},{64,32},{80,48},{96,64},{112,80},{1... | collective-permute-start | bytes 1572872 | tf_op jit(solution)/shard_map/ppermute | solution.py:363
  90.6 7.8 %copy-start.2 = (s32[32,128]{1,0:T(8,128)S(1)}, s32[32,128]{1,0:T(8,128)}, u32[]{:S(2)}) copy-start(s32[32,128]{1,0:T(8,128)} %get-tuple-element.17) | copy-start | bytes 49156
  96.2 6.9 %collective-permute-start.5 = (f32[32,64,128]{2,1,0:T(8,128)}, f32[32,64,128]{2,1,0:T(8,128)}, u32[]{:S(2)}, u32[]{:S(2)}) collective-permute-start(f32[32,64,128]{2,1,0:T(8,128)} %gather_rows.14.refs_4_), channel_id=1, source_target_pairs={{0,16},{16,0},{32,48},{48,32},{64,80},{80,64},{96,112},{112,96},{1... | collective-permute-start | bytes 3145736 | tf_op jit(solution)/shard_map/ppermute | solution.py:365
  105.4 18.7 %all-to-all-start = ((f32[16,64,128]{2,1,0:T(8,128)}), f32[16,64,128]{2,1,0:T(8,128)S(1)}, u32[]{:S(2)}, u32[]{:S(2)}) async-start(f32[16,64,128]{2,1,0:T(8,128)} %fusion.1), calls=%async_computation | async-start | bytes 1048576 | tf_op jit(solution)/shard_map/all_to_all | solution.py:371
  124.1 13.8 %all-to-all-start.1 = ((f32[16,64,128]{2,1,0:T(8,128)}), f32[16,64,128]{2,1,0:T(8,128)S(1)}, u32[]{:S(2)}, u32[]{:S(2)}) async-start(f32[16,64,128]{2,1,0:T(8,128)} %add_add_fusion), calls=%async_computation.1 | async-start | bytes 1048576 | tf_op jit(solution)/shard_map/all_to_all | solution.py:371
  127.7 12.5 %collective-permute-start.10 = (f32[16,64,128]{2,1,0:T(8,128)S(1)}, f32[16,64,128]{2,1,0:T(8,128)S(1)}, u32[]{:S(2)}, u32[]{:S(2)}) collective-permute-start(f32[16,64,128]{2,1,0:T(8,128)S(1)} %all-to-all-done.refs_0_), channel_id=1, source_target_pairs={{0,16},{16,0},{32,48},{48,32},{64,80},{80,64},{96,112},{112,96},{1... | collective-permute-start | bytes 1572872 | tf_op jit(solution)/shard_map/ppermute | solution.py:372
  137.9 3.8 %collective-permute-start.11 = (f32[16,64,128]{2,1,0:T(8,128)S(1)}, f32[16,64,128]{2,1,0:T(8,128)S(1)}, u32[]{:S(2)}, u32[]{:S(2)}) collective-permute-start(f32[16,64,128]{2,1,0:T(8,128)S(1)} %all-to-all-done.1.refs_1_), channel_id=1, source_target_pairs={{0,16},{16,0},{32,48},{48,32},{64,80},{80,64},{96,112},{112,96},{1... | collective-permute-start | bytes 1572872 | tf_op jit(solution)/shard_map/ppermute | solution.py:372
  171.0 6.4 %collective-permute-start.12 = (f32[64,64]{1,0:T(8,128)S(1)}, f32[64,64]{1,0:T(8,128)S(1)}, u32[]{:S(2)}, u32[]{:S(2)}) collective-permute-start(f32[64,64]{1,0:T(8,128)S(1)} %get-tuple-element.39), channel_id=1, source_target_pairs={{0,1},{1,2},{2,3},{3,4},{4,5},{5,6},{6,7},{7,8},{8,9},{9,10},{10,1... | collective-permute-start | bytes 49160 | tf_op jit(solution)/shard_map/ppermute | solution.py:392
  178.3 12.5 %all-to-all-start.3 = ((f32[8,72,128]{2,1,0:T(8,128)}), f32[8,72,128]{2,1,0:T(8,128)S(1)}, u32[]{:S(2)}, u32[]{:S(2)}) async-start(f32[8,72,128]{2,1,0:T(8,128)} %broadcast_in_dim.2), calls=%async_computation.3 | async-start | bytes 589824 | tf_op jit(solution)/shard_map/all_to_all | solution.py:394
  190.8 0.7 copy-start.10

commit v5 on v4

--- a/solution.py
+++ b/solution.py
@@ -15,9 +15,10 @@
 TOKS = 128
 K = 32768
 LANES = 128
-ROW_COST = 1_000_000_000
+ROW_COST = 10_000_000
 STEP_EX = 8
 TAP = 256
+EXTRA_ROWS = 8
 
 
 def walsh_table(order):
@@ -41,21 +42,29 @@
     return parts
 
 
-def table_kernel(n_ex, width, acts_ref, cots_ref, ids_ref, signs_ref, walsh_ref, table_ref, grad_ref, flip_ref):
+def table_kernel(n_ex, width, acts_ref, *refs):
+    sources, (table_ref, grad_ref, flip_ref), copies, sems = refs[:4], refs[4:7], refs[7:11], refs[11]
+    cots_ref, ids_ref, signs_ref, walsh_ref = copies
     step = pl.program_id(0)
     tiles = width // LANES
     rows = SLAB
+    stride = SLAB + EXTRA_ROWS
 
     @pl.when(step == 0)
     def _():
+        started = [pltpu.make_async_copy(a, b, sems.at[i]) for i, (a, b) in enumerate(zip(sources, copies))]
+        for copy in started:
+            copy.start()
+        for copy in started:
+            copy.wait()
         factor = 1.0 / math.sqrt(TOKS) / math.sqrt(SLAB * D)
         flip_ref[...] = signs_ref[...].astype(jnp.float32) * factor
 
-    @pl.loop(0, STEP_EX)
+    @pl.loop(0, STEP_EX, unroll=4)
     def _(i):
         e = step * STEP_EX + i
-        live = (ids_ref[pl.ds(i, 1), :] != 0).astype(jnp.bfloat16)
-        g = jnp.dot(cots_ref[i] * live, acts_ref[i], preferred_element_type=jnp.float32)
+        live = (ids_ref[pl.ds(e, 1), :] != 0).astype(jnp.bfloat16)
+        g = jnp.dot(cots_ref[e] * live, acts_ref[i], preferred_element_type=jnp.float32)
         g = g * flip_ref[...]
         for low in range(2):
             tile = [g[:, (2 * q + low) * LANES:(2 * q + low + 1) * LANES] for q in range(tiles // 2)]
@@ -63,21 +72,21 @@
             for q in range(tiles // 2):
                 parts = butterfly([tile[q][8 * s:8 * s + 8] for s in range(rows // 8)])
                 for s in range(rows // 8):
-                    grad_ref[2 * q + low, pl.ds(e * rows + 8 * s, 8), :] = parts[s]
+                    grad_ref[2 * q + low, pl.ds(e * stride + 8 * s, 8), :] = parts[s]
 
     @pl.when(step == pl.num_programs(0) - 1)
     def _():
         lane = lax.broadcasted_iota(jnp.int32, (TAP, LANES), 1)
         low_half = jnp.where(lane < LANES // 2, 1.0, -1.0).astype(jnp.float32)
 
-        @pl.loop(0, (rows // 8) * (tiles // 2))
+        @pl.loop(0, (rows // 8) * (tiles // 2), unroll=4)
         def _(index):
             s = index // (tiles // 2)
             q = index % (tiles // 2)
             high, low = [], []
             for r in range(8):
                 pieces = [
-                    grad_ref.at[2 * q + j][pl.ds(s * 8 + r, n_ex, stride=rows), :] for j in range(2)
+                    grad_ref.at[2 * q + j][pl.ds(s * 8 + r, n_ex, stride=stride), :] for j in range(2)
                 ]
                 x = jnp.concatenate(pieces, axis=1)
                 h = x.astype(jnp.bfloat16)
@@ -134,19 +143,21 @@
         grid=(n_ex // STEP_EX,),
         in_specs=[
             pl.BlockSpec((STEP_EX, toks, width), lambda i: (i, 0, 0)),
-            pl.BlockSpec((STEP_EX, slab, toks), lambda i: (i, 0, 0)),
-            pl.BlockSpec((STEP_EX, toks), lambda i: (i, 0)),
-            whole((slab, width)),
-            whole((TAP, TAP)),
-        ],
+        ] + [pl.BlockSpec(memory_space=pltpu.HBM)] * 4,
         out_specs=pl.BlockSpec(memory_space=pltpu.VMEM),
         scratch_shapes=[
-            pltpu.VMEM((width // LANES, n_ex * slab, LANES), jnp.float32),
+            pltpu.VMEM((width // LANES, n_ex * (slab + EXTRA_ROWS), LANES), jnp.float32),
             pltpu.VMEM((slab, width), jnp.float32),
+            pltpu.VMEM((n_ex, slab, toks), cotangents.dtype),
+            pltpu.VMEM(token_ids.shape, token_ids.dtype),
+            pltpu.VMEM(signs.shape, signs.dtype),
+            pltpu.VMEM((TAP, TAP), jnp.bfloat16),
+            pltpu.SemaphoreType.DMA((4,)),
         ],
         compiler_params=pltpu.CompilerParams(
-            dimension_semantics=("arbitrary",), vmem_limit_bytes=46 * 1024 * 1024
+            dimension_semantics=("arbitrary",), vmem_limit_bytes=30 * 1024 * 1024
         ),
+        cost_estimate=pl.CostEstimate(flops=10**13, bytes_accessed=2**25, transcendentals=0),
         name="make_table",
     )(activations, jnp.swapaxes(cotangents, 1, 2), token_ids, signs, jnp.asarray(walsh_table(TAP)))
 
@@ -222,6 +233,7 @@
         ) + (jax.ShapeDtypeStruct((n_block // n_param, LANES), jnp.int32),) * n_param,
         in_specs=[pl.BlockSpec(memory_space=pltpu.SMEM), vmem],
         out_specs=(vmem,) * (2 + n_param),
+        compiler_params=pltpu.CompilerParams(vmem_limit_bytes=4 * 1024 * 1024),
         name="make_index",
     )(me.reshape(1), select.reshape(n_param // 2, 2, n_block // n_param, LANES))
 
@@ -303,7 +315,7 @@
         ),
         in_specs=[vmem],
         out_specs=(vmem, vmem),
-        compiler_params=pltpu.CompilerParams(vmem_limit_bytes=16 * 1024 * 1024),
+        compiler_params=pltpu.CompilerParams(vmem_limit_bytes=4 * 1024 * 1024),
         name="sum_tiles",
     )(received)
 
@@ -328,6 +340,7 @@
         out_shape=jax.ShapeDtypeStruct((n_ex, count * n_ex), jnp.float32),
         in_specs=[pl.BlockSpec(memory_space=pltpu.SMEM), vmem],
         out_specs=vmem,
+        compiler_params=pltpu.CompilerParams(vmem_limit_bytes=4 * 1024 * 1024),
         name="place_tiles",
     )(me.reshape(1), tiles)
 

time: 194 us -> 168 us (0.87)
  Pallas kernels: 87.2 us -> 61.9 us
  other arithmetic: 14 us -> 5.96 us
  local copies, waits for them, and re-layouts: 1.49 us -> 6.44 us
    pallas_call x1, Pallas kernels: 38 us -> 19.6 us  [make_table(): pl.pallas_call(functools.partial(table_kernel, n_ex, width), out_shape=pl...]
    unnamed x22 -> x12, local copies, waits for them, and re-layouts: 0.75 us -> 5.69 us
    pallas_call x8, Pallas kernels: 41.4 us -> 36.9 us  [gather_rows(): pl.pallas_call(kernel, out_shape=jax.ShapeDtypeStruct((n_block, LANES //...]
    add x1, other arithmetic: 2.37 us -> 0.18 us  [body(): first[mid:] + arrived_first[mid:]]
    add x1, other arithmetic: 2.35 us -> 0.18 us  [body(): outward = (far[:mid] + arrived[:mid], far[mid:] + arrived[mid:])]
    add x1, other arithmetic: 2.3 us -> 0.18 us  [body(): second[:mid] + arrived_second[:mid]]
  transfers between devices with their start and end apart: 16 -> 16, of which waited for: 6 -> 6; matrix products, arithmetic and copies ran while one was open for 6% -> 3% of each run, Pallas kernels for 19% -> 19%
where the time goes in v5:
time: 168 us; the launch traced here: 167 us
  Pallas kernels  61.9 us (37%)
  starting transfers between devices  33.5 us (20%)
  waiting for transfers between devices  33.4 us (20%)
  blocking collectives  25 us (15%)
  local copies, waits for them, and re-layouts  6.44 us (4%)
  other arithmetic  5.96 us (4%)
    pallas_call x8, Pallas kernels, gather_rows(): pl.pallas_call(kernel, out_shape=jax.ShapeDtypeStruct((n_block, LANES //...  36.9 us
    all_to_all x1, blocking collectives, body(): lax.all_to_all(partial.reshape(n_y * n_group, rows_out, LANES), everyone,...  25 us
    pallas_call x1, Pallas kernels, make_table(): pl.pallas_call(functools.partial(table_kernel, n_ex, width), out_shape=pl...  19.6 us
    all_to_all x2, waiting for transfers between devices, body(): lax.all_to_all(x, 'ex', split_axis=0, concat_axis=0)  17.6 us
    all_to_all x2, starting transfers between devices, body(): lax.all_to_all(x, 'ex', split_axis=0, concat_axis=0)  11.2 us
    unnamed x12, local copies, waits for them, and re-layouts  5.69 us
    all_to_all x1, starting transfers between devices, body(): lax.all_to_all(jnp.broadcast_to(message[None], (n_param,) + message.shape...  5.67 us
    ppermute x3, starting transfers between devices, body(): lax.ppermute(outward[1], 'param', along(-1))  5.62 us
  transfers between devices with their start and end apart: 16, of which 6 were waited for; matrix products, arithmetic and copies ran while one was open for 3% of the time, Pallas kernels for 19%

profile of v5, /device:TPU:1, one launch (start us, length us, event | category | flops | bytes accessed | tf_op | source)
XLA Modules:
  0.0 167.1 jit_solution(2829328405823154471)
XLA Ops:
  0.6 0.0 copy-start
  0.6 0.9 copy-done
  1.5 0.1 make_index.1
  1.6 0.0 copy-start.1
  1.6 1.2 copy-done.1
  2.9 0.0 copy-start.2
  2.9 0.9 copy-done.2
  3.8 0.8 copy-done.3
  4.6 0.9 copy-done.4
  5.5 19.6 %make_table.1.refs_1_ = f32[32768,128]{1,0:T(8,128)S(1)} custom-call(bf16[64,128,1024]{2,1,0:T(8,128)(2,1)} %acts_ref.1, bf16[64,64,128]{2,1,0:T(8,128)(2,1)S(1)} %bitcast.26, s32[64,128]{1,0:T(8,128)S(1)} %copy-done.3, s32[64,1024]{1,0:T(8,128)S(1)} %copy-done.2, bf16[256,256]{1,0:T(8,128)(2,1)S(1)} %copy-done.4), custom_call_target="tpu_custom_call" | custom-call | flops 9999999827968 | bytes 33554432 | tf_op jit(solution)/shard_map/make_table/pallas_call | solution.py:140
  25.1 4.6 %gather_rows.8.refs_4_ = f32[32,64,128]{2,1,0:T(8,128)S(1)} custom-call(s32[4096]{0:T(1024)S(1)} %bitcast.34, f32[32768,128]{1,0:T(8,128)S(1)} %make_table.1.refs_1_, s32[256,128]{1,0:T(8,128)S(1)} %get-tuple-element.18.refs_2_, f32[256,128]{1,0:T(8,128)S(1)} %get-tuple-element.19.refs_3_), custom_call_target="tpu_custom_call" | custom-call | flops 40960000000 | bytes 16777216 | tf_op jit(solution)/shard_map/gather_rows/pallas_call | solution.py:184
  29.7 1.5 collective-permute-start
  31.2 4.6 %gather_rows.9 = f32[32,64,128]{2,1,0:T(8,128)S(1)} custom-call(s32[4096]{0:T(1024)S(1)} %bitcast.33, f32[32768,128]{1,0:T(8,128)S(1)} %make_table.1.refs_1_, s32[256,128]{1,0:T(8,128)S(1)} %get-tuple-element.18.refs_2_, f32[256,128]{1,0:T(8,128)S(1)} %get-tuple-element.19.refs_3_, f32[32,64,128]{2,1,0:T(8,128)S(1)} %gather_rows.8.refs_4_), custom_call_target="tpu_custom_call" | custom-call | flops 40960000000 | bytes 16777216 | tf_op jit(solution)/shard_map/gather_rows/pallas_call | solution.py:184
  35.8 0.0 collective-permute-done
  35.8 0.2 slice_add_fusion.6
  36.0 2.9 %collective-permute-start.1 = (f32[16,64,128]{2,1,0:T(8,128)S(1)}, f32[16,64,128]{2,1,0:T(8,128)S(1)}, u32[]{:S(2)}, u32[]{:S(2)}) collective-permute-start(f32[16,64,128]{2,1,0:T(8,128)S(1)} %get-tuple-element.36.refs_5_), channel_id=1, source_target_pairs={{0,96},{16,112},{32,0},{48,16},{64,32},{80,48},{96,64},{112,80},{1... | collective-permute-start | bytes 1572872 | tf_op jit(solution)/shard_map/ppermute | solution.py:366
  38.9 0.0 collective-permute-start.2
  38.9 4.6 %gather_rows.10.refs_4_ = f32[32,64,128]{2,1,0:T(8,128)S(1)} custom-call(s32[4096]{0:T(1024)S(1)} %bitcast.32, f32[32768,128]{1,0:T(8,128)S(1)} %make_table.1.refs_1_, s32[256,128]{1,0:T(8,128)S(1)} %get-tuple-element.18.refs_2_, f32[256,128]{1,0:T(8,128)S(1)} %get-tuple-element.19.refs_3_, f32[16,64,128]{2,1,0:T(8,128)S(1)} %get-tuple-element.37.refs_4_, ...), custom_call_target="tpu_custom_call" | custom-call | flops 40960000000 | bytes 16777216 | tf_op jit(solution)/shard_map/gather_rows/pallas_call | solution.py:184
  43.5 0.4 collective-permute-start.3
  43.9 4.6 %gather_rows.11.refs_5_ = f32[32,64,128]{2,1,0:T(8,128)S(1)} custom-call(s32[4096]{0:T(1024)S(1)} %bitcast.31, f32[32768,128]{1,0:T(8,128)S(1)} %make_table.1.refs_1_, s32[256,128]{1,0:T(8,128)S(1)} %get-tuple-element.18.refs_2_, f32[256,128]{1,0:T(8,128)S(1)} %get-tuple-element.19.refs_3_, f32[32,64,128]{2,1,0:T(8,128)S(1)} %gather_rows.10.refs_4_), custom_call_target="tpu_custom_call" | custom-call | flops 40960000000 | bytes 16777216 | tf_op jit(solution)/shard_map/gather_rows/pallas_call | solution.py:184
  48.5 0.3 collective-permute-start.4
  48.8 4.5 %collective-permute-done.2.refs_4_ = f32[16,64,128]{2,1,0:T(8,128)S(1)} collective-permute-done((f32[16,64,128]{2,1,0:T(8,128)S(1)}, f32[16,64,128]{2,1,0:T(8,128)S(1)}, u32[]{:S(2)}, u32[]{:S(2)}) %collective-permute-start.2) | collective-permute-done | bytes 524320 | tf_op jit(solution)/shard_map/ppermute | solution.py:366
  53.3 4.6 %gather_rows.12 = f32[32,64,128]{2,1,0:T(8,128)S(1)} custom-call(s32[4096]{0:T(1024)S(1)} %bitcast.30, f32[32768,128]{1,0:T(8,128)S(1)} %make_table.1.refs_1_, s32[256,128]{1,0:T(8,128)S(1)} %get-tuple-element.18.refs_2_, f32[256,128]{1,0:T(8,128)S(1)} %get-tuple-element.19.refs_3_, f32[16,64,128]{2,1,0:T(8,128)S(1)} %collective-permute-done.2.refs_4_, ...), custom_call_target="tpu_custom_call" | custom-call | flops 40960000000 | bytes 16777216 | tf_op jit(solution)/shard_map/gather_rows/pallas_call | solution.py:184
  58.0 0.0 collective-permute-done.3
  58.0 0.2 slice_add_fusion.3
  58.2 0.1 collective-permute-start.7
  58.3 1.5 collective-permute-start.6
  59.7 0.0 collective-permute-done.1.refs_4_
  59.7 4.6 %gather_rows.13 = f32[32,64,128]{2,1,0:T(8,128)S(1)} custom-call(s32[4096]{0:T(1024)S(1)} %bitcast.29, f32[32768,128]{1,0:T(8,128)S(1)} %make_table.1.refs_1_, s32[256,128]{1,0:T(8,128)S(1)} %get-tuple-element.18.refs_2_, f32[256,128]{1,0:T(8,128)S(1)} %get-tuple-element.19.refs_3_, f32[16,64,128]{2,1,0:T(8,128)S(1)} %collective-permute-done.1.refs_4_, ...), custom_call_target="tpu_custom_call" | custom-call | flops 40960000000 | bytes 16777216 | tf_op jit(solution)/shard_map/gather_rows/pallas_call | solution.py:184
  64.4 0.0 collective-permute-done.4
  64.4 0.2 slice_add_fusion.2
  64.6 0.1 collective-permute-start.8
  64.7 2.7 %collective-permute-start.9 = (f32[16,64,128]{2,1,0:T(8,128)S(1)}, f32[16,64,128]{2,1,0:T(8,128)}, u32[]{:S(2)}, u32[]{:S(2)}) collective-permute-start(f32[16,64,128]{2,1,0:T(8,128)S(1)} %get-tuple-element.33.refs_5_), channel_id=1, source_target_pairs={{0,96},{16,112},{32,0},{48,16},{64,32},{80,48},{96,64},{112,80},{1... | collective-permute-start | bytes 1572872 | tf_op jit(solution)/shard_map/ppermute | solution.py:376
  67.3 4.6 %gather_rows.14.refs_4_ = f32[32,64,128]{2,1,0:T(8,128)S(1)} custom-call(s32[4096]{0:T(1024)S(1)} %bitcast.28, f32[32768,128]{1,0:T(8,128)S(1)} %make_table.1.refs_1_, s32[256,128]{1,0:T(8,128)S(1)} %get-tuple-element.18.refs_2_, f32[256,128]{1,0:T(8,128)S(1)} %get-tuple-element.19.refs_3_, f32[16,64,128]{2,1,0:T(8,128)S(1)} %get-tuple-element.32.refs_4_, ...), custom_call_target="tpu_custom_call" | custom-call | flops 40960000000 | bytes 16777216 | tf_op jit(solution)/shard_map/gather_rows/pallas_call | solution.py:184
  71.9 2.3 %collective-permute-start.5 = (f32[32,64,128]{2,1,0:T(8,128)S(1)}, f32[32,64,128]{2,1,0:T(8,128)S(1)}, u32[]{:S(2)}, u32[]{:S(2)}) collective-permute-start(f32[32,64,128]{2,1,0:T(8,128)S(1)} %gather_rows.14.refs_4_), channel_id=1, source_target_pairs={{0,16},{16,0},{32,48},{48,32},{64,80},{80,64},{96,112},{112,96},{1... | collective-permute-start | bytes 3145736 | tf_op jit(solution)/shard_map/ppermute | solution.py:378
  74.2 4.6 %gather_rows.15 = f32[32,64,128]{2,1,0:T(8,128)S(1)} custom-call(s32[4096]{0:T(1024)S(1)} %bitcast.27, f32[32768,128]{1,0:T(8,128)S(1)} %make_table.1.refs_1_, s32[256,128]{1,0:T(8,128)S(1)} %get-tuple-element.18.refs_2_, f32[256,128]{1,0:T(8,128)S(1)} %get-tuple-element.19.refs_3_, f32[32,64,128]{2,1,0:T(8,128)S(1)} %gather_rows.14.refs_4_), custom_call_target="tpu_custom_call" | custom-call | flops 40960000000 | bytes 16777216 | tf_op jit(solution)/shard_map/gather_rows/pallas_call | solution.py:184
  78.9 0.0 collective-permute-done.7
  78.9 0.0 collective-permute-done.6
  78.9 0.0 collective-permute-done.5
  78.9 0.0 copy-start.5
  78.9 1.0 copy-done.5
  79.9 0.9 fusion.1
  80.8 7.6 %all-to-all-start = ((f32[16,64,128]{2,1,0:T(8,128)}), f32[16,64,128]{2,1,0:T(8,128)S(1)}, u32[]{:S(2)}, u32[]{:S(2)}) async-start(f32[16,64,128]{2,1,0:T(8,128)} %fusion.1), calls=%async_computation | async-start | bytes 1048576 | tf_op jit(solution)/shard_map/all_to_all | solution.py:384
  88.4 0.0 collective-permute-done.8
  88.4 0.0 collective-permute-done.9
  88.5 2.2 %add_add_fusion = f32[16,64,128]{2,1,0:T(8,128)} fusion(f32[16,64,128]{2,1,0:T(8,128)} %collective-permute-done.9, f32[16,64,128]{2,1,0:T(8,128)S(1)} %collective-permute-done.8, f32[32,64,128]{2,1,0:T(8,128)} %copy-done.5, f32[32,64,128]{2,1,0:T(8,128)S(1)} %gather_rows.15), kind=kLoop, calls=%fused_computation.11 | loop fusion | flops 393216 | bytes 2621440 | tf_op jit(solution)/shard_map/add | solution.py:382
  90.6 8.9 %all-to-all-done.refs_0_ = f32[16,64,128]{2,1,0:T(8,128)S(1)} async-done(((f32[16,64,128]{2,1,0:T(8,128)}), f32[16,64,128]{2,1,0:T(8,128)S(1)}, u32[]{:S(2)}, u32[]{:S(2)}) %all-to-all-start) | async-done | bytes 524320 | tf_op jit(solution)/shard_map/all_to_all | solution.py:384
  99.5 3.6 %all-to-all-start.1 = ((f32[16,64,128]{2,1,0:T(8,128)}), f32[16,64,128]{2,1,0:T(8,128)S(1)}, u32[]{:S(2)}, u32[]{:S(2)}) async-start(f32[16,64,128]{2,1,0:T(8,128)} %add_add_fusion), calls=%async_computation.1 | async-start | bytes 1048576 | tf_op jit(solution)/shard_map/all_to_all | solution.py:384
  103.1 1.5 collective-permute-start.10
  104.6 8.7 %all-to-all-done.1.refs_1_ = f32[16,64,128]{2,1,0:T(8,128)S(1)} async-done(((f32[16,64,128]{2,1,0:T(8,128)}), f32[16,64,128]{2,1,0:T(8,128)S(1)}, u32[]{:S(2)}, u32[]{:S(2)}) %all-to-all-start.1) | async-done | bytes 524320 | tf_op jit(solution)/shard_map/all_to_all | solution.py:384
  113.2 2.3 %collective-permute-start.11 = (f32[16,64,128]{2,1,0:T(8,128)S(1)}, f32[16,64,128]{2,1,0:T(8,128)S(1)}, u32[]{:S(2)}, u32[]{:S(2)}) collective-permute-start(f32[16,64,128]{2,1,0:T(8,128)S(1)} %all-to-all-done.1.refs_1_), channel_id=1, source_target_pairs={{0,16},{16,0},{32,48},{48,32},{64,80},{80,64},{96,112},{112,96},{1... | collective-permute-start | bytes 1572872 | tf_op jit(solution)/shard_map/ppermute | solution.py:385
  115.5 0.0 collective-permute-done.10.refs_2_
  115.5 1.5 collective-permute-done.11.refs_3_
  117.1 4.1 %partial_gram.1 = f32[4,16,40,128]{3,2,1,0:T(8,128)S(1)} custom-call(s32[1]{0:T(128)} %bitcast.13.core_ref, f32[16,64,128]{2,1,0:T(8,128)S(1)} %all-to-all-done.refs_0_, f32[16,64,128]{2,1,0:T(8,128)S(1)} %all-to-all-done.1.refs_1_, f32[16,64,128]{2,1,0:T(8,128)S(1)} %collective-permute-done.10.refs_2_, f32[16,64,128]{2,1,0:T(8,128)S(1)} %collective-permute-done.11.refs_3_), custom_call_target="tpu_custom_call" | custom-call | tf_op jit(solution)/shard_map/partial_gram/pallas_call | solution.py:286
  121.1 25.0 %all_to_all.20.x_ref = f32[64,40,128]{2,1,0:T(8,128)S(1)} all-to-all(f32[64,40,128]{2,1,0:T(8,128)S(1)} %bitcast.24), channel_id=1, replica_groups={{0,1,2,3,4,5,6,7,8,9,10,11,12,13,14,15,32,33,34,35,36,37,38,39,40,41,42..., dimensions={0} | all-to-all | bytes 2621440 | tf_op jit(solution)/shard_map/all_to_all | solution.py:394
  146.2 0.2 sum_tiles.1
  146.4 1.3 collective-permute-start.12
  147.7 5.2 %collective-permute-done.12 = f32[64,64]{1,0:T(8,128)S(1)} collective-permute-done((f32[64,64]{1,0:T(8,128)S(1)}, f32[64,64]{1,0:T(8,128)S(1)}, u32[]{:S(2)}, u32[]{:S(2)}) %collective-permute-start.12) | collective-permute-done | bytes 16416 | tf_op jit(solution)/shard_map/ppermute | solution.py:405
  152.9 0.1 pad_maximum_fusion
  153.0 0.7 broadcast_in_dim.2
  153.7 5.7 %all-to-all-start.3 = ((f32[8,72,128]{2,1,0:T(8,128)}), f32[8,72,128]{2,1,0:T(8,128)S(1)}, u32[]{:S(2)}, u32[]{:S(2)}) async-start(f32[8,72,128]{2,1,0:T(8,128)} %broadcast_in_dim.2), calls=%async_computation.3 | async-start | bytes 589824 | tf_op jit(solution)/shard_map/all_to_all | solution.py:407
  159.4 2.2 %copy_bitcast_fusion = f32[64,4096]{1,0:T(8,128)} fusion(f32[16,64,128]{2,1,0:T(8,128)} %add_add_fusion, f32[16,64,128]{2,1,0:T(8,128)} %fusion.1), kind=kLoop, calls=%fused_computation | loop fusion | flops 262144 | bytes 2097152 | tf_op jit(solution)/shard_map/reshape | solution.py:386
  161.6 4.6 %all-to-all-done.3.x_ref = f32[8,72,128]{2,1,0:T(8,128)S(1)} async-done(((f32[8,72,128]{2,1,0:T(8,128)}), f32[8,72,128]{2,1,0:T(8,128)S(1)}, u32[]{:S(2)}, u32[]{:S(2)}) %all-to-all-start.3) | async-done | bytes 294944 | tf_op jit(solution)/shard_map/all_to_all | solution.py:407
  166.2 0.9 place_tiles.1
  (3 shorter events, 0.0 us)
Async XLA Ops:
  0.6 0.9 copy-start
  1.6 1.2 copy-start.1
  2.9 0.9 copy-start.2
  3.8 0.8 copy-start.3
  4.6 0.9 copy-start.4
  29.7 6.1 %collective-permute-start = (f32[32,64,128]{2,1,0:T(8,128)S(1)}, f32[32,64,128]{2,1,0:T(8,128)S(1)}, u32[]{:S(2)}, u32[]{:S(2)}) collective-permute-start(f32[32,64,128]{2,1,0:T(8,128)S(1)} %gather_rows.8.refs_4_), channel_id=1, source_target_pairs={{0,16},{16,0},{32,48},{48,32},{64,80},{80,64},{96,112},{112,96},{1... | collective-permute-start | bytes 3145736 | tf_op jit(solution)/shard_map/ppermute | solution.py:363
  36.0 23.7 %collective-permute-start.1 = (f32[16,64,128]{2,1,0:T(8,128)S(1)}, f32[16,64,128]{2,1,0:T(8,128)S(1)}, u32[]{:S(2)}, u32[]{:S(2)}) collective-permute-start(f32[16,64,128]{2,1,0:T(8,128)S(1)} %get-tuple-element.36.refs_5_), channel_id=1, source_target_pairs={{0,96},{16,112},{32,0},{48,16},{64,32},{80,48},{96,64},{112,80},{1... | collective-permute-start | bytes 1572872 | tf_op jit(solution)/shard_map/ppermute | solution.py:366
  38.9 14.4 %collective-permute-start.2 = (f32[16,64,128]{2,1,0:T(8,128)S(1)}, f32[16,64,128]{2,1,0:T(8,128)S(1)}, u32[]{:S(2)}, u32[]{:S(2)}) collective-permute-start(f32[16,64,128]{2,1,0:T(8,128)S(1)} %get-tuple-element.37.refs_4_), channel_id=1, source_target_pairs={{0,32},{16,48},{32,64},{48,80},{64,96},{80,112},{96,0},{112,16},{1... | collective-permute-start | bytes 1572872 | tf_op jit(solution)/shard_map/ppermute | solution.py:366
  43.5 14.5 %collective-permute-start.3 = (f32[32,64,128]{2,1,0:T(8,128)S(1)}, f32[32,64,128]{2,1,0:T(8,128)S(1)}, u32[]{:S(2)}, u32[]{:S(2)}) collective-permute-start(f32[32,64,128]{2,1,0:T(8,128)S(1)} %gather_rows.10.refs_4_), channel_id=1, source_target_pairs={{0,16},{16,0},{32,48},{48,32},{64,80},{80,64},{96,112},{112,96},{1... | collective-permute-start | bytes 3145736 | tf_op jit(solution)/shard_map/ppermute | solution.py:368
  48.5 15.9 %collective-permute-start.4 = (f32[32,64,128]{2,1,0:T(8,128)S(1)}, f32[32,64,128]{2,1,0:T(8,128)S(1)}, u32[]{:S(2)}, u32[]{:S(2)}) collective-permute-start(f32[32,64,128]{2,1,0:T(8,128)S(1)} %gather_rows.11.refs_5_), channel_id=1, source_target_pairs={{0,16},{16,0},{32,48},{48,32},{64,80},{80,64},{96,112},{112,96},{1... | collective-permute-start | bytes 3145736 | tf_op jit(solution)/shard_map/ppermute | solution.py:370
  58.2 20.7 %collective-permute-start.7 = (f32[16,64,128]{2,1,0:T(8,128)S(1)}, f32[16,64,128]{2,1,0:T(8,128)S(1)}, u32[]{:S(2)}, u32[]{:S(2)}) collective-permute-start(f32[16,64,128]{2,1,0:T(8,128)S(1)} %get-tuple-element.34.refs_6_), channel_id=1, source_target_pairs={{0,96},{16,112},{32,0},{48,16},{64,32},{80,48},{96,64},{112,80},{1... | collective-permute-start | bytes 1572872 | tf_op jit(solution)/shard_map/ppermute | solution.py:373
  58.3 20.6 %collective-permute-start.6 = (f32[16,64,128]{2,1,0:T(8,128)S(1)}, f32[16,64,128]{2,1,0:T(8,128)S(1)}, u32[]{:S(2)}, u32[]{:S(2)}) collective-permute-start(f32[16,64,128]{2,1,0:T(8,128)S(1)} %get-tuple-element.35.refs_5_), channel_id=1, source_target_pairs={{0,32},{16,48},{32,64},{48,80},{64,96},{80,112},{96,0},{112,16},{1... | collective-permute-start | bytes 1572872 | tf_op jit(solution)/shard_map/ppermute | solution.py:373
  64.6 23.9 %collective-permute-start.8 = (f32[16,64,128]{2,1,0:T(8,128)S(1)}, f32[16,64,128]{2,1,0:T(8,128)S(1)}, u32[]{:S(2)}, u32[]{:S(2)}) collective-permute-start(f32[16,64,128]{2,1,0:T(8,128)S(1)} %get-tuple-element.32.refs_4_), channel_id=1, source_target_pairs={{0,32},{16,48},{32,64},{48,80},{64,96},{80,112},{96,0},{112,16},{1... | collective-permute-start | bytes 1572872 | tf_op jit(solution)/shard_map/ppermute | solution.py:376
  64.7 23.8 %collective-permute-start.9 = (f32[16,64,128]{2,1,0:T(8,128)S(1)}, f32[16,64,128]{2,1,0:T(8,128)}, u32[]{:S(2)}, u32[]{:S(2)}) collective-permute-start(f32[16,64,128]{2,1,0:T(8,128)S(1)} %get-tuple-element.33.refs_5_), channel_id=1, source_target_pairs={{0,96},{16,112},{32,0},{48,16},{64,32},{80,48},{96,64},{112,80},{1... | collective-permute-start | bytes 1572872 | tf_op jit(solution)/shard_map/ppermute | solution.py:376
  71.9 7.0 %collective-permute-start.5 = (f32[32,64,128]{2,1,0:T(8,128)S(1)}, f32[32,64,128]{2,1,0:T(8,128)S(1)}, u32[]{:S(2)}, u32[]{:S(2)}) collective-permute-start(f32[32,64,128]{2,1,0:T(8,128)S(1)} %gather_rows.14.refs_4_), channel_id=1, source_target_pairs={{0,16},{16,0},{32,48},{48,32},{64,80},{80,64},{96,112},{112,96},{1... | collective-permute-start | bytes 3145736 | tf_op jit(solution)/shard_map/ppermute | solution.py:378
  78.9 1.0 copy-start.5
  80.8 18.7 %all-to-all-start = ((f32[16,64,128]{2,1,0:T(8,128)}), f32[16,64,128]{2,1,0:T(8,128)S(1)}, u32[]{:S(2)}, u32[]{:S(2)}) async-start(f32[16,64,128]{2,1,0:T(8,128)} %fusion.1), calls=%async_computation | async-start | bytes 1048576 | tf_op jit(solution)/shard_map/all_to_all | solution.py:384
  99.5 13.7 %all-to-all-start.1 = ((f32[16,64,128]{2,1,0:T(8,128)}), f32[16,64,128]{2,1,0:T(8,128)S(1)}, u32[]{:S(2)}, u32[]{:S(2)}) async-start(f32[16,64,128]{2,1,0:T(8,128)} %add_add_fusion), calls=%async_computation.1 | async-start | bytes 1048576 | tf_op jit(solution)/shard_map/all_to_all | solution.py:384
  103.1 12.5 %collective-permute-start.10 = (f32[16,64,128]{2,1,0:T(8,128)S(1)}, f32[16,64,128]{2,1,0:T(8,128)S(1)}, u32[]{:S(2)}, u32[]{:S(2)}) collective-permute-start(f32[16,64,128]{2,1,0:T(8,128)S(1)} %all-to-all-done.refs_0_), channel_id=1, source_target_pairs={{0,16},{16,0},{32,48},{48,32},{64,80},{80,64},{96,112},{112,96},{1... | collective-permute-start | bytes 1572872 | tf_op jit(solution)/shard_map/ppermute | solution.py:385
  113.2 3.8 %collective-permute-start.11 = (f32[16,64,128]{2,1,0:T(8,128)S(1)}, f32[16,64,128]{2,1,0:T(8,128)S(1)}, u32[]{:S(2)}, u32[]{:S(2)}) collective-permute-start(f32[16,64,128]{2,1,0:T(8,128)S(1)} %all-to-all-done.1.refs_1_), channel_id=1, source_target_pairs={{0,16},{16,0},{32,48},{48,32},{64,80},{80,64},{96,112},{112,96},{1... | collective-permute-start | bytes 1572872 | tf_op jit(solution)/shard_map/ppermute | solution.py:385
  146.4 6.4 %collective-permute-start.12 = (f32[64,64]{1,0:T(8,128)S(1)}, f32[64,64]{1,0:T(8,128)S(1)}, u32[]{:S(2)}, u32[]{:S(2)}) collective-permute-start(f32[64,64]{1,0:T(8,128)S(1)} %get-tuple-element.39), channel_id=1, source_target_pairs={{0,1},{1,2},{2,3},{3,4},{4,5},{5,6},{6,7},{7,8},{8,9},{9,10},{10,1... | collective-permute-start | bytes 49160 | tf_op jit(solution)/shard_map/ppermute | solution.py:405
  153.7 12.5 %all-to-all-start.3 = ((f32[8,72,128]{2,1,0:T(8,128)}), f32[8,72,128]{2,1,0:T(8,128)S(1)}, u32[]{:S(2)}, u32[]{:S(2)}) async-start(f32[8,72,128]{2,1,0:T(8,128)} %broadcast_in_dim.2), calls=%async_computation.3 | async-start | bytes 589824 | tf_op jit(solution)/shard_map/all_to_all | solution.py:407

commit v6 on v5

--- a/solution.py
+++ b/solution.py
@@ -137,6 +137,10 @@
 def make_table(activations, cotangents, token_ids, signs):
     n_ex, toks, width = activations.shape
     slab = cotangents.shape[2]
+    small = [
+        pltpu.with_memory_space_constraint(x, pltpu.HBM)
+        for x in (jnp.swapaxes(cotangents, 1, 2), token_ids, signs, jnp.asarray(walsh_table(TAP)))
+    ]
     return pl.pallas_call(
         functools.partial(table_kernel, n_ex, width),
         out_shape=pltpu.VMEM((slab // 2 * width, LANES), jnp.float32),
@@ -155,11 +159,11 @@
             pltpu.SemaphoreType.DMA((4,)),
         ],
         compiler_params=pltpu.CompilerParams(
-            dimension_semantics=("arbitrary",), vmem_limit_bytes=30 * 1024 * 1024
+            dimension_semantics=("arbitrary",), vmem_limit_bytes=26 * 1024 * 1024
         ),
         cost_estimate=pl.CostEstimate(flops=10**13, bytes_accessed=2**25, transcendentals=0),
         name="make_table",
-    )(activations, jnp.swapaxes(cotangents, 1, 2), token_ids, signs, jnp.asarray(walsh_table(TAP)))
+    )(activations, *small)
 
 
 def gather_rows(table, index, core, group, after=(), add=()):
@@ -368,15 +372,15 @@
     arrived_first = lax.ppermute(sent_first, "param", swap)
     sent_second = gather_rows(table, index, 0, SECOND, after=(sent_first,))
     arrived_second = lax.ppermute(sent_second, "param", swap)
-    first = gather_rows(table, index, 1, FIRST, after=(sent_second,), add=((0, mid, up),))
+    sent = gather_rows(table, index, 0, OWN, after=(sent_second,))
+    arrived = lax.ppermute(sent, "param", swap)
+    first = gather_rows(table, index, 1, FIRST, after=(sent,), add=((0, mid, up),))
     outward = (first[:mid] + arrived_first[:mid], first[mid:] + arrived_first[mid:])
     first = lax.ppermute(outward[0], "param", along(1)), lax.ppermute(outward[1], "param", along(-1))
     second = gather_rows(table, index, 1, SECOND, after=outward, add=((mid, n_block, down),))
     outward = (second[:mid] + arrived_second[:mid], second[mid:] + arrived_second[mid:])
     second = lax.ppermute(outward[0], "param", along(1)), lax.ppermute(outward[1], "param", along(-1))
-    sent = gather_rows(table, index, 0, OWN, after=outward)
-    arrived = lax.ppermute(sent, "param", swap)
-    own = gather_rows(table, index, 1, OWN, after=(sent,))
+    own = gather_rows(table, index, 1, OWN, after=outward)
     front = own[:mid] + arrived[:mid] + first[0] + first[1]
     own, arrived, front = lax.optimization_barrier((own, arrived, front))
     back = own[mid:] + arrived[mid:] + second[0] + second[1]

time: 168 us -> 162 us (0.964)
  waiting for transfers between devices: 33.4 us -> 26.2 us
  local copies, waits for them, and re-layouts: 6.44 us -> 1.66 us
  starting transfers between devices: 33.5 us -> 37.2 us
    all_to_all x2, waiting for transfers between devices: 17.6 us -> 10.5 us  [body(): lax.all_to_all(x, 'ex', split_axis=0, concat_axis=0)]
    unnamed x12 -> x4, local copies, waits for them, and re-layouts: 5.69 us -> 0.9 us
    ppermute x2, starting transfers between devices: 3.79 us -> 7.25 us  [body(): shares += [lax.ppermute(x, 'param', swap) for x in shares]]
    ppermute x3, starting transfers between devices: 5.62 us -> 8.57 us  [body(): lax.ppermute(outward[1], 'param', along(-1))]
    ppermute x2, starting transfers between devices: 3.81 us -> 1.9 us  [body(): arrived = lax.ppermute(sent, 'param', swap)]
  transfers between devices with their start and end apart: 16 -> 16, of which waited for: 6 -> 7; matrix products, arithmetic and copies ran while one was open for 3% -> 4% of each run, Pallas kernels for 19% -> 20%
where the time goes in v6:
time: 162 us
  Pallas kernels  63.3 us (39%)
  starting transfers between devices  37.2 us (23%)
  waiting for transfers between devices  26.2 us (16%)
  blocking collectives  25.8 us (16%)
  other arithmetic  6.71 us (4%)
  local copies, waits for them, and re-layouts  1.66 us (1%)
    pallas_call x8, Pallas kernels, gather_rows(): pl.pallas_call(kernel, out_shape=jax.ShapeDtypeStruct((n_block, LANES //...  37.2 us
    all_to_all x1, blocking collectives, body(): lax.all_to_all(partial.reshape(n_y * n_group, rows_out, LANES), everyone,...  25.8 us
    pallas_call x1, Pallas kernels, make_table(): pl.pallas_call(functools.partial(table_kernel, n_ex, width), out_shape=pl...  20.8 us
    all_to_all x2, starting transfers between devices, body(): lax.all_to_all(x, 'ex', split_axis=0, concat_axis=0)  11.2 us
    all_to_all x2, waiting for transfers between devices, body(): lax.all_to_all(x, 'ex', split_axis=0, concat_axis=0)  10.5 us
    ppermute x3, starting transfers between devices, body(): lax.ppermute(outward[1], 'param', along(-1))  8.57 us
    ppermute x2, starting transfers between devices, body(): shares += [lax.ppermute(x, 'param', swap) for x in shares]  7.25 us
    all_to_all x1, starting transfers between devices, body(): lax.all_to_all(jnp.broadcast_to(message[None], (n_param,) + message.shape...  6.06 us
  transfers between devices with their start and end apart: 16, of which 7 were waited for; matrix products, arithmetic and copies ran while one was open for 4% of the time, Pallas kernels for 20%

profile of v6, /device:TPU:1, one launch (start us, length us, event | category | flops | bytes accessed | tf_op | source)
XLA Modules:
  0.0 161.7 jit_solution(3123505023899059973)
XLA Ops:
  0.6 0.0 copy-start
  0.6 0.9 copy-done
  1.5 0.1 make_index.1
  1.6 20.8 %make_table.1.refs_1_ = f32[32768,128]{1,0:T(8,128)S(1)} custom-call(bf16[64,128,1024]{2,1,0:T(8,128)(2,1)} %acts_ref.1, bf16[64,64,128]{2,1,0:T(8,128)(2,1)} %bitcast.34, s32[64,128]{1,0:T(8,128)} %refs_1_.1, s32[64,1024]{1,0:T(8,128)} %refs_2_.1, bf16[256,256]{1,0:T(8,128)(2,1)} %constant.24.clone.refs_3_), custom_call_target="tpu_custom_call" | custom-call | flops 9999999827968 | bytes 33554432 | tf_op jit(solution)/shard_map/make_table/pallas_call | solution.py:144
  22.4 4.6 %gather_rows.8.refs_4_ = f32[32,64,128]{2,1,0:T(8,128)S(1)} custom-call(s32[4096]{0:T(1024)S(1)} %bitcast.33, f32[32768,128]{1,0:T(8,128)S(1)} %make_table.1.refs_1_, s32[256,128]{1,0:T(8,128)S(1)} %get-tuple-element.18.refs_2_, f32[256,128]{1,0:T(8,128)S(1)} %get-tuple-element.19.refs_3_), custom_call_target="tpu_custom_call" | custom-call | flops 40960000000 | bytes 16777216 | tf_op jit(solution)/shard_map/gather_rows/pallas_call | solution.py:188
  27.1 1.5 collective-permute-start
  28.6 4.6 %gather_rows.9 = f32[32,64,128]{2,1,0:T(8,128)S(1)} custom-call(s32[4096]{0:T(1024)S(1)} %bitcast.32, f32[32768,128]{1,0:T(8,128)S(1)} %make_table.1.refs_1_, s32[256,128]{1,0:T(8,128)S(1)} %get-tuple-element.18.refs_2_, f32[256,128]{1,0:T(8,128)S(1)} %get-tuple-element.19.refs_3_, f32[32,64,128]{2,1,0:T(8,128)S(1)} %gather_rows.8.refs_4_), custom_call_target="tpu_custom_call" | custom-call | flops 40960000000 | bytes 16777216 | tf_op jit(solution)/shard_map/gather_rows/pallas_call | solution.py:188
  33.2 0.0 collective-permute-done
  33.2 1.0 slice_add_fusion.6
  34.1 2.8 %collective-permute-start.1 = (f32[16,64,128]{2,1,0:T(8,128)}, f32[16,64,128]{2,1,0:T(8,128)}, u32[]{:S(2)}, u32[]{:S(2)}) collective-permute-start(f32[16,64,128]{2,1,0:T(8,128)} %get-tuple-element.36.refs_5_), channel_id=1, source_target_pairs={{0,96},{16,112},{32,0},{48,16},{64,32},{80,48},{96,64},{112,80},{1... | collective-permute-start | bytes 1572872 | tf_op jit(solution)/shard_map/ppermute | solution.py:370
  37.0 0.0 collective-permute-start.2
  37.0 4.6 %gather_rows.10.refs_4_ = f32[32,64,128]{2,1,0:T(8,128)S(1)} custom-call(s32[4096]{0:T(1024)S(1)} %bitcast.31, f32[32768,128]{1,0:T(8,128)S(1)} %make_table.1.refs_1_, s32[256,128]{1,0:T(8,128)S(1)} %get-tuple-element.18.refs_2_, f32[256,128]{1,0:T(8,128)S(1)} %get-tuple-element.19.refs_3_, f32[16,64,128]{2,1,0:T(8,128)S(1)} %get-tuple-element.37.refs_4_, ...), custom_call_target="tpu_custom_call" | custom-call | flops 40960000000 | bytes 16777216 | tf_op jit(solution)/shard_map/gather_rows/pallas_call | solution.py:188
  41.6 0.4 collective-permute-start.3
  41.9 4.6 %gather_rows.11.refs_4_ = f32[32,64,128]{2,1,0:T(8,128)S(1)} custom-call(s32[4096]{0:T(1024)S(1)} %bitcast.30, f32[32768,128]{1,0:T(8,128)S(1)} %make_table.1.refs_1_, s32[256,128]{1,0:T(8,128)S(1)} %get-tuple-element.18.refs_2_, f32[256,128]{1,0:T(8,128)S(1)} %get-tuple-element.19.refs_3_, f32[32,64,128]{2,1,0:T(8,128)S(1)} %gather_rows.10.refs_4_), custom_call_target="tpu_custom_call" | custom-call | flops 40960000000 | bytes 16777216 | tf_op jit(solution)/shard_map/gather_rows/pallas_call | solution.py:188
  46.6 0.3 collective-permute-start.4
  46.8 4.6 %gather_rows.12.refs_5_ = f32[32,64,128]{2,1,0:T(8,128)S(1)} custom-call(s32[4096]{0:T(1024)S(1)} %bitcast.29, f32[32768,128]{1,0:T(8,128)S(1)} %make_table.1.refs_1_, s32[256,128]{1,0:T(8,128)S(1)} %get-tuple-element.18.refs_2_, f32[256,128]{1,0:T(8,128)S(1)} %get-tuple-element.19.refs_3_, f32[32,64,128]{2,1,0:T(8,128)S(1)} %gather_rows.11.refs_4_), custom_call_target="tpu_custom_call" | custom-call | flops 40960000000 | bytes 16777216 | tf_op jit(solution)/shard_map/gather_rows/pallas_call | solution.py:188
  51.5 0.4 collective-permute-start.5
  51.8 0.0 collective-permute-done.2.refs_4_
  51.9 4.6 %gather_rows.13 = f32[32,64,128]{2,1,0:T(8,128)S(1)} custom-call(s32[4096]{0:T(1024)S(1)} %bitcast.28, f32[32768,128]{1,0:T(8,128)S(1)} %make_table.1.refs_1_, s32[256,128]{1,0:T(8,128)S(1)} %get-tuple-element.18.refs_2_, f32[256,128]{1,0:T(8,128)S(1)} %get-tuple-element.19.refs_3_, f32[16,64,128]{2,1,0:T(8,128)S(1)} %collective-permute-done.2.refs_4_, ...), custom_call_target="tpu_custom_call" | custom-call | flops 40960000000 | bytes 16777216 | tf_op jit(solution)/shard_map/gather_rows/pallas_call | solution.py:188
  56.5 0.0 collective-permute-done.3
  56.5 0.2 slice_add_fusion.3
  56.7 3.0 %collective-permute-start.7 = (f32[16,64,128]{2,1,0:T(8,128)S(1)}, f32[16,64,128]{2,1,0:T(8,128)S(1)}, u32[]{:S(2)}, u32[]{:S(2)}) collective-permute-start(f32[16,64,128]{2,1,0:T(8,128)S(1)} %get-tuple-element.34.refs_6_), channel_id=1, source_target_pairs={{0,96},{16,112},{32,0},{48,16},{64,32},{80,48},{96,64},{112,80},{1... | collective-permute-start | bytes 1572872 | tf_op jit(solution)/shard_map/ppermute | solution.py:379
  59.7 0.0 collective-permute-start.6
  59.7 0.0 collective-permute-done.1.refs_4_
  59.7 4.9 %gather_rows.14 = f32[32,64,128]{2,1,0:T(8,128)S(1)} custom-call(s32[4096]{0:T(1024)S(1)} %bitcast.27, f32[32768,128]{1,0:T(8,128)S(1)} %make_table.1.refs_1_, s32[256,128]{1,0:T(8,128)S(1)} %get-tuple-element.18.refs_2_, f32[256,128]{1,0:T(8,128)S(1)} %get-tuple-element.19.refs_3_, f32[16,64,128]{2,1,0:T(8,128)} %collective-permute-done.1.refs_4_, ...), custom_call_target="tpu_custom_call" | custom-call | flops 40960000000 | bytes 16777216 | tf_op jit(solution)/shard_map/gather_rows/pallas_call | solution.py:188
  64.6 0.0 collective-permute-done.4
  64.6 0.2 slice_add_fusion.2
  64.8 2.7 %collective-permute-start.9 = (f32[16,64,128]{2,1,0:T(8,128)S(1)}, f32[16,64,128]{2,1,0:T(8,128)S(1)}, u32[]{:S(2)}, u32[]{:S(2)}) collective-permute-start(f32[16,64,128]{2,1,0:T(8,128)S(1)} %get-tuple-element.33.refs_5_), channel_id=1, source_target_pairs={{0,96},{16,112},{32,0},{48,16},{64,32},{80,48},{96,64},{112,80},{1... | collective-permute-start | bytes 1572872 | tf_op jit(solution)/shard_map/ppermute | solution.py:382
  67.6 0.0 collective-permute-start.8
  67.6 4.6 %gather_rows.15 = f32[32,64,128]{2,1,0:T(8,128)S(1)} custom-call(s32[4096]{0:T(1024)S(1)} %bitcast.26, f32[32768,128]{1,0:T(8,128)S(1)} %make_table.1.refs_1_, s32[256,128]{1,0:T(8,128)S(1)} %get-tuple-element.18.refs_2_, f32[256,128]{1,0:T(8,128)S(1)} %get-tuple-element.19.refs_3_, f32[16,64,128]{2,1,0:T(8,128)S(1)} %get-tuple-element.32.refs_4_, ...), custom_call_target="tpu_custom_call" | custom-call | flops 40960000000 | bytes 16777216 | tf_op jit(solution)/shard_map/gather_rows/pallas_call | solution.py:188
  72.2 0.0 collective-permute-done.5
  72.2 0.0 copy-start.1
  72.2 0.0 collective-permute-done.7
  72.2 1.9 %collective-permute-done.6 = f32[16,64,128]{2,1,0:T(8,128)S(1)} collective-permute-done((f32[16,64,128]{2,1,0:T(8,128)S(1)}, f32[16,64,128]{2,1,0:T(8,128)S(1)}, u32[]{:S(2)}, u32[]{:S(2)}) %collective-permute-start.6) | collective-permute-done | bytes 524320 | tf_op jit(solution)/shard_map/ppermute | solution.py:379
  74.2 0.0 copy-done.1
  74.2 0.9 fusion.1
  75.1 7.6 %all-to-all-start = ((f32[16,64,128]{2,1,0:T(8,128)}), f32[16,64,128]{2,1,0:T(8,128)S(1)}, u32[]{:S(2)}, u32[]{:S(2)}) async-start(f32[16,64,128]{2,1,0:T(8,128)} %fusion.1), calls=%async_computation | async-start | bytes 1048576 | tf_op jit(solution)/shard_map/all_to_all | solution.py:388
  82.7 0.0 collective-permute-done.9
  82.7 2.8 %collective-permute-done.8 = f32[16,64,128]{2,1,0:T(8,128)} collective-permute-done((f32[16,64,128]{2,1,0:T(8,128)S(1)}, f32[16,64,128]{2,1,0:T(8,128)}, u32[]{:S(2)}, u32[]{:S(2)}) %collective-permute-start.8) | collective-permute-done | bytes 524320 | tf_op jit(solution)/shard_map/ppermute | solution.py:382
  85.5 2.1 %add_add_fusion = f32[16,64,128]{2,1,0:T(8,128)} fusion(f32[16,64,128]{2,1,0:T(8,128)S(1)} %collective-permute-done.9, f32[16,64,128]{2,1,0:T(8,128)} %collective-permute-done.8, f32[32,64,128]{2,1,0:T(8,128)} %copy-done.1, f32[32,64,128]{2,1,0:T(8,128)S(1)} %gather_rows.15), kind=kLoop, calls=%fused_computation.11 | loop fusion | flops 393216 | bytes 2621440 | tf_op jit(solution)/shard_map/add | solution.py:386
  87.6 4.6 %all-to-all-done.refs_0_ = f32[16,64,128]{2,1,0:T(8,128)S(1)} async-done(((f32[16,64,128]{2,1,0:T(8,128)}), f32[16,64,128]{2,1,0:T(8,128)S(1)}, u32[]{:S(2)}, u32[]{:S(2)}) %all-to-all-start) | async-done | bytes 524320 | tf_op jit(solution)/shard_map/all_to_all | solution.py:388
  92.2 3.6 %all-to-all-start.1 = ((f32[16,64,128]{2,1,0:T(8,128)}), f32[16,64,128]{2,1,0:T(8,128)S(1)}, u32[]{:S(2)}, u32[]{:S(2)}) async-start(f32[16,64,128]{2,1,0:T(8,128)} %add_add_fusion), calls=%async_computation.1 | async-start | bytes 1048576 | tf_op jit(solution)/shard_map/all_to_all | solution.py:388
  95.8 3.1 %collective-permute-start.10 = (f32[16,64,128]{2,1,0:T(8,128)S(1)}, f32[16,64,128]{2,1,0:T(8,128)S(1)}, u32[]{:S(2)}, u32[]{:S(2)}) collective-permute-start(f32[16,64,128]{2,1,0:T(8,128)S(1)} %all-to-all-done.refs_0_), channel_id=1, source_target_pairs={{0,16},{16,0},{32,48},{48,32},{64,80},{80,64},{96,112},{112,96},{1... | collective-permute-start | bytes 1572872 | tf_op jit(solution)/shard_map/ppermute | solution.py:389
  98.9 5.9 %all-to-all-done.1.refs_1_ = f32[16,64,128]{2,1,0:T(8,128)S(1)} async-done(((f32[16,64,128]{2,1,0:T(8,128)}), f32[16,64,128]{2,1,0:T(8,128)S(1)}, u32[]{:S(2)}, u32[]{:S(2)}) %all-to-all-start.1) | async-done | bytes 524320 | tf_op jit(solution)/shard_map/all_to_all | solution.py:388
  104.8 4.2 %collective-permute-start.11 = (f32[16,64,128]{2,1,0:T(8,128)S(1)}, f32[16,64,128]{2,1,0:T(8,128)S(1)}, u32[]{:S(2)}, u32[]{:S(2)}) collective-permute-start(f32[16,64,128]{2,1,0:T(8,128)S(1)} %all-to-all-done.1.refs_1_), channel_id=1, source_target_pairs={{0,16},{16,0},{32,48},{48,32},{64,80},{80,64},{96,112},{112,96},{1... | collective-permute-start | bytes 1572872 | tf_op jit(solution)/shard_map/ppermute | solution.py:389
  108.9 0.0 collective-permute-done.10.refs_2_
  108.9 1.5 collective-permute-done.11.refs_3_
  110.5 4.1 %partial_gram.1 = f32[4,16,40,128]{3,2,1,0:T(8,128)S(1)} custom-call(s32[1]{0:T(128)} %bitcast.13.core_ref, f32[16,64,128]{2,1,0:T(8,128)S(1)} %all-to-all-done.refs_0_, f32[16,64,128]{2,1,0:T(8,128)S(1)} %all-to-all-done.1.refs_1_, f32[16,64,128]{2,1,0:T(8,128)S(1)} %collective-permute-done.10.refs_2_, f32[16,64,128]{2,1,0:T(8,128)S(1)} %collective-permute-done.11.refs_3_), custom_call_target="tpu_custom_call" | custom-call | tf_op jit(solution)/shard_map/partial_gram/pallas_call | solution.py:290
  114.5 25.8 %all_to_all.20.x_ref = f32[64,40,128]{2,1,0:T(8,128)S(1)} all-to-all(f32[64,40,128]{2,1,0:T(8,128)S(1)} %bitcast.24), channel_id=1, replica_groups={{0,1,2,3,4,5,6,7,8,9,10,11,12,13,14,15,32,33,34,35,36,37,38,39,40,41,42..., dimensions={0} | all-to-all | bytes 2621440 | tf_op jit(solution)/shard_map/all_to_all | solution.py:398
  140.4 0.2 sum_tiles.1
  140.6 1.5 collective-permute-start.12
  142.1 4.9 %collective-permute-done.12 = f32[64,64]{1,0:T(8,128)S(1)} collective-permute-done((f32[64,64]{1,0:T(8,128)S(1)}, f32[64,64]{1,0:T(8,128)S(1)}, u32[]{:S(2)}, u32[]{:S(2)}) %collective-permute-start.12) | collective-permute-done | bytes 16416 | tf_op jit(solution)/shard_map/ppermute | solution.py:409
  147.0 0.1 pad_maximum_fusion
  147.1 0.7 broadcast_in_dim.2
  147.9 6.1 %all-to-all-start.3 = ((f32[8,72,128]{2,1,0:T(8,128)}), f32[8,72,128]{2,1,0:T(8,128)S(1)}, u32[]{:S(2)}, u32[]{:S(2)}) async-start(f32[8,72,128]{2,1,0:T(8,128)} %broadcast_in_dim.2), calls=%async_computation.3 | async-start | bytes 589824 | tf_op jit(solution)/shard_map/all_to_all | solution.py:411
  153.9 2.2 %copy_bitcast_fusion = f32[64,4096]{1,0:T(8,128)} fusion(f32[16,64,128]{2,1,0:T(8,128)} %add_add_fusion, f32[16,64,128]{2,1,0:T(8,128)} %fusion.1), kind=kLoop, calls=%fused_computation | loop fusion | flops 262144 | bytes 2097152 | tf_op jit(solution)/shard_map/reshape | solution.py:390
  156.2 4.6 %all-to-all-done.3.x_ref = f32[8,72,128]{2,1,0:T(8,128)S(1)} async-done(((f32[8,72,128]{2,1,0:T(8,128)}), f32[8,72,128]{2,1,0:T(8,128)S(1)}, u32[]{:S(2)}, u32[]{:S(2)}) %all-to-all-start.3) | async-done | bytes 294944 | tf_op jit(solution)/shard_map/all_to_all | solution.py:411
  160.8 0.9 place_tiles.1
  (1 shorter events, 0.0 us)
Async XLA Ops:
  0.6 0.9 copy-start
  27.1 6.1 %collective-permute-start = (f32[32,64,128]{2,1,0:T(8,128)S(1)}, f32[32,64,128]{2,1,0:T(8,128)S(1)}, u32[]{:S(2)}, u32[]{:S(2)}) collective-permute-start(f32[32,64,128]{2,1,0:T(8,128)S(1)} %gather_rows.8.refs_4_), channel_id=1, source_target_pairs={{0,16},{16,0},{32,48},{48,32},{64,80},{80,64},{96,112},{112,96},{1... | collective-permute-start | bytes 3145736 | tf_op jit(solution)/shard_map/ppermute | solution.py:367
  34.1 25.6 %collective-permute-start.1 = (f32[16,64,128]{2,1,0:T(8,128)}, f32[16,64,128]{2,1,0:T(8,128)}, u32[]{:S(2)}, u32[]{:S(2)}) collective-permute-start(f32[16,64,128]{2,1,0:T(8,128)} %get-tuple-element.36.refs_5_), channel_id=1, source_target_pairs={{0,96},{16,112},{32,0},{48,16},{64,32},{80,48},{96,64},{112,80},{1... | collective-permute-start | bytes 1572872 | tf_op jit(solution)/shard_map/ppermute | solution.py:370
  37.0 14.9 %collective-permute-start.2 = (f32[16,64,128]{2,1,0:T(8,128)S(1)}, f32[16,64,128]{2,1,0:T(8,128)S(1)}, u32[]{:S(2)}, u32[]{:S(2)}) collective-permute-start(f32[16,64,128]{2,1,0:T(8,128)S(1)} %get-tuple-element.37.refs_4_), channel_id=1, source_target_pairs={{0,32},{16,48},{32,64},{48,80},{64,96},{80,112},{96,0},{112,16},{1... | collective-permute-start | bytes 1572872 | tf_op jit(solution)/shard_map/ppermute | solution.py:370
  41.6 14.9 %collective-permute-start.3 = (f32[32,64,128]{2,1,0:T(8,128)S(1)}, f32[32,64,128]{2,1,0:T(8,128)S(1)}, u32[]{:S(2)}, u32[]{:S(2)}) collective-permute-start(f32[32,64,128]{2,1,0:T(8,128)S(1)} %gather_rows.10.refs_4_), channel_id=1, source_target_pairs={{0,16},{16,0},{32,48},{48,32},{64,80},{80,64},{96,112},{112,96},{1... | collective-permute-start | bytes 3145736 | tf_op jit(solution)/shard_map/ppermute | solution.py:372
  46.6 18.1 %collective-permute-start.4 = (f32[32,64,128]{2,1,0:T(8,128)S(1)}, f32[32,64,128]{2,1,0:T(8,128)S(1)}, u32[]{:S(2)}, u32[]{:S(2)}) collective-permute-start(f32[32,64,128]{2,1,0:T(8,128)S(1)} %gather_rows.11.refs_4_), channel_id=1, source_target_pairs={{0,16},{16,0},{32,48},{48,32},{64,80},{80,64},{96,112},{112,96},{1... | collective-permute-start | bytes 3145736 | tf_op jit(solution)/shard_map/ppermute | solution.py:374
  51.5 20.7 %collective-permute-start.5 = (f32[32,64,128]{2,1,0:T(8,128)S(1)}, f32[32,64,128]{2,1,0:T(8,128)S(1)}, u32[]{:S(2)}, u32[]{:S(2)}) collective-permute-start(f32[32,64,128]{2,1,0:T(8,128)S(1)} %gather_rows.12.refs_5_), channel_id=1, source_target_pairs={{0,16},{16,0},{32,48},{48,32},{64,80},{80,64},{96,112},{112,96},{1... | collective-permute-start | bytes 3145736 | tf_op jit(solution)/shard_map/ppermute | solution.py:376
  56.7 15.5 %collective-permute-start.7 = (f32[16,64,128]{2,1,0:T(8,128)S(1)}, f32[16,64,128]{2,1,0:T(8,128)S(1)}, u32[]{:S(2)}, u32[]{:S(2)}) collective-permute-start(f32[16,64,128]{2,1,0:T(8,128)S(1)} %get-tuple-element.34.refs_6_), channel_id=1, source_target_pairs={{0,96},{16,112},{32,0},{48,16},{64,32},{80,48},{96,64},{112,80},{1... | collective-permute-start | bytes 1572872 | tf_op jit(solution)/shard_map/ppermute | solution.py:379
  59.7 14.4 %collective-permute-start.6 = (f32[16,64,128]{2,1,0:T(8,128)S(1)}, f32[16,64,128]{2,1,0:T(8,128)S(1)}, u32[]{:S(2)}, u32[]{:S(2)}) collective-permute-start(f32[16,64,128]{2,1,0:T(8,128)S(1)} %get-tuple-element.35.refs_5_), channel_id=1, source_target_pairs={{0,32},{16,48},{32,64},{48,80},{64,96},{80,112},{96,0},{112,16},{1... | collective-permute-start | bytes 1572872 | tf_op jit(solution)/shard_map/ppermute | solution.py:379
  64.8 17.9 %collective-permute-start.9 = (f32[16,64,128]{2,1,0:T(8,128)S(1)}, f32[16,64,128]{2,1,0:T(8,128)S(1)}, u32[]{:S(2)}, u32[]{:S(2)}) collective-permute-start(f32[16,64,128]{2,1,0:T(8,128)S(1)} %get-tuple-element.33.refs_5_), channel_id=1, source_target_pairs={{0,96},{16,112},{32,0},{48,16},{64,32},{80,48},{96,64},{112,80},{1... | collective-permute-start | bytes 1572872 | tf_op jit(solution)/shard_map/ppermute | solution.py:382
  67.6 17.9 %collective-permute-start.8 = (f32[16,64,128]{2,1,0:T(8,128)S(1)}, f32[16,64,128]{2,1,0:T(8,128)}, u32[]{:S(2)}, u32[]{:S(2)}) collective-permute-start(f32[16,64,128]{2,1,0:T(8,128)S(1)} %get-tuple-element.32.refs_4_), channel_id=1, source_target_pairs={{0,32},{16,48},{32,64},{48,80},{64,96},{80,112},{96,0},{112,16},{1... | collective-permute-start | bytes 1572872 | tf_op jit(solution)/shard_map/ppermute | solution.py:382
  72.2 2.0 %copy-start.1 = (f32[32,64,128]{2,1,0:T(8,128)}, f32[32,64,128]{2,1,0:T(8,128)S(1)}, u32[]{:S(2)}) copy-start(f32[32,64,128]{2,1,0:T(8,128)S(1)} %collective-permute-done.5) | copy-start | bytes 3145732
  75.1 17.1 %all-to-all-start = ((f32[16,64,128]{2,1,0:T(8,128)}), f32[16,64,128]{2,1,0:T(8,128)S(1)}, u32[]{:S(2)}, u32[]{:S(2)}) async-start(f32[16,64,128]{2,1,0:T(8,128)} %fusion.1), calls=%async_computation | async-start | bytes 1048576 | tf_op jit(solution)/shard_map/all_to_all | solution.py:388
  92.2 12.5 %all-to-all-start.1 = ((f32[16,64,128]{2,1,0:T(8,128)}), f32[16,64,128]{2,1,0:T(8,128)S(1)}, u32[]{:S(2)}, u32[]{:S(2)}) async-start(f32[16,64,128]{2,1,0:T(8,128)} %add_add_fusion), calls=%async_computation.1 | async-start | bytes 1048576 | tf_op jit(solution)/shard_map/all_to_all | solution.py:388
  95.8 13.1 %collective-permute-start.10 = (f32[16,64,128]{2,1,0:T(8,128)S(1)}, f32[16,64,128]{2,1,0:T(8,128)S(1)}, u32[]{:S(2)}, u32[]{:S(2)}) collective-permute-start(f32[16,64,128]{2,1,0:T(8,128)S(1)} %all-to-all-done.refs_0_), channel_id=1, source_target_pairs={{0,16},{16,0},{32,48},{48,32},{64,80},{80,64},{96,112},{112,96},{1... | collective-permute-start | bytes 1572872 | tf_op jit(solution)/shard_map/ppermute | solution.py:389
  104.8 5.7 %collective-permute-start.11 = (f32[16,64,128]{2,1,0:T(8,128)S(1)}, f32[16,64,128]{2,1,0:T(8,128)S(1)}, u32[]{:S(2)}, u32[]{:S(2)}) collective-permute-start(f32[16,64,128]{2,1,0:T(8,128)S(1)} %all-to-all-done.1.refs_1_), channel_id=1, source_target_pairs={{0,16},{16,0},{32,48},{48,32},{64,80},{80,64},{96,112},{112,96},{1... | collective-permute-start | bytes 1572872 | tf_op jit(solution)/shard_map/ppermute | solution.py:389
  140.6 6.4 %collective-permute-start.12 = (f32[64,64]{1,0:T(8,128)S(1)}, f32[64,64]{1,0:T(8,128)S(1)}, u32[]{:S(2)}, u32[]{:S(2)}) collective-permute-start(f32[64,64]{1,0:T(8,128)S(1)} %get-tuple-element.39), channel_id=1, source_target_pairs={{0,1},{1,2},{2,3},{3,4},{4,5},{5,6},{6,7},{7,8},{8,9},{9,10},{10,1... | collective-permute-start | bytes 49160 | tf_op jit(solution)/shard_map/ppermute | solution.py:409
  147.9 12.9 %all-to-all-start.3 = ((f32[8,72,128]{2,1,0:T(8,128)}), f32[8,72,128]{2,1,0:T(8,128)S(1)}, u32[]{:S(2)}, u32[]{:S(2)}) async-start(f32[8,72,128]{2,1,0:T(8,128)} %broadcast_in_dim.2), calls=%async_computation.3 | async-start | bytes 589824 | tf_op jit(solution)/shard_map/all_to_all | solution.py:411

commit v7 on v6

--- a/solution.py
+++ b/solution.py
@@ -203,7 +203,7 @@
 FAR, FIRST, SECOND, OWN = range(4)
 
 
-def index_kernel(width, bits, me_ref, select_ref, half_ref, sign_ref, *rows_refs):
+def index_kernel(width, bits, me_ref, select_ref, table_ref, half_ref, sign_ref, *rows_refs):
     me = me_ref[0]
     n_y, _, n_block, _ = select_ref.shape
     mid = n_block // 2
@@ -226,7 +226,7 @@
                 sign_ref[here, :] = (1 - 2 * parity).astype(jnp.float32)
 
 
-def make_index(select, me, n_param, width):
+def make_index(select, me, n_param, width, after):
     n_block = select.shape[0] // LANES
     vmem = pl.BlockSpec(memory_space=pltpu.VMEM)
     return pl.pallas_call(
@@ -235,11 +235,11 @@
             jax.ShapeDtypeStruct((n_block, LANES), jnp.int32),
             jax.ShapeDtypeStruct((n_block, LANES), jnp.float32),
         ) + (jax.ShapeDtypeStruct((n_block // n_param, LANES), jnp.int32),) * n_param,
-        in_specs=[pl.BlockSpec(memory_space=pltpu.SMEM), vmem],
+        in_specs=[pl.BlockSpec(memory_space=pltpu.SMEM), vmem, pl.BlockSpec(memory_space=pl.ANY)],
         out_specs=(vmem,) * (2 + n_param),
         compiler_params=pltpu.CompilerParams(vmem_limit_bytes=4 * 1024 * 1024),
         name="make_index",
-    )(me.reshape(1), select.reshape(n_param // 2, 2, n_block // n_param, LANES))
+    )(me.reshape(1), select.reshape(n_param // 2, 2, n_block // n_param, LANES), after)
 
 
 def gram_kernel(n_ex, core_ref, *refs):
@@ -272,15 +272,12 @@
                 first = pl.multiple_of((8 + v - offset) * n_ex, n_ex)
                 top = part_ref[pl.ds(first, n_ex // 2), lanes]
                 low = part_ref[pl.ds(first + n_ex // 2, n_ex // 2), lanes]
-                strip = part_ref[pl.ds(pl.multiple_of((8 + v) * n_ex + 8 * (offset - 1), 8), 8), lanes]
                 if v % 2:
                     top = pltpu.roll(top, half, 1)
-                    strip = pltpu.roll(strip, half, 1)
                 else:
                     low = pltpu.roll(low, half, 1)
                 row_block = (quad * 4 + v + blocks - offset) & (blocks - 1)
-                out_ref[m, row_block, :n_ex // 2, :] = jnp.where(left, top, low)
-                out_ref[m, quad * 4 + v, n_ex // 2:, :] = strip
+                out_ref[m, row_block] = jnp.where(left, top, low)
 
 
 def partial_gram(shares, core):
@@ -289,7 +286,7 @@
     vmem = pl.BlockSpec(memory_space=pltpu.VMEM)
     return pl.pallas_call(
         functools.partial(gram_kernel, n_ex),
-        out_shape=jax.ShapeDtypeStruct((4, blocks, n_ex // 2 + 8, LANES), jnp.float32),
+        out_shape=jax.ShapeDtypeStruct((4, blocks, n_ex // 2, LANES), jnp.float32),
         in_specs=[pl.BlockSpec(memory_space=pltpu.SMEM)] + [vmem] * len(shares),
         out_specs=vmem,
         scratch_shapes=[pltpu.VMEM(((blocks + 8) * n_ex, width), jnp.bfloat16)] * 2
@@ -299,24 +296,55 @@
     )(core.reshape(1), *shares)
 
 
-def sum_kernel(scale, x_ref, tile_ref, strip_ref):
-    half = LANES // 2
-    total = jnp.sum(x_ref[...], axis=0) * scale
-    pair = total[:half // 2]
-    tile = jnp.concatenate([pair[:, :half], pair[:, half:]], axis=0)
-    tile_ref[0] = tile
-    tile_ref[1] = tile.T
-    strip_ref[...] = total[half // 2:]
+def halves_side_by_side(tile):
+    rows = tile.shape[0] // 2
+    return jnp.concatenate([tile[:rows], tile[rows:]], axis=1)
+
+
+def halves_stacked(pair):
+    lanes = pair.shape[1] // 2
+    return jnp.concatenate([pair[:, :lanes], pair[:, lanes:]], axis=0)
+
+
+def diagonal_kernel(*refs):
+    out_ref = refs[-1]
+    nt = (((1,), (1,)), ((), ()))
+    same = cross = 0.0
+    for ref in refs[:-1]:
+        x = jnp.concatenate([ref[b] for b in range(ref.shape[0])], axis=1)
+        high = x.astype(jnp.bfloat16)
+        low = (x - high.astype(jnp.float32)).astype(jnp.bfloat16)
+        same += lax.dot_general(high, high, nt, preferred_element_type=jnp.float32)
+        cross += lax.dot_general(high, low, nt, preferred_element_type=jnp.float32)
+    out_ref[...] = halves_side_by_side((same + cross + cross.T) * (1.0 / K))
+
+
+def diagonal_part(features):
+    n_ex = features[0].shape[1]
+    vmem = pl.BlockSpec(memory_space=pltpu.VMEM)
+    return pl.pallas_call(
+        diagonal_kernel,
+        out_shape=jax.ShapeDtypeStruct((n_ex // 2, 2 * n_ex), jnp.float32),
+        in_specs=[vmem] * len(features),
+        out_specs=vmem,
+        compiler_params=pltpu.CompilerParams(vmem_limit_bytes=8 * 1024 * 1024),
+        cost_estimate=pl.CostEstimate(flops=4 * 10**9, bytes_accessed=2**20, transcendentals=0),
+        name="diagonal_part",
+    )(*features)
+
+
+def sum_kernel(x_ref, tile_ref, turned_ref):
+    tile = halves_stacked(jnp.sum(x_ref[...], axis=0) * (1.0 / K))
+    tile_ref[...] = tile
+    turned_ref[...] = tile.T
 
 
 def sum_tiles(received):
-    vmem = pl.BlockSpec(memory_space=pltpu.VMEM)
-    return pl.pallas_call(
-        functools.partial(sum_kernel, 1.0 / K),
-        out_shape=(
-            jax.ShapeDtypeStruct((2, LANES // 2, LANES // 2), jnp.float32),
-            jax.ShapeDtypeStruct((8, LANES), jnp.float32),
-        ),
+    n_ex = 2 * received.shape[1]
+    vmem = pl.BlockSpec(memory_space=pltpu.VMEM)
+    return pl.pallas_call(
+        sum_kernel,
+        out_shape=(jax.ShapeDtypeStruct((n_ex, n_ex), jnp.float32),) * 2,
         in_specs=[vmem],
         out_specs=(vmem, vmem),
         compiler_params=pltpu.CompilerParams(vmem_limit_bytes=4 * 1024 * 1024),
@@ -324,11 +352,32 @@
     )(received)
 
 
+def message_kernel(tile_ref, turned_ref, part_ref, out_ref):
+    n_ex = tile_ref.shape[0]
+    pair = jnp.concatenate([tile_ref[...], turned_ref[...]], axis=1)
+    for p in range(out_ref.shape[0]):
+        out_ref[p, :n_ex, :] = pair
+        out_ref[p, n_ex:, :] = part_ref[...]
+
+
+def messages(tile, turned, part, count):
+    rows = tile.shape[0] + part.shape[0]
+    vmem = pl.BlockSpec(memory_space=pltpu.VMEM)
+    return pl.pallas_call(
+        message_kernel,
+        out_shape=jax.ShapeDtypeStruct((count, rows, LANES), jnp.float32),
+        in_specs=[vmem] * 3,
+        out_specs=vmem,
+        compiler_params=pltpu.CompilerParams(vmem_limit_bytes=4 * 1024 * 1024),
+        name="messages",
+    )(tile, turned, part)
+
+
 def place_kernel(me_ref, x_ref, out_ref):
     half = LANES // 2
     count = out_ref.shape[1] // half
     columns = [None] * count
-    columns[0] = jnp.concatenate([x_ref[p, half:, :half] for p in range(8)], axis=0)
+    columns[0] = halves_stacked(jnp.sum(x_ref[:, half:, :], axis=0))
     for p in range(8):
         columns[p + 1] = x_ref[p, :half, :half]
         if count - 1 - p > p + 1:
@@ -354,7 +403,7 @@
     n_ex, _, width = activations.shape
     me = lax.axis_index("param")
     table = make_table(activations, cotangents, token_ids, signs)
-    index = make_index(select, me, n_param, width)
+    index = make_index(select, me, n_param, width, table)
     n_block = select.shape[0] // n_param // LANES
     n_y = n_param // 2
     swap = [(i, i ^ 1) for i in range(n_param)]
@@ -402,14 +451,13 @@
         concat_axis=0,
         axis_index_groups=alike,
     )
-    tile, strip = sum_tiles(received)
+    tile, turned = sum_tiles(received)
     onward = [
         (p * n_group + e, p * n_group + (e + p + 1) % n_group) for p in range(n_param) for e in range(n_group)
     ]
-    turned = lax.ppermute(tile[1], everyone, onward)
-    message = jnp.concatenate([jnp.concatenate([tile[0], turned], axis=1), strip], axis=0)
+    turned = lax.ppermute(turned, everyone, onward)
     spread = lax.all_to_all(
-        jnp.broadcast_to(message[None], (n_param,) + message.shape), "param", split_axis=0, concat_axis=0
+        messages(tile, turned, diagonal_part(features), n_param), "param", split_axis=0, concat_axis=0
     )
     gram = place_tiles(spread, lax.axis_index("ex"), n_ex, n_group)
     return (whole_features, gram)

time: 162 us -> 161 us (level)
  blocking collectives: 25.8 us -> 0 us
  waiting for transfers between devices: 26.2 us -> 43.9 us
  starting transfers between devices: 37.2 us -> 42.2 us
  Pallas kernels: 63.3 us -> 66.9 us
  local copies, waits for them, and re-layouts: 1.66 us -> 0.01 us
    all_to_all x1 -> x0, blocking collectives: 25.8 us -> none  [body(): lax.all_to_all(partial.reshape(n_y * n_group, rows_out, LANES), everyone,...]
    all_to_all x1 -> x2, waiting for transfers between devices: 4.59 us -> 24 us  [the longest x1 18.1 us: body(): lax.all_to_all(partial.reshape(n_y * n_group, rows_out, LANES), everyone,...]
    all_to_all x1 -> x2, starting transfers between devices: 6.06 us -> 11.2 us  [the longest x1 5.99 us: body(): lax.all_to_all(messages(tile, turned, diagonal_part(features), n_param),...]
    pallas_call x1 -> x3, Pallas kernels: 0.23 us -> 2.82 us  [the longest x1 1.76 us: diagonal_part(): pl.pallas_call(diagonal_kernel, out_shape=jax.ShapeDtypeStruct((n_ex // 2...]
    ppermute x1, waiting for transfers between devices: 4.9 us -> 3.28 us  [body(): turned = lax.ppermute(turned, everyone, onward)]
  transfers between devices with their start and end apart: 16 -> 17, of which waited for: 7 -> 8; matrix products, arithmetic and copies ran while one was open for 4% -> 4% of each run, Pallas kernels for 20% -> 21%
where the time goes in v7:
time: 161 us; the launch traced here: 160 us
  Pallas kernels  66.9 us (42%)
  waiting for transfers between devices  43.9 us (27%)
  starting transfers between devices  42.2 us (26%)
  other arithmetic  6.65 us (4%)
    pallas_call x8, Pallas kernels, gather_rows(): pl.pallas_call(kernel, out_shape=jax.ShapeDtypeStruct((n_block, LANES //...  37.2 us
    pallas_call x1, Pallas kernels, make_table(): pl.pallas_call(functools.partial(table_kernel, n_ex, width), out_shape=pl...  20.8 us
    all_to_all x1, waiting for transfers between devices, body(): lax.all_to_all(partial.reshape(n_y * n_group, rows_out, LANES), everyone,...  18.1 us
    all_to_all x2, starting transfers between devices, body(): lax.all_to_all(x, 'ex', split_axis=0, concat_axis=0)  11.2 us
    all_to_all x2, waiting for transfers between devices, body(): lax.all_to_all(x, 'ex', split_axis=0, concat_axis=0)  10.4 us
    ppermute x3, starting transfers between devices, body(): lax.ppermute(outward[1], 'param', along(-1))  8.58 us
    ppermute x2, starting transfers between devices, body(): shares += [lax.ppermute(x, 'param', swap) for x in shares]  7.34 us
    all_to_all x1, starting transfers between devices, body(): lax.all_to_all(messages(tile, turned, diagonal_part(features), n_param),...  5.99 us
  transfers between devices with their start and end apart: 17, of which 8 were waited for; matrix products, arithmetic and copies ran while one was open for 4% of the time, Pallas kernels for 21%

profile of v7, /device:TPU:1, one launch (start us, length us, event | category | flops | bytes accessed | tf_op | source)
XLA Modules:
  0.0 160.4 jit_solution(13363611616557458177)
XLA Ops:
  0.6 0.0 copy-start
  0.6 20.8 %make_table.1.table_ref.refs_1_ = f32[32768,128]{1,0:T(8,128)S(1)} custom-call(bf16[64,128,1024]{2,1,0:T(8,128)(2,1)} %acts_ref.1, bf16[64,64,128]{2,1,0:T(8,128)(2,1)} %bitcast.29, s32[64,128]{1,0:T(8,128)} %refs_1_.1, s32[64,1024]{1,0:T(8,128)} %refs_2_.1, bf16[256,256]{1,0:T(8,128)(2,1)} %constant.24.clone.refs_3_), custom_call_target="tpu_custom_call" | custom-call | flops 9999999827968 | bytes 33554432 | tf_op jit(solution)/shard_map/make_table/pallas_call | solution.py:144
  21.5 0.0 copy-done
  21.5 0.1 make_index.1
  21.6 4.6 %gather_rows.8.refs_4_ = f32[32,64,128]{2,1,0:T(8,128)S(1)} custom-call(s32[4096]{0:T(1024)S(1)} %bitcast.28, f32[32768,128]{1,0:T(8,128)S(1)} %make_table.1.table_ref.refs_1_, s32[256,128]{1,0:T(8,128)S(1)} %get-tuple-element.18.refs_2_, f32[256,128]{1,0:T(8,128)S(1)} %get-tuple-element.19.refs_3_), custom_call_target="tpu_custom_call" | custom-call | flops 40960000000 | bytes 16777216 | tf_op jit(solution)/shard_map/gather_rows/pallas_call | solution.py:188
  26.2 1.5 collective-permute-start
  27.7 4.6 %gather_rows.9 = f32[32,64,128]{2,1,0:T(8,128)S(1)} custom-call(s32[4096]{0:T(1024)S(1)} %bitcast.27, f32[32768,128]{1,0:T(8,128)S(1)} %make_table.1.table_ref.refs_1_, s32[256,128]{1,0:T(8,128)S(1)} %get-tuple-element.18.refs_2_, f32[256,128]{1,0:T(8,128)S(1)} %get-tuple-element.19.refs_3_, f32[32,64,128]{2,1,0:T(8,128)S(1)} %gather_rows.8.refs_4_), custom_call_target="tpu_custom_call" | custom-call | flops 40960000000 | bytes 16777216 | tf_op jit(solution)/shard_map/gather_rows/pallas_call | solution.py:188
  32.3 0.0 collective-permute-done
  32.3 1.0 slice_add_fusion.6
  33.3 2.8 %collective-permute-start.1 = (f32[16,64,128]{2,1,0:T(8,128)}, f32[16,64,128]{2,1,0:T(8,128)}, u32[]{:S(2)}, u32[]{:S(2)}) collective-permute-start(f32[16,64,128]{2,1,0:T(8,128)} %get-tuple-element.36.refs_5_), channel_id=1, source_target_pairs={{0,96},{16,112},{32,0},{48,16},{64,32},{80,48},{96,64},{112,80},{1... | collective-permute-start | bytes 1572872 | tf_op jit(solution)/shard_map/ppermute | solution.py:419
  36.1 0.0 collective-permute-start.2
  36.1 4.6 %gather_rows.10.refs_4_ = f32[32,64,128]{2,1,0:T(8,128)S(1)} custom-call(s32[4096]{0:T(1024)S(1)} %bitcast.26, f32[32768,128]{1,0:T(8,128)S(1)} %make_table.1.table_ref.refs_1_, s32[256,128]{1,0:T(8,128)S(1)} %get-tuple-element.18.refs_2_, f32[256,128]{1,0:T(8,128)S(1)} %get-tuple-element.19.refs_3_, f32[16,64,128]{2,1,0:T(8,128)S(1)} %get-tuple-element.37.refs_4_, ...), custom_call_target="tpu_custom_call" | custom-call | flops 40960000000 | bytes 16777216 | tf_op jit(solution)/shard_map/gather_rows/pallas_call | solution.py:188
  40.7 0.4 collective-permute-start.3
  41.1 4.6 %gather_rows.11.refs_4_ = f32[32,64,128]{2,1,0:T(8,128)S(1)} custom-call(s32[4096]{0:T(1024)S(1)} %bitcast.25, f32[32768,128]{1,0:T(8,128)S(1)} %make_table.1.table_ref.refs_1_, s32[256,128]{1,0:T(8,128)S(1)} %get-tuple-element.18.refs_2_, f32[256,128]{1,0:T(8,128)S(1)} %get-tuple-element.19.refs_3_, f32[32,64,128]{2,1,0:T(8,128)S(1)} %gather_rows.10.refs_4_), custom_call_target="tpu_custom_call" | custom-call | flops 40960000000 | bytes 16777216 | tf_op jit(solution)/shard_map/gather_rows/pallas_call | solution.py:188
  45.7 0.3 collective-permute-start.4
  46.0 4.6 %gather_rows.12.refs_5_ = f32[32,64,128]{2,1,0:T(8,128)S(1)} custom-call(s32[4096]{0:T(1024)S(1)} %bitcast.24, f32[32768,128]{1,0:T(8,128)S(1)} %make_table.1.table_ref.refs_1_, s32[256,128]{1,0:T(8,128)S(1)} %get-tuple-element.18.refs_2_, f32[256,128]{1,0:T(8,128)S(1)} %get-tuple-element.19.refs_3_, f32[32,64,128]{2,1,0:T(8,128)S(1)} %gather_rows.11.refs_4_), custom_call_target="tpu_custom_call" | custom-call | flops 40960000000 | bytes 16777216 | tf_op jit(solution)/shard_map/gather_rows/pallas_call | solution.py:188
  50.6 0.4 collective-permute-start.5
  51.0 0.0 collective-permute-done.2.refs_4_
  51.0 4.6 %gather_rows.13 = f32[32,64,128]{2,1,0:T(8,128)S(1)} custom-call(s32[4096]{0:T(1024)S(1)} %bitcast.23, f32[32768,128]{1,0:T(8,128)S(1)} %make_table.1.table_ref.refs_1_, s32[256,128]{1,0:T(8,128)S(1)} %get-tuple-element.18.refs_2_, f32[256,128]{1,0:T(8,128)S(1)} %get-tuple-element.19.refs_3_, f32[16,64,128]{2,1,0:T(8,128)S(1)} %collective-permute-done.2.refs_4_, ...), custom_call_target="tpu_custom_call" | custom-call | flops 40960000000 | bytes 16777216 | tf_op jit(solution)/shard_map/gather_rows/pallas_call | solution.py:188
  55.7 0.0 collective-permute-done.3
  55.7 0.2 slice_add_fusion.3
  55.9 3.0 %collective-permute-start.7 = (f32[16,64,128]{2,1,0:T(8,128)S(1)}, f32[16,64,128]{2,1,0:T(8,128)S(1)}, u32[]{:S(2)}, u32[]{:S(2)}) collective-permute-start(f32[16,64,128]{2,1,0:T(8,128)S(1)} %get-tuple-element.34.refs_6_), channel_id=1, source_target_pairs={{0,96},{16,112},{32,0},{48,16},{64,32},{80,48},{96,64},{112,80},{1... | collective-permute-start | bytes 1572872 | tf_op jit(solution)/shard_map/ppermute | solution.py:428
  58.9 0.0 collective-permute-start.6
  58.9 0.0 collective-permute-done.1.refs_4_
  58.9 4.9 %gather_rows.14 = f32[32,64,128]{2,1,0:T(8,128)S(1)} custom-call(s32[4096]{0:T(1024)S(1)} %bitcast.22, f32[32768,128]{1,0:T(8,128)S(1)} %make_table.1.table_ref.refs_1_, s32[256,128]{1,0:T(8,128)S(1)} %get-tuple-element.18.refs_2_, f32[256,128]{1,0:T(8,128)S(1)} %get-tuple-element.19.refs_3_, f32[16,64,128]{2,1,0:T(8,128)} %collective-permute-done.1.refs_4_, ...), custom_call_target="tpu_custom_call" | custom-call | flops 40960000000 | bytes 16777216 | tf_op jit(solution)/shard_map/gather_rows/pallas_call | solution.py:188
  63.8 0.0 collective-permute-done.4
  63.8 0.2 slice_add_fusion.2
  64.0 2.7 %collective-permute-start.9 = (f32[16,64,128]{2,1,0:T(8,128)S(1)}, f32[16,64,128]{2,1,0:T(8,128)S(1)}, u32[]{:S(2)}, u32[]{:S(2)}) collective-permute-start(f32[16,64,128]{2,1,0:T(8,128)S(1)} %get-tuple-element.33.refs_5_), channel_id=1, source_target_pairs={{0,96},{16,112},{32,0},{48,16},{64,32},{80,48},{96,64},{112,80},{1... | collective-permute-start | bytes 1572872 | tf_op jit(solution)/shard_map/ppermute | solution.py:431
  66.7 0.0 collective-permute-start.8
  66.7 4.6 %gather_rows.15 = f32[32,64,128]{2,1,0:T(8,128)S(1)} custom-call(s32[4096]{0:T(1024)S(1)} %bitcast.21, f32[32768,128]{1,0:T(8,128)S(1)} %make_table.1.table_ref.refs_1_, s32[256,128]{1,0:T(8,128)S(1)} %get-tuple-element.18.refs_2_, f32[256,128]{1,0:T(8,128)S(1)} %get-tuple-element.19.refs_3_, f32[16,64,128]{2,1,0:T(8,128)S(1)} %get-tuple-element.32.refs_4_, ...), custom_call_target="tpu_custom_call" | custom-call | flops 40960000000 | bytes 16777216 | tf_op jit(solution)/shard_map/gather_rows/pallas_call | solution.py:188
  71.3 0.0 collective-permute-done.5
  71.3 0.0 copy-start.1
  71.4 0.0 collective-permute-done.7
  71.4 1.9 %collective-permute-done.6 = f32[16,64,128]{2,1,0:T(8,128)S(1)} collective-permute-done((f32[16,64,128]{2,1,0:T(8,128)S(1)}, f32[16,64,128]{2,1,0:T(8,128)S(1)}, u32[]{:S(2)}, u32[]{:S(2)}) %collective-permute-start.6) | collective-permute-done | bytes 524320 | tf_op jit(solution)/shard_map/ppermute | solution.py:428
  73.3 0.0 copy-done.1
  73.3 1.0 fusion.1.refs_0_
  74.2 7.6 %all-to-all-start = ((f32[16,64,128]{2,1,0:T(8,128)}), f32[16,64,128]{2,1,0:T(8,128)S(1)}, u32[]{:S(2)}, u32[]{:S(2)}) async-start(f32[16,64,128]{2,1,0:T(8,128)} %fusion.1.refs_0_), calls=%async_computation | async-start | bytes 1048576 | tf_op jit(solution)/shard_map/all_to_all | solution.py:437
  81.9 0.0 collective-permute-done.9
  81.9 2.8 %collective-permute-done.8 = f32[16,64,128]{2,1,0:T(8,128)} collective-permute-done((f32[16,64,128]{2,1,0:T(8,128)S(1)}, f32[16,64,128]{2,1,0:T(8,128)}, u32[]{:S(2)}, u32[]{:S(2)}) %collective-permute-start.8) | collective-permute-done | bytes 524320 | tf_op jit(solution)/shard_map/ppermute | solution.py:431
  84.6 2.2 %add_add_fusion.refs_1_ = f32[16,64,128]{2,1,0:T(8,128)} fusion(f32[16,64,128]{2,1,0:T(8,128)S(1)} %collective-permute-done.9, f32[16,64,128]{2,1,0:T(8,128)} %collective-permute-done.8, f32[32,64,128]{2,1,0:T(8,128)} %copy-done.1, f32[32,64,128]{2,1,0:T(8,128)S(1)} %gather_rows.15), kind=kLoop, calls=%fused_computation.11 | loop fusion | flops 393216 | bytes 2621440 | tf_op jit(solution)/shard_map/add | solution.py:435
  86.8 4.6 %all-to-all-done.refs_0_ = f32[16,64,128]{2,1,0:T(8,128)S(1)} async-done(((f32[16,64,128]{2,1,0:T(8,128)}), f32[16,64,128]{2,1,0:T(8,128)S(1)}, u32[]{:S(2)}, u32[]{:S(2)}) %all-to-all-start) | async-done | bytes 524320 | tf_op jit(solution)/shard_map/all_to_all | solution.py:437
  91.3 3.6 %all-to-all-start.1 = ((f32[16,64,128]{2,1,0:T(8,128)}), f32[16,64,128]{2,1,0:T(8,128)S(1)}, u32[]{:S(2)}, u32[]{:S(2)}) async-start(f32[16,64,128]{2,1,0:T(8,128)} %add_add_fusion.refs_1_), calls=%async_computation.1 | async-start | bytes 1048576 | tf_op jit(solution)/shard_map/all_to_all | solution.py:437
  94.9 3.1 %collective-permute-start.10 = (f32[16,64,128]{2,1,0:T(8,128)S(1)}, f32[16,64,128]{2,1,0:T(8,128)S(1)}, u32[]{:S(2)}, u32[]{:S(2)}) collective-permute-start(f32[16,64,128]{2,1,0:T(8,128)S(1)} %all-to-all-done.refs_0_), channel_id=1, source_target_pairs={{0,16},{16,0},{32,48},{48,32},{64,80},{80,64},{96,112},{112,96},{1... | collective-permute-start | bytes 1572872 | tf_op jit(solution)/shard_map/ppermute | solution.py:438
  98.1 5.8 %all-to-all-done.1.refs_1_ = f32[16,64,128]{2,1,0:T(8,128)S(1)} async-done(((f32[16,64,128]{2,1,0:T(8,128)}), f32[16,64,128]{2,1,0:T(8,128)S(1)}, u32[]{:S(2)}, u32[]{:S(2)}) %all-to-all-start.1) | async-done | bytes 524320 | tf_op jit(solution)/shard_map/all_to_all | solution.py:437
  103.9 4.2 %collective-permute-start.11 = (f32[16,64,128]{2,1,0:T(8,128)S(1)}, f32[16,64,128]{2,1,0:T(8,128)S(1)}, u32[]{:S(2)}, u32[]{:S(2)}) collective-permute-start(f32[16,64,128]{2,1,0:T(8,128)S(1)} %all-to-all-done.1.refs_1_), channel_id=1, source_target_pairs={{0,16},{16,0},{32,48},{48,32},{64,80},{80,64},{96,112},{112,96},{1... | collective-permute-start | bytes 1572872 | tf_op jit(solution)/shard_map/ppermute | solution.py:438
  108.1 0.0 collective-permute-done.10.refs_2_
  108.1 1.5 collective-permute-done.11.refs_3_
  109.6 5.0 %partial_gram.1 = f32[4,16,32,128]{3,2,1,0:T(8,128)} custom-call(s32[1]{0:T(128)} %bitcast.13.core_ref, f32[16,64,128]{2,1,0:T(8,128)S(1)} %all-to-all-done.refs_0_, f32[16,64,128]{2,1,0:T(8,128)S(1)} %all-to-all-done.1.refs_1_, f32[16,64,128]{2,1,0:T(8,128)S(1)} %collective-permute-done.10.refs_2_, f32[16,64,128]{2,1,0:T(8,128)S(1)} %collective-permute-done.11.refs_3_), custom_call_target="tpu_custom_call" | custom-call | tf_op jit(solution)/shard_map/partial_gram/pallas_call | solution.py:287
  114.6 5.2 %all-to-all-start.2 = ((f32[64,32,128]{2,1,0:T(8,128)}), f32[64,32,128]{2,1,0:T(8,128)S(1)}, u32[]{:S(2)}, u32[]{:S(2)}) async-start(f32[64,32,128]{2,1,0:T(8,128)} %bitcast.14), calls=%async_computation.2 | async-start | bytes 2097152 | tf_op jit(solution)/shard_map/all_to_all | solution.py:447
  119.8 18.1 %all-to-all-done.2.x_ref = f32[64,32,128]{2,1,0:T(8,128)S(1)} async-done(((f32[64,32,128]{2,1,0:T(8,128)}), f32[64,32,128]{2,1,0:T(8,128)S(1)}, u32[]{:S(2)}, u32[]{:S(2)}) %all-to-all-start.2) | async-done | bytes 1048608 | tf_op jit(solution)/shard_map/all_to_all | solution.py:447
  137.9 0.2 sum_tiles.1
  138.2 1.4 collective-permute-start.12
  139.5 1.8 %diagonal_part.1.part_ref = f32[32,128]{1,0:T(8,128)S(1)} custom-call(f32[16,64,128]{2,1,0:T(8,128)} %fusion.1.refs_0_, f32[16,64,128]{2,1,0:T(8,128)} %add_add_fusion.refs_1_), custom_call_target="tpu_custom_call" | custom-call | flops 4000000000 | bytes 1048576 | tf_op jit(solution)/shard_map/diagonal_part/pallas_call | solution.py:325
  141.3 3.3 %collective-permute-done.12.turned_ref = f32[64,64]{1,0:T(8,128)S(1)} collective-permute-done((f32[64,64]{1,0:T(8,128)S(1)}, f32[64,64]{1,0:T(8,128)S(1)}, u32[]{:S(2)}, u32[]{:S(2)}) %collective-permute-start.12) | collective-permute-done | bytes 16416 | tf_op jit(solution)/shard_map/ppermute | solution.py:458
  144.6 0.8 messages.1
  145.4 6.0 %all-to-all-start.3 = ((f32[8,96,128]{2,1,0:T(8,128)}), f32[8,96,128]{2,1,0:T(8,128)S(1)}, u32[]{:S(2)}, u32[]{:S(2)}) async-start(f32[8,96,128]{2,1,0:T(8,128)} %messages.1), calls=%async_computation.3 | async-start | bytes 786432 | tf_op jit(solution)/shard_map/all_to_all | solution.py:459
  151.4 2.2 %copy_bitcast_fusion = f32[64,4096]{1,0:T(8,128)} fusion(f32[16,64,128]{2,1,0:T(8,128)} %add_add_fusion.refs_1_, f32[16,64,128]{2,1,0:T(8,128)} %fusion.1.refs_0_), kind=kLoop, calls=%fused_computation | loop fusion | flops 262144 | bytes 2097152 | tf_op jit(solution)/shard_map/reshape | solution.py:439
  153.6 5.9 %all-to-all-done.3.x_ref = f32[8,96,128]{2,1,0:T(8,128)S(1)} async-done(((f32[8,96,128]{2,1,0:T(8,128)}), f32[8,96,128]{2,1,0:T(8,128)S(1)}, u32[]{:S(2)}, u32[]{:S(2)}) %all-to-all-start.3) | async-done | bytes 393248 | tf_op jit(solution)/shard_map/all_to_all | solution.py:459
  159.5 0.9 place_tiles.1
Async XLA Ops:
  0.6 20.8 %copy-start = (s32[32768]{0:T(1024)S(1)}, s32[32768]{0:T(1024)}, u32[]{:S(2)}) copy-start(s32[32768]{0:T(1024)} %param.10) | copy-start | bytes 393220
  26.2 6.1 %collective-permute-start = (f32[32,64,128]{2,1,0:T(8,128)S(1)}, f32[32,64,128]{2,1,0:T(8,128)S(1)}, u32[]{:S(2)}, u32[]{:S(2)}) collective-permute-start(f32[32,64,128]{2,1,0:T(8,128)S(1)} %gather_rows.8.refs_4_), channel_id=1, source_target_pairs={{0,16},{16,0},{32,48},{48,32},{64,80},{80,64},{96,112},{112,96},{1... | collective-permute-start | bytes 3145736 | tf_op jit(solution)/shard_map/ppermute | solution.py:416
  33.3 25.6 %collective-permute-start.1 = (f32[16,64,128]{2,1,0:T(8,128)}, f32[16,64,128]{2,1,0:T(8,128)}, u32[]{:S(2)}, u32[]{:S(2)}) collective-permute-start(f32[16,64,128]{2,1,0:T(8,128)} %get-tuple-element.36.refs_5_), channel_id=1, source_target_pairs={{0,96},{16,112},{32,0},{48,16},{64,32},{80,48},{96,64},{112,80},{1... | collective-permute-start | bytes 1572872 | tf_op jit(solution)/shard_map/ppermute | solution.py:419
  36.1 14.9 %collective-permute-start.2 = (f32[16,64,128]{2,1,0:T(8,128)S(1)}, f32[16,64,128]{2,1,0:T(8,128)S(1)}, u32[]{:S(2)}, u32[]{:S(2)}) collective-permute-start(f32[16,64,128]{2,1,0:T(8,128)S(1)} %get-tuple-element.37.refs_4_), channel_id=1, source_target_pairs={{0,32},{16,48},{32,64},{48,80},{64,96},{80,112},{96,0},{112,16},{1... | collective-permute-start | bytes 1572872 | tf_op jit(solution)/shard_map/ppermute | solution.py:419
  40.7 14.9 %collective-permute-start.3 = (f32[32,64,128]{2,1,0:T(8,128)S(1)}, f32[32,64,128]{2,1,0:T(8,128)S(1)}, u32[]{:S(2)}, u32[]{:S(2)}) collective-permute-start(f32[32,64,128]{2,1,0:T(8,128)S(1)} %gather_rows.10.refs_4_), channel_id=1, source_target_pairs={{0,16},{16,0},{32,48},{48,32},{64,80},{80,64},{96,112},{112,96},{1... | collective-permute-start | bytes 3145736 | tf_op jit(solution)/shard_map/ppermute | solution.py:421
  45.7 18.1 %collective-permute-start.4 = (f32[32,64,128]{2,1,0:T(8,128)S(1)}, f32[32,64,128]{2,1,0:T(8,128)S(1)}, u32[]{:S(2)}, u32[]{:S(2)}) collective-permute-start(f32[32,64,128]{2,1,0:T(8,128)S(1)} %gather_rows.11.refs_4_), channel_id=1, source_target_pairs={{0,16},{16,0},{32,48},{48,32},{64,80},{80,64},{96,112},{112,96},{1... | collective-permute-start | bytes 3145736 | tf_op jit(solution)/shard_map/ppermute | solution.py:423
  50.6 20.7 %collective-permute-start.5 = (f32[32,64,128]{2,1,0:T(8,128)S(1)}, f32[32,64,128]{2,1,0:T(8,128)S(1)}, u32[]{:S(2)}, u32[]{:S(2)}) collective-permute-start(f32[32,64,128]{2,1,0:T(8,128)S(1)} %gather_rows.12.refs_5_), channel_id=1, source_target_pairs={{0,16},{16,0},{32,48},{48,32},{64,80},{80,64},{96,112},{112,96},{1... | collective-permute-start | bytes 3145736 | tf_op jit(solution)/shard_map/ppermute | solution.py:425
  55.9 15.5 %collective-permute-start.7 = (f32[16,64,128]{2,1,0:T(8,128)S(1)}, f32[16,64,128]{2,1,0:T(8,128)S(1)}, u32[]{:S(2)}, u32[]{:S(2)}) collective-permute-start(f32[16,64,128]{2,1,0:T(8,128)S(1)} %get-tuple-element.34.refs_6_), channel_id=1, source_target_pairs={{0,96},{16,112},{32,0},{48,16},{64,32},{80,48},{96,64},{112,80},{1... | collective-permute-start | bytes 1572872 | tf_op jit(solution)/shard_map/ppermute | solution.py:428
  58.9 14.4 %collective-permute-start.6 = (f32[16,64,128]{2,1,0:T(8,128)S(1)}, f32[16,64,128]{2,1,0:T(8,128)S(1)}, u32[]{:S(2)}, u32[]{:S(2)}) collective-permute-start(f32[16,64,128]{2,1,0:T(8,128)S(1)} %get-tuple-element.35.refs_5_), channel_id=1, source_target_pairs={{0,32},{16,48},{32,64},{48,80},{64,96},{80,112},{96,0},{112,16},{1... | collective-permute-start | bytes 1572872 | tf_op jit(solution)/shard_map/ppermute | solution.py:428
  64.0 17.9 %collective-permute-start.9 = (f32[16,64,128]{2,1,0:T(8,128)S(1)}, f32[16,64,128]{2,1,0:T(8,128)S(1)}, u32[]{:S(2)}, u32[]{:S(2)}) collective-permute-start(f32[16,64,128]{2,1,0:T(8,128)S(1)} %get-tuple-element.33.refs_5_), channel_id=1, source_target_pairs={{0,96},{16,112},{32,0},{48,16},{64,32},{80,48},{96,64},{112,80},{1... | collective-permute-start | bytes 1572872 | tf_op jit(solution)/shard_map/ppermute | solution.py:431
  66.7 17.9 %collective-permute-start.8 = (f32[16,64,128]{2,1,0:T(8,128)S(1)}, f32[16,64,128]{2,1,0:T(8,128)}, u32[]{:S(2)}, u32[]{:S(2)}) collective-permute-start(f32[16,64,128]{2,1,0:T(8,128)S(1)} %get-tuple-element.32.refs_4_), channel_id=1, source_target_pairs={{0,32},{16,48},{32,64},{48,80},{64,96},{80,112},{96,0},{112,16},{1... | collective-permute-start | bytes 1572872 | tf_op jit(solution)/shard_map/ppermute | solution.py:431
  71.3 1.9 %copy-start.1 = (f32[32,64,128]{2,1,0:T(8,128)}, f32[32,64,128]{2,1,0:T(8,128)S(1)}, u32[]{:S(2)}) copy-start(f32[32,64,128]{2,1,0:T(8,128)S(1)} %collective-permute-done.5) | copy-start | bytes 3145732
  74.2 17.1 %all-to-all-start = ((f32[16,64,128]{2,1,0:T(8,128)}), f32[16,64,128]{2,1,0:T(8,128)S(1)}, u32[]{:S(2)}, u32[]{:S(2)}) async-start(f32[16,64,128]{2,1,0:T(8,128)} %fusion.1.refs_0_), calls=%async_computation | async-start | bytes 1048576 | tf_op jit(solution)/shard_map/all_to_all | solution.py:437
  91.3 12.5 %all-to-all-start.1 = ((f32[16,64,128]{2,1,0:T(8,128)}), f32[16,64,128]{2,1,0:T(8,128)S(1)}, u32[]{:S(2)}, u32[]{:S(2)}) async-start(f32[16,64,128]{2,1,0:T(8,128)} %add_add_fusion.refs_1_), calls=%async_computation.1 | async-start | bytes 1048576 | tf_op jit(solution)/shard_map/all_to_all | solution.py:437
  94.9 13.2 %collective-permute-start.10 = (f32[16,64,128]{2,1,0:T(8,128)S(1)}, f32[16,64,128]{2,1,0:T(8,128)S(1)}, u32[]{:S(2)}, u32[]{:S(2)}) collective-permute-start(f32[16,64,128]{2,1,0:T(8,128)S(1)} %all-to-all-done.refs_0_), channel_id=1, source_target_pairs={{0,16},{16,0},{32,48},{48,32},{64,80},{80,64},{96,112},{112,96},{1... | collective-permute-start | bytes 1572872 | tf_op jit(solution)/shard_map/ppermute | solution.py:438
  103.9 5.7 %collective-permute-start.11 = (f32[16,64,128]{2,1,0:T(8,128)S(1)}, f32[16,64,128]{2,1,0:T(8,128)S(1)}, u32[]{:S(2)}, u32[]{:S(2)}) collective-permute-start(f32[16,64,128]{2,1,0:T(8,128)S(1)} %all-to-all-done.1.refs_1_), channel_id=1, source_target_pairs={{0,16},{16,0},{32,48},{48,32},{64,80},{80,64},{96,112},{112,96},{1... | collective-permute-start | bytes 1572872 | tf_op jit(solution)/shard_map/ppermute | solution.py:438
  114.6 23.3 %all-to-all-start.2 = ((f32[64,32,128]{2,1,0:T(8,128)}), f32[64,32,128]{2,1,0:T(8,128)S(1)}, u32[]{:S(2)}, u32[]{:S(2)}) async-start(f32[64,32,128]{2,1,0:T(8,128)} %bitcast.14), calls=%async_computation.2 | async-start | bytes 2097152 | tf_op jit(solution)/shard_map/all_to_all | solution.py:447
  138.2 6.4 %collective-permute-start.12 = (f32[64,64]{1,0:T(8,128)S(1)}, f32[64,64]{1,0:T(8,128)S(1)}, u32[]{:S(2)}, u32[]{:S(2)}) collective-permute-start(f32[64,64]{1,0:T(8,128)S(1)} %get-tuple-element.31), channel_id=1, source_target_pairs={{0,1},{1,2},{2,3},{3,4},{4,5},{5,6},{6,7},{7,8},{8,9},{9,10},{10,1... | collective-permute-start | bytes 49160 | tf_op jit(solution)/shard_map/ppermute | solution.py:458
  145.4 14.1 %all-to-all-start.3 = ((f32[8,96,128]{2,1,0:T(8,128)}), f32[8,96,128]{2,1,0:T(8,128)S(1)}, u32[]{:S(2)}, u32[]{:S(2)}) async-start(f32[8,96,128]{2,1,0:T(8,128)} %messages.1), calls=%async_computation.3 | async-start | bytes 786432 | tf_op jit(solution)/shard_map/all_to_all | solution.py:459

commit v8 on v7

--- a/solution.py
+++ b/solution.py
@@ -102,32 +102,30 @@
                 table_ref[pl.ds((s * 4 + j) * width + q * TAP, TAP), :] = v
 
 
-def gather_kernel(segments, start, rows_ref, table_ref, half_ref, sign_ref, *refs):
-    n_extra = sum(extra is not None for _, _, extra in segments)
-    extras, out_ref, bufs = refs[:n_extra], refs[-3], refs[-2:]
-    n_block = segments[-1][1]
+def gather_kernel(start, rows_ref, table_ref, half_ref, sign_ref, *refs):
+    out_ref, bufs = refs[-3], refs[-2:]
+    n_block = out_ref.shape[0]
 
     def fetch(block, slot):
         base = pl.multiple_of(block * LANES, LANES)
         for j in range(LANES):
             bufs[slot][j:j + 1, :] = table_ref[pl.ds(rows_ref[base + j], 1), :]
 
-    def finish(block, t, extra, first):
+    def finish(block, t):
         here = pl.ds(start + block, 1)
-        picked = jnp.where(half_ref[here, :] > 0, t[LANES // 2:], t[:LANES // 2]) * sign_ref[here, :]
-        out_ref[block] = picked if extra is None else picked + extras[extra][block - first]
+        picked = jnp.where(half_ref[here, :] > 0, t[LANES // 2:], t[:LANES // 2])
+        out_ref[block] = picked * sign_ref[here, :]
 
     fetch(0, 0)
-    for first, last, extra in segments:
-
-        @pl.loop(first // 2, last // 2)
-        def _(i):
-            t = bufs[0][...].T
-            fetch(2 * i + 1, 1)
-            finish(2 * i, t, extra, first)
-            t = bufs[1][...].T
-            fetch(jnp.minimum(2 * i + 2, n_block - 1), 0)
-            finish(2 * i + 1, t, extra, first)
+
+    @pl.loop(0, n_block // 2)
+    def _(i):
+        t = bufs[0][...].T
+        fetch(2 * i + 1, 1)
+        finish(2 * i, t)
+        t = bufs[1][...].T
+        fetch(jnp.minimum(2 * i + 2, n_block - 1), 0)
+        finish(2 * i + 1, t)
 
 
 def whole(shape):
@@ -166,29 +164,17 @@
     )(activations, *small)
 
 
-def gather_rows(table, index, core, group, after=(), add=()):
+def gather_rows(table, index, core, group, after=()):
     half, sign = index[:2]
     rows = index[2 + core * len(GROUPS) + group]
     n_block = rows.shape[0]
     start = (core * len(GROUPS) + group) * n_block
-    segments, at = [], 0
-    for number, (low, high, _) in enumerate(add):
-        if at < low:
-            segments.append((at, low, None))
-        segments.append((low, high, number))
-        at = high
-    if at < n_block:
-        segments.append((at, n_block, None))
-    vmem = pl.BlockSpec(memory_space=pltpu.VMEM)
-    n_add = len(add)
-
-    def kernel(*refs):
-        gather_kernel(segments, start, *refs[:4 + n_add], *refs[4 + n_add + len(after):])
-
-    return pl.pallas_call(
-        kernel,
+    vmem = pl.BlockSpec(memory_space=pltpu.VMEM)
+    return pl.pallas_call(
+        functools.partial(gather_kernel, start),
         out_shape=jax.ShapeDtypeStruct((n_block, LANES // 2, LANES), jnp.float32),
-        in_specs=[pl.BlockSpec(memory_space=pltpu.SMEM)] + [vmem] * (3 + n_add) + [pl.BlockSpec(memory_space=pl.ANY)] * len(after),
+        in_specs=[pl.BlockSpec(memory_space=pltpu.SMEM)] + [vmem] * 3
+        + [pl.BlockSpec(memory_space=pl.ANY)] * len(after),
         out_specs=vmem,
         scratch_shapes=[pltpu.VMEM((LANES, LANES), jnp.float32)] * 2,
         compiler_params=pltpu.CompilerParams(vmem_limit_bytes=4 * 1024 * 1024),
@@ -196,7 +182,7 @@
             flops=n_block * LANES * ROW_COST, bytes_accessed=n_block * LANES * 4096, transcendentals=0
         ),
         name="gather_rows",
-    )(rows.reshape(-1), table, half, sign, *[x for _, _, x in add], *after)
+    )(rows.reshape(-1), table, half, sign, *after)
 
 
 GROUPS = (((2, 0), (2, 1)), ((1, 0), (3, 0)), ((1, 1), (3, 1)), ((0, 0), (0, 1)))
@@ -414,25 +400,23 @@
     mid = n_block // 2
     sent = gather_rows(table, index, 0, FAR)
     arrived = lax.ppermute(sent, "param", swap)
-    far = gather_rows(table, index, 1, FAR, after=(sent,))
-    outward = (far[:mid] + arrived[:mid], far[mid:] + arrived[mid:])
-    up, down = lax.ppermute(outward[0], "param", along(1)), lax.ppermute(outward[1], "param", along(-1))
-    sent_first = gather_rows(table, index, 0, FIRST, after=outward)
-    arrived_first = lax.ppermute(sent_first, "param", swap)
-    sent_second = gather_rows(table, index, 0, SECOND, after=(sent_first,))
-    arrived_second = lax.ppermute(sent_second, "param", swap)
-    sent = gather_rows(table, index, 0, OWN, after=(sent_second,))
+    outward = gather_rows(table, index, 1, FAR, after=(sent,)) + arrived
+    opposite = lax.ppermute(outward, "param", along(2))
+    near, outward = [], (outward,)
+    for group in (FIRST, SECOND):
+        sent = gather_rows(table, index, 0, group, after=outward)
+        arrived = lax.ppermute(sent, "param", swap)
+        kept = gather_rows(table, index, 1, group, after=(sent,))
+        outward = (kept[:mid] + arrived[:mid], kept[mid:] + arrived[mid:])
+        near.append(
+            lax.ppermute(outward[0], "param", along(1)) + lax.ppermute(outward[1], "param", along(-1))
+        )
+    sent = gather_rows(table, index, 0, OWN, after=outward)
     arrived = lax.ppermute(sent, "param", swap)
-    first = gather_rows(table, index, 1, FIRST, after=(sent,), add=((0, mid, up),))
-    outward = (first[:mid] + arrived_first[:mid], first[mid:] + arrived_first[mid:])
-    first = lax.ppermute(outward[0], "param", along(1)), lax.ppermute(outward[1], "param", along(-1))
-    second = gather_rows(table, index, 1, SECOND, after=outward, add=((mid, n_block, down),))
-    outward = (second[:mid] + arrived_second[:mid], second[mid:] + arrived_second[mid:])
-    second = lax.ppermute(outward[0], "param", along(1)), lax.ppermute(outward[1], "param", along(-1))
-    own = gather_rows(table, index, 1, OWN, after=outward)
-    front = own[:mid] + arrived[:mid] + first[0] + first[1]
-    own, arrived, front = lax.optimization_barrier((own, arrived, front))
-    back = own[mid:] + arrived[mid:] + second[0] + second[1]
+    own = gather_rows(table, index, 1, OWN, after=(sent,))
+    front = own[:mid] + arrived[:mid] + opposite[:mid] + near[0]
+    own, arrived, opposite, front = lax.optimization_barrier((own, arrived, opposite, front))
+    back = own[mid:] + arrived[mid:] + opposite[mid:] + near[1]
     features = (front, back)
     shares = [lax.all_to_all(x, "ex", split_axis=0, concat_axis=0) for x in features]
     shares += [lax.ppermute(x, "param", swap) for x in shares]

time: 161 us -> 163 us (1.012)
  other arithmetic: 6.65 us -> 9.42 us
  starting transfers between devices: 42.2 us -> 40.5 us
    ppermute x3 -> x2, starting transfers between devices: 8.58 us -> 2.87 us  [body(): lax.ppermute(outward[1], 'param', along(-1))]
    ppermute x3 -> x2, waiting for transfers between devices: 4.68 us -> 0.01 us  [body(): lax.ppermute(outward[0], 'param', along(1))]
    all_to_all x2, waiting for transfers between devices: 10.4 us -> 14.4 us  [body(): lax.all_to_all(x, 'ex', split_axis=0, concat_axis=0)]
    add x5, other arithmetic: 4.42 us -> 7.18 us  [the longest x1 2.37 us: body(): front = own[:mid] + arrived[:mid] + opposite[:mid] + near[0]]
    ppermute x2 -> x1, starting transfers between devices: 0.67 us -> 3 us  [body(): opposite = lax.ppermute(outward, 'param', along(2))]
    ppermute x2, starting transfers between devices: 7.34 us -> 5.61 us  [body(): shares += [lax.ppermute(x, 'param', swap) for x in shares]]
  transfers between devices with their start and end apart: 17 -> 16, of which waited for: 8 -> 8; matrix products, arithmetic and copies ran while one was open for 4% -> 5% of each run, Pallas kernels for 21% -> 21%
where the time goes in v8:
time: 163 us
  Pallas kernels  66.6 us (41%)
  waiting for transfers between devices  44.5 us (27%)
  starting transfers between devices  40.5 us (25%)
  other arithmetic  9.42 us (6%)
    pallas_call x8, Pallas kernels, gather_rows(): pl.pallas_call(functools.partial(gather_kernel, start), out_shape=jax.Sha...  36.9 us
    pallas_call x1, Pallas kernels, make_table(): pl.pallas_call(functools.partial(table_kernel, n_ex, width), out_shape=pl...  20.8 us
    all_to_all x1, waiting for transfers between devices, body(): lax.all_to_all(partial.reshape(n_y * n_group, rows_out, LANES), everyone,...  18.1 us
    all_to_all x2, waiting for transfers between devices, body(): lax.all_to_all(x, 'ex', split_axis=0, concat_axis=0)  14.4 us
    all_to_all x2, starting transfers between devices, body(): lax.all_to_all(x, 'ex', split_axis=0, concat_axis=0)  11.2 us
    all_to_all x1, starting transfers between devices, body(): lax.all_to_all(partial.reshape(n_y * n_group, rows_out, LANES), everyone,...  6.66 us
    all_to_all x1, starting transfers between devices, body(): lax.all_to_all(messages(tile, turned, diagonal_part(features), n_param),...  6.02 us
    all_to_all x1, waiting for transfers between devices, body(): lax.all_to_all(messages(tile, turned, diagonal_part(features), n_param),...  5.86 us
  transfers between devices with their start and end apart: 16, of which 8 were waited for; matrix products, arithmetic and copies ran while one was open for 5% of the time, Pallas kernels for 21%

profile of v8, /device:TPU:1, one launch (start us, length us, event | category | flops | bytes accessed | tf_op | source)
XLA Modules:
  0.0 162.7 jit_solution(12924648165230872667)
XLA Ops:
  0.6 0.0 copy-start
  0.6 20.8 %make_table.1.table_ref = f32[32768,128]{1,0:T(8,128)S(1)} custom-call(bf16[64,128,1024]{2,1,0:T(8,128)(2,1)} %acts_ref.1, bf16[64,64,128]{2,1,0:T(8,128)(2,1)} %bitcast.29, s32[64,128]{1,0:T(8,128)} %refs_1_.1, s32[64,1024]{1,0:T(8,128)} %refs_2_.1, bf16[256,256]{1,0:T(8,128)(2,1)} %constant.24.clone.refs_3_), custom_call_target="tpu_custom_call" | custom-call | flops 9999999827968 | bytes 33554432 | tf_op jit(solution)/shard_map/make_table/pallas_call | solution.py:142
  21.5 0.0 copy-done
  21.5 0.1 make_index.1
  21.6 4.6 %gather_rows.8.refs_0_ = f32[32,64,128]{2,1,0:T(8,128)S(1)} custom-call(s32[4096]{0:T(1024)S(1)} %bitcast.28, f32[32768,128]{1,0:T(8,128)S(1)} %make_table.1.table_ref, s32[256,128]{1,0:T(8,128)S(1)} %get-tuple-element.19.half_ref, f32[256,128]{1,0:T(8,128)S(1)} %get-tuple-element.20.sign_ref), custom_call_target="tpu_custom_call" | custom-call | flops 40960000000 | bytes 16777216 | tf_op jit(solution)/shard_map/gather_rows/pallas_call | solution.py:173
  26.2 1.5 collective-permute-start
  27.7 4.6 %gather_rows.9 = f32[32,64,128]{2,1,0:T(8,128)S(1)} custom-call(s32[4096]{0:T(1024)S(1)} %bitcast.27, f32[32768,128]{1,0:T(8,128)S(1)} %make_table.1.table_ref, s32[256,128]{1,0:T(8,128)S(1)} %get-tuple-element.19.half_ref, f32[256,128]{1,0:T(8,128)S(1)} %get-tuple-element.20.sign_ref, f32[32,64,128]{2,1,0:T(8,128)S(1)} %gather_rows.8.refs_0_), custom_call_target="tpu_custom_call" | custom-call | flops 40960000000 | bytes 16777216 | tf_op jit(solution)/shard_map/gather_rows/pallas_call | solution.py:173
  32.3 0.0 collective-permute-done
  32.3 1.2 add.43.refs_0_
  33.5 3.0 %collective-permute-start.4 = (f32[32,64,128]{2,1,0:T(8,128)}, f32[32,64,128]{2,1,0:T(8,128)}, u32[]{:S(2)}, u32[]{:S(2)}) collective-permute-start(f32[32,64,128]{2,1,0:T(8,128)} %add.43.refs_0_), channel_id=1, source_target_pairs={{0,64},{16,80},{32,96},{48,112},{64,0},{80,16},{96,32},{112,48},{1... | collective-permute-start | bytes 3145736 | tf_op jit(solution)/shard_map/ppermute | solution.py:404
  36.5 4.6 %gather_rows.10.refs_0_ = f32[32,64,128]{2,1,0:T(8,128)S(1)} custom-call(s32[4096]{0:T(1024)S(1)} %bitcast.26, f32[32768,128]{1,0:T(8,128)S(1)} %make_table.1.table_ref, s32[256,128]{1,0:T(8,128)S(1)} %get-tuple-element.19.half_ref, f32[256,128]{1,0:T(8,128)S(1)} %get-tuple-element.20.sign_ref, f32[32,64,128]{2,1,0:T(8,128)} %add.43.refs_0_), custom_call_target="tpu_custom_call" | custom-call | flops 40960000000 | bytes 16777216 | tf_op jit(solution)/shard_map/gather_rows/pallas_call | solution.py:173
  41.1 0.4 collective-permute-start.1
  41.5 4.6 %gather_rows.11 = f32[32,64,128]{2,1,0:T(8,128)S(1)} custom-call(s32[4096]{0:T(1024)S(1)} %bitcast.25, f32[32768,128]{1,0:T(8,128)S(1)} %make_table.1.table_ref, s32[256,128]{1,0:T(8,128)S(1)} %get-tuple-element.19.half_ref, f32[256,128]{1,0:T(8,128)S(1)} %get-tuple-element.20.sign_ref, f32[32,64,128]{2,1,0:T(8,128)S(1)} %gather_rows.10.refs_0_), custom_call_target="tpu_custom_call" | custom-call | flops 40960000000 | bytes 16777216 | tf_op jit(solution)/shard_map/gather_rows/pallas_call | solution.py:173
  46.1 0.0 collective-permute-done.1
  46.1 1.1 slice_add_fusion.4
  47.2 0.8 collective-permute-start.6
  48.0 0.7 collective-permute-start.5
  48.7 4.6 %gather_rows.12.refs_0_ = f32[32,64,128]{2,1,0:T(8,128)S(1)} custom-call(s32[4096]{0:T(1024)S(1)} %bitcast.24, f32[32768,128]{1,0:T(8,128)S(1)} %make_table.1.table_ref, s32[256,128]{1,0:T(8,128)S(1)} %get-tuple-element.19.half_ref, f32[256,128]{1,0:T(8,128)S(1)} %get-tuple-element.20.sign_ref, f32[16,64,128]{2,1,0:T(8,128)} %get-tuple-element.37.refs_0_, ...), custom_call_target="tpu_custom_call" | custom-call | flops 40960000000 | bytes 16777216 | tf_op jit(solution)/shard_map/gather_rows/pallas_call | solution.py:173
  53.3 0.8 collective-permute-start.2
  54.2 4.6 %gather_rows.13 = f32[32,64,128]{2,1,0:T(8,128)S(1)} custom-call(s32[4096]{0:T(1024)S(1)} %bitcast.23, f32[32768,128]{1,0:T(8,128)S(1)} %make_table.1.table_ref, s32[256,128]{1,0:T(8,128)S(1)} %get-tuple-element.19.half_ref, f32[256,128]{1,0:T(8,128)S(1)} %get-tuple-element.20.sign_ref, f32[32,64,128]{2,1,0:T(8,128)S(1)} %gather_rows.12.refs_0_), custom_call_target="tpu_custom_call" | custom-call | flops 40960000000 | bytes 16777216 | tf_op jit(solution)/shard_map/gather_rows/pallas_call | solution.py:173
  58.8 0.0 collective-permute-done.2
  58.8 0.2 slice_add_fusion.2
  59.0 2.1 %collective-permute-start.8 = (f32[16,64,128]{2,1,0:T(8,128)S(1)}, f32[16,64,128]{2,1,0:T(8,128)S(1)}, u32[]{:S(2)}, u32[]{:S(2)}) collective-permute-start(f32[16,64,128]{2,1,0:T(8,128)S(1)} %get-tuple-element.34.refs_1_), channel_id=1, source_target_pairs={{0,96},{16,112},{32,0},{48,16},{64,32},{80,48},{96,64},{112,80},{1... | collective-permute-start | bytes 1572872 | tf_op jit(solution)/shard_map/ppermute | solution.py:412
  61.1 0.0 collective-permute-start.7
  61.1 4.6 %gather_rows.14.refs_0_ = f32[32,64,128]{2,1,0:T(8,128)S(1)} custom-call(s32[4096]{0:T(1024)S(1)} %bitcast.22, f32[32768,128]{1,0:T(8,128)S(1)} %make_table.1.table_ref, s32[256,128]{1,0:T(8,128)S(1)} %get-tuple-element.19.half_ref, f32[256,128]{1,0:T(8,128)S(1)} %get-tuple-element.20.sign_ref, f32[16,64,128]{2,1,0:T(8,128)S(1)} %get-tuple-element.35.refs_0_, ...), custom_call_target="tpu_custom_call" | custom-call | flops 40960000000 | bytes 16777216 | tf_op jit(solution)/shard_map/gather_rows/pallas_call | solution.py:173
  65.7 0.0 collective-permute-done.4
  65.7 0.4 collective-permute-start.3
  66.1 4.6 %gather_rows.15 = f32[32,64,128]{2,1,0:T(8,128)S(1)} custom-call(s32[4096]{0:T(1024)S(1)} %bitcast.21, f32[32768,128]{1,0:T(8,128)S(1)} %make_table.1.table_ref, s32[256,128]{1,0:T(8,128)S(1)} %get-tuple-element.19.half_ref, f32[256,128]{1,0:T(8,128)S(1)} %get-tuple-element.20.sign_ref, f32[32,64,128]{2,1,0:T(8,128)S(1)} %gather_rows.14.refs_0_), custom_call_target="tpu_custom_call" | custom-call | flops 40960000000 | bytes 16777216 | tf_op jit(solution)/shard_map/gather_rows/pallas_call | solution.py:173
  70.7 1.1 collective-permute-done.6
  71.8 0.0 collective-permute-done.5
  71.8 0.0 collective-permute-done.3
  71.8 0.0 copy-start.1
  71.8 1.0 copy-done.1
  72.8 2.4 %fusion.refs_0_ = f32[16,64,128]{2,1,0:T(8,128)} fusion(f32[32,64,128]{2,1,0:T(8,128)} %collective-permute-done.4, f32[32,64,128]{2,1,0:T(8,128)S(1)} %collective-permute-done.3, f32[32,64,128]{2,1,0:T(8,128)S(1)} %gather_rows.15, f32[16,64,128]{2,1,0:T(8,128)} %collective-permute-done.5, f32[16,64,128]{2,1,0:T(8,128)} %collective-permute-done.6), kind=kLoop, calls=%fused_computation.3 | loop fusion | flops 524288 | bytes 3145728 | tf_op jit(solution)/shard_map/add | solution.py:417
  75.1 7.6 %all-to-all-start = ((f32[16,64,128]{2,1,0:T(8,128)}), f32[16,64,128]{2,1,0:T(8,128)S(1)}, u32[]{:S(2)}, u32[]{:S(2)}) async-start(f32[16,64,128]{2,1,0:T(8,128)} %fusion.refs_0_), calls=%async_computation | async-start | bytes 1048576 | tf_op jit(solution)/shard_map/all_to_all | solution.py:421
  82.8 0.2 collective-permute-done.8
  83.0 0.0 collective-permute-done.7
  83.0 2.4 %add_add_fusion.refs_1_ = f32[16,64,128]{2,1,0:T(8,128)} fusion(f32[16,64,128]{2,1,0:T(8,128)} %collective-permute-done.7, f32[16,64,128]{2,1,0:T(8,128)S(1)} %collective-permute-done.8, f32[32,64,128]{2,1,0:T(8,128)} %collective-permute-done.4, f32[32,64,128]{2,1,0:T(8,128)} %copy-done.1, f32[32,64,128]{2,1,0:T(8,128)S(1)} %gather_rows.15), kind=kLoop, calls=%fused_computation.9 | loop fusion | flops 524288 | bytes 3145728 | tf_op jit(solution)/shard_map/add | solution.py:419
  85.4 7.5 %all-to-all-done.refs_0_ = f32[16,64,128]{2,1,0:T(8,128)S(1)} async-done(((f32[16,64,128]{2,1,0:T(8,128)}), f32[16,64,128]{2,1,0:T(8,128)S(1)}, u32[]{:S(2)}, u32[]{:S(2)}) %all-to-all-start) | async-done | bytes 524320 | tf_op jit(solution)/shard_map/all_to_all | solution.py:421
  92.9 3.6 %all-to-all-start.1 = ((f32[16,64,128]{2,1,0:T(8,128)}), f32[16,64,128]{2,1,0:T(8,128)S(1)}, u32[]{:S(2)}, u32[]{:S(2)}) async-start(f32[16,64,128]{2,1,0:T(8,128)} %add_add_fusion.refs_1_), calls=%async_computation.1 | async-start | bytes 1048576 | tf_op jit(solution)/shard_map/all_to_all | solution.py:421
  96.5 2.4 %collective-permute-start.9 = (f32[16,64,128]{2,1,0:T(8,128)S(1)}, f32[16,64,128]{2,1,0:T(8,128)S(1)}, u32[]{:S(2)}, u32[]{:S(2)}) collective-permute-start(f32[16,64,128]{2,1,0:T(8,128)S(1)} %all-to-all-done.refs_0_), channel_id=1, source_target_pairs={{0,16},{16,0},{32,48},{48,32},{64,80},{80,64},{96,112},{112,96},{1... | collective-permute-start | bytes 1572872 | tf_op jit(solution)/shard_map/ppermute | solution.py:422
  98.9 6.8 %all-to-all-done.1.refs_1_ = f32[16,64,128]{2,1,0:T(8,128)S(1)} async-done(((f32[16,64,128]{2,1,0:T(8,128)}), f32[16,64,128]{2,1,0:T(8,128)S(1)}, u32[]{:S(2)}, u32[]{:S(2)}) %all-to-all-start.1) | async-done | bytes 524320 | tf_op jit(solution)/shard_map/all_to_all | solution.py:421
  105.8 3.2 %collective-permute-start.10 = (f32[16,64,128]{2,1,0:T(8,128)S(1)}, f32[16,64,128]{2,1,0:T(8,128)S(1)}, u32[]{:S(2)}, u32[]{:S(2)}) collective-permute-start(f32[16,64,128]{2,1,0:T(8,128)S(1)} %all-to-all-done.1.refs_1_), channel_id=1, source_target_pairs={{0,16},{16,0},{32,48},{48,32},{64,80},{80,64},{96,112},{112,96},{1... | collective-permute-start | bytes 1572872 | tf_op jit(solution)/shard_map/ppermute | solution.py:422
  108.9 0.0 collective-permute-done.9.refs_2_
  108.9 1.5 collective-permute-done.10.refs_3_
  110.5 5.0 %partial_gram.1 = f32[4,16,32,128]{3,2,1,0:T(8,128)} custom-call(s32[1]{0:T(128)} %bitcast.13.core_ref, f32[16,64,128]{2,1,0:T(8,128)S(1)} %all-to-all-done.refs_0_, f32[16,64,128]{2,1,0:T(8,128)S(1)} %all-to-all-done.1.refs_1_, f32[16,64,128]{2,1,0:T(8,128)S(1)} %collective-permute-done.9.refs_2_, f32[16,64,128]{2,1,0:T(8,128)S(1)} %collective-permute-done.10.refs_3_), custom_call_target="tpu_custom_call" | custom-call | tf_op jit(solution)/shard_map/partial_gram/pallas_call | solution.py:273
  115.5 6.7 %all-to-all-start.2 = ((f32[64,32,128]{2,1,0:T(8,128)}), f32[64,32,128]{2,1,0:T(8,128)S(1)}, u32[]{:S(2)}, u32[]{:S(2)}) async-start(f32[64,32,128]{2,1,0:T(8,128)} %bitcast.14), calls=%async_computation.2 | async-start | bytes 2097152 | tf_op jit(solution)/shard_map/all_to_all | solution.py:431
  122.1 18.1 %all-to-all-done.2.x_ref = f32[64,32,128]{2,1,0:T(8,128)S(1)} async-done(((f32[64,32,128]{2,1,0:T(8,128)}), f32[64,32,128]{2,1,0:T(8,128)S(1)}, u32[]{:S(2)}, u32[]{:S(2)}) %all-to-all-start.2) | async-done | bytes 1048608 | tf_op jit(solution)/shard_map/all_to_all | solution.py:431
  140.2 0.2 sum_tiles.1
  140.4 1.4 collective-permute-start.11
  141.8 1.8 %diagonal_part.1.part_ref = f32[32,128]{1,0:T(8,128)S(1)} custom-call(f32[16,64,128]{2,1,0:T(8,128)} %fusion.refs_0_, f32[16,64,128]{2,1,0:T(8,128)} %add_add_fusion.refs_1_), custom_call_target="tpu_custom_call" | custom-call | flops 4000000000 | bytes 1048576 | tf_op jit(solution)/shard_map/diagonal_part/pallas_call | solution.py:311
  143.6 3.3 %collective-permute-done.11.turned_ref = f32[64,64]{1,0:T(8,128)S(1)} collective-permute-done((f32[64,64]{1,0:T(8,128)S(1)}, f32[64,64]{1,0:T(8,128)S(1)}, u32[]{:S(2)}, u32[]{:S(2)}) %collective-permute-start.11) | collective-permute-done | bytes 16416 | tf_op jit(solution)/shard_map/ppermute | solution.py:442
  146.9 0.8 messages.1
  147.7 6.0 %all-to-all-start.3 = ((f32[8,96,128]{2,1,0:T(8,128)}), f32[8,96,128]{2,1,0:T(8,128)S(1)}, u32[]{:S(2)}, u32[]{:S(2)}) async-start(f32[8,96,128]{2,1,0:T(8,128)} %messages.1), calls=%async_computation.3 | async-start | bytes 786432 | tf_op jit(solution)/shard_map/all_to_all | solution.py:443
  153.7 2.2 %copy_bitcast_fusion = f32[64,4096]{1,0:T(8,128)} fusion(f32[16,64,128]{2,1,0:T(8,128)} %add_add_fusion.refs_1_, f32[16,64,128]{2,1,0:T(8,128)} %fusion.refs_0_), kind=kLoop, calls=%fused_computation | loop fusion | flops 262144 | bytes 2097152 | tf_op jit(solution)/shard_map/reshape | solution.py:423
  155.9 5.9 %all-to-all-done.3.x_ref = f32[8,96,128]{2,1,0:T(8,128)S(1)} async-done(((f32[8,96,128]{2,1,0:T(8,128)}), f32[8,96,128]{2,1,0:T(8,128)S(1)}, u32[]{:S(2)}, u32[]{:S(2)}) %all-to-all-start.3) | async-done | bytes 393248 | tf_op jit(solution)/shard_map/all_to_all | solution.py:443
  161.8 0.9 place_tiles.1
Async XLA Ops:
  0.6 20.8 %copy-start = (s32[32768]{0:T(1024)S(1)}, s32[32768]{0:T(1024)}, u32[]{:S(2)}) copy-start(s32[32768]{0:T(1024)} %param.10) | copy-start | bytes 393220
  26.2 6.1 %collective-permute-start = (f32[32,64,128]{2,1,0:T(8,128)S(1)}, f32[32,64,128]{2,1,0:T(8,128)S(1)}, u32[]{:S(2)}, u32[]{:S(2)}) collective-permute-start(f32[32,64,128]{2,1,0:T(8,128)S(1)} %gather_rows.8.refs_0_), channel_id=1, source_target_pairs={{0,16},{16,0},{32,48},{48,32},{64,80},{80,64},{96,112},{112,96},{1... | collective-permute-start | bytes 3145736 | tf_op jit(solution)/shard_map/ppermute | solution.py:402
  33.5 32.2 %collective-permute-start.4 = (f32[32,64,128]{2,1,0:T(8,128)}, f32[32,64,128]{2,1,0:T(8,128)}, u32[]{:S(2)}, u32[]{:S(2)}) collective-permute-start(f32[32,64,128]{2,1,0:T(8,128)} %add.43.refs_0_), channel_id=1, source_target_pairs={{0,64},{16,80},{32,96},{48,112},{64,0},{80,16},{96,32},{112,48},{1... | collective-permute-start | bytes 3145736 | tf_op jit(solution)/shard_map/ppermute | solution.py:404
  41.1 5.0 %collective-permute-start.1 = (f32[32,64,128]{2,1,0:T(8,128)S(1)}, f32[32,64,128]{2,1,0:T(8,128)S(1)}, u32[]{:S(2)}, u32[]{:S(2)}) collective-permute-start(f32[32,64,128]{2,1,0:T(8,128)S(1)} %gather_rows.10.refs_0_), channel_id=1, source_target_pairs={{0,16},{16,0},{32,48},{48,32},{64,80},{80,64},{96,112},{112,96},{1... | collective-permute-start | bytes 3145736 | tf_op jit(solution)/shard_map/ppermute | solution.py:408
  47.2 24.6 %collective-permute-start.6 = (f32[16,64,128]{2,1,0:T(8,128)}, f32[16,64,128]{2,1,0:T(8,128)}, u32[]{:S(2)}, u32[]{:S(2)}) collective-permute-start(f32[16,64,128]{2,1,0:T(8,128)} %get-tuple-element.36.refs_1_), channel_id=1, source_target_pairs={{0,96},{16,112},{32,0},{48,16},{64,32},{80,48},{96,64},{112,80},{1... | collective-permute-start | bytes 1572872 | tf_op jit(solution)/shard_map/ppermute | solution.py:412
  48.0 23.8 %collective-permute-start.5 = (f32[16,64,128]{2,1,0:T(8,128)}, f32[16,64,128]{2,1,0:T(8,128)}, u32[]{:S(2)}, u32[]{:S(2)}) collective-permute-start(f32[16,64,128]{2,1,0:T(8,128)} %get-tuple-element.37.refs_0_), channel_id=1, source_target_pairs={{0,32},{16,48},{32,64},{48,80},{64,96},{80,112},{96,0},{112,16},{1... | collective-permute-start | bytes 1572872 | tf_op jit(solution)/shard_map/ppermute | solution.py:412
  53.3 5.5 %collective-permute-start.2 = (f32[32,64,128]{2,1,0:T(8,128)S(1)}, f32[32,64,128]{2,1,0:T(8,128)S(1)}, u32[]{:S(2)}, u32[]{:S(2)}) collective-permute-start(f32[32,64,128]{2,1,0:T(8,128)S(1)} %gather_rows.12.refs_0_), channel_id=1, source_target_pairs={{0,16},{16,0},{32,48},{48,32},{64,80},{80,64},{96,112},{112,96},{1... | collective-permute-start | bytes 3145736 | tf_op jit(solution)/shard_map/ppermute | solution.py:408
  59.0 24.0 %collective-permute-start.8 = (f32[16,64,128]{2,1,0:T(8,128)S(1)}, f32[16,64,128]{2,1,0:T(8,128)S(1)}, u32[]{:S(2)}, u32[]{:S(2)}) collective-permute-start(f32[16,64,128]{2,1,0:T(8,128)S(1)} %get-tuple-element.34.refs_1_), channel_id=1, source_target_pairs={{0,96},{16,112},{32,0},{48,16},{64,32},{80,48},{96,64},{112,80},{1... | collective-permute-start | bytes 1572872 | tf_op jit(solution)/shard_map/ppermute | solution.py:412
  61.1 21.9 %collective-permute-start.7 = (f32[16,64,128]{2,1,0:T(8,128)S(1)}, f32[16,64,128]{2,1,0:T(8,128)}, u32[]{:S(2)}, u32[]{:S(2)}) collective-permute-start(f32[16,64,128]{2,1,0:T(8,128)S(1)} %get-tuple-element.35.refs_0_), channel_id=1, source_target_pairs={{0,32},{16,48},{32,64},{48,80},{64,96},{80,112},{96,0},{112,16},{1... | collective-permute-start | bytes 1572872 | tf_op jit(solution)/shard_map/ppermute | solution.py:412
  65.7 6.1 %collective-permute-start.3 = (f32[32,64,128]{2,1,0:T(8,128)S(1)}, f32[32,64,128]{2,1,0:T(8,128)S(1)}, u32[]{:S(2)}, u32[]{:S(2)}) collective-permute-start(f32[32,64,128]{2,1,0:T(8,128)S(1)} %gather_rows.14.refs_0_), channel_id=1, source_target_pairs={{0,16},{16,0},{32,48},{48,32},{64,80},{80,64},{96,112},{112,96},{1... | collective-permute-start | bytes 3145736 | tf_op jit(solution)/shard_map/ppermute | solution.py:415
  71.8 1.0 copy-start.1
  75.1 17.7 %all-to-all-start = ((f32[16,64,128]{2,1,0:T(8,128)}), f32[16,64,128]{2,1,0:T(8,128)S(1)}, u32[]{:S(2)}, u32[]{:S(2)}) async-start(f32[16,64,128]{2,1,0:T(8,128)} %fusion.refs_0_), calls=%async_computation | async-start | bytes 1048576 | tf_op jit(solution)/shard_map/all_to_all | solution.py:421
  92.9 12.9 %all-to-all-start.1 = ((f32[16,64,128]{2,1,0:T(8,128)}), f32[16,64,128]{2,1,0:T(8,128)S(1)}, u32[]{:S(2)}, u32[]{:S(2)}) async-start(f32[16,64,128]{2,1,0:T(8,128)} %add_add_fusion.refs_1_), calls=%async_computation.1 | async-start | bytes 1048576 | tf_op jit(solution)/shard_map/all_to_all | solution.py:421
  96.5 12.5 %collective-permute-start.9 = (f32[16,64,128]{2,1,0:T(8,128)S(1)}, f32[16,64,128]{2,1,0:T(8,128)S(1)}, u32[]{:S(2)}, u32[]{:S(2)}) collective-permute-start(f32[16,64,128]{2,1,0:T(8,128)S(1)} %all-to-all-done.refs_0_), channel_id=1, source_target_pairs={{0,16},{16,0},{32,48},{48,32},{64,80},{80,64},{96,112},{112,96},{1... | collective-permute-start | bytes 1572872 | tf_op jit(solution)/shard_map/ppermute | solution.py:422
  105.8 4.7 %collective-permute-start.10 = (f32[16,64,128]{2,1,0:T(8,128)S(1)}, f32[16,64,128]{2,1,0:T(8,128)S(1)}, u32[]{:S(2)}, u32[]{:S(2)}) collective-permute-start(f32[16,64,128]{2,1,0:T(8,128)S(1)} %all-to-all-done.1.refs_1_), channel_id=1, source_target_pairs={{0,16},{16,0},{32,48},{48,32},{64,80},{80,64},{96,112},{112,96},{1... | collective-permute-start | bytes 1572872 | tf_op jit(solution)/shard_map/ppermute | solution.py:422
  115.5 24.8 %all-to-all-start.2 = ((f32[64,32,128]{2,1,0:T(8,128)}), f32[64,32,128]{2,1,0:T(8,128)S(1)}, u32[]{:S(2)}, u32[]{:S(2)}) async-start(f32[64,32,128]{2,1,0:T(8,128)} %bitcast.14), calls=%async_computation.2 | async-start | bytes 2097152 | tf_op jit(solution)/shard_map/all_to_all | solution.py:431
  140.4 6.4 %collective-permute-start.11 = (f32[64,64]{1,0:T(8,128)S(1)}, f32[64,64]{1,0:T(8,128)S(1)}, u32[]{:S(2)}, u32[]{:S(2)}) collective-permute-start(f32[64,64]{1,0:T(8,128)S(1)} %get-tuple-element.33), channel_id=1, source_target_pairs={{0,1},{1,2},{2,3},{3,4},{4,5},{5,6},{6,7},{7,8},{8,9},{9,10},{10,1... | collective-permute-start | bytes 49160 | tf_op jit(solution)/shard_map/ppermute | solution.py:442
  147.7 14.1 %all-to-all-start.3 = ((f32[8,96,128]{2,1,0:T(8,128)}), f32[8,96,128]{2,1,0:T(8,128)S(1)}, u32[]{:S(2)}, u32[]{:S(2)}) async-start(f32[8,96,128]{2,1,0:T(8,128)} %messages.1), calls=%async_computation.3 | async-start | bytes 786432 | tf_op jit(solution)/shard_map/all_to_all | solution.py:443

commit v9 on v8

--- a/solution.py
+++ b/solution.py
@@ -384,6 +384,30 @@
     )(me.reshape(1), tiles)
 
 
+def join_kernel(first, n_terms, *refs):
+    out_ref = refs[-1]
+    n_block = out_ref.shape[0]
+
+    @pl.loop(0, n_block)
+    def _(b):
+        total = 0.0
+        for ref in refs[:n_terms]:
+            total += ref[b + (first if ref.shape[0] > n_block else 0)]
+        out_ref[b] = total
+
+
+def join(first, count, terms, after=()):
+    vmem = pl.BlockSpec(memory_space=pltpu.VMEM)
+    return pl.pallas_call(
+        functools.partial(join_kernel, first, len(terms)),
+        out_shape=jax.ShapeDtypeStruct((count,) + terms[0].shape[1:], jnp.float32),
+        in_specs=[vmem] * len(terms) + [pl.BlockSpec(memory_space=pl.ANY)] * len(after),
+        out_specs=vmem,
+        compiler_params=pltpu.CompilerParams(vmem_limit_bytes=4 * 1024 * 1024),
+        name="join",
+    )(*terms, *after)
+
+
 def body(activations, cotangents, token_ids, signs, select):
     n_param, n_group = lax.axis_size("param"), lax.axis_size("ex")
     n_ex, _, width = activations.shape
@@ -409,14 +433,13 @@
         kept = gather_rows(table, index, 1, group, after=(sent,))
         outward = (kept[:mid] + arrived[:mid], kept[mid:] + arrived[mid:])
         near.append(
-            lax.ppermute(outward[0], "param", along(1)) + lax.ppermute(outward[1], "param", along(-1))
+            (lax.ppermute(outward[0], "param", along(1)), lax.ppermute(outward[1], "param", along(-1)))
         )
     sent = gather_rows(table, index, 0, OWN, after=outward)
     arrived = lax.ppermute(sent, "param", swap)
     own = gather_rows(table, index, 1, OWN, after=(sent,))
-    front = own[:mid] + arrived[:mid] + opposite[:mid] + near[0]
-    own, arrived, opposite, front = lax.optimization_barrier((own, arrived, opposite, front))
-    back = own[mid:] + arrived[mid:] + opposite[mid:] + near[1]
+    front = join(0, mid, (own, arrived, opposite, *near[0]))
+    back = join(mid, mid, (own, arrived, opposite, *near[1]), after=(front,))
     features = (front, back)
     shares = [lax.all_to_all(x, "ex", split_axis=0, concat_axis=0) for x in features]
     shares += [lax.ppermute(x, "param", swap) for x in shares]

time: 163 us -> 163 us (level)
  Pallas kernels: 66.6 us -> 71.4 us
  other arithmetic: 9.42 us -> 5.65 us
    pallas_call x0 -> x2, Pallas kernels: none -> 4.89 us  [join(): pl.pallas_call(functools.partial(join_kernel, first, len(terms)), out_sha...]
    add x2 -> x0, other arithmetic: 4.73 us -> none  [the longest x1 2.37 us: body(): front = own[:mid] + arrived[:mid] + opposite[:mid] + near[0]]
  transfers between devices with their start and end apart: 16 -> 16, of which waited for: 8 -> 8; matrix products, arithmetic and copies ran while one was open for 5% -> 3% of each run, Pallas kernels for 21% -> 24%
where the time goes in v9:
time: 163 us; the launch traced here: 162 us
  Pallas kernels  71.4 us (44%)
  waiting for transfers between devices  43.6 us (27%)
  starting transfers between devices  40.6 us (25%)
  other arithmetic  5.65 us (3%)
    pallas_call x8, Pallas kernels, gather_rows(): pl.pallas_call(functools.partial(gather_kernel, start), out_shape=jax.Sha...  36.9 us
    pallas_call x1, Pallas kernels, make_table(): pl.pallas_call(functools.partial(table_kernel, n_ex, width), out_shape=pl...  20.8 us
    all_to_all x1, waiting for transfers between devices, body(): lax.all_to_all(partial.reshape(n_y * n_group, rows_out, LANES), everyone,...  18.1 us
    all_to_all x2, waiting for transfers between devices, body(): lax.all_to_all(x, 'ex', split_axis=0, concat_axis=0)  13.6 us
    all_to_all x2, starting transfers between devices, body(): lax.all_to_all(x, 'ex', split_axis=0, concat_axis=0)  11.2 us
    all_to_all x1, starting transfers between devices, body(): lax.all_to_all(partial.reshape(n_y * n_group, rows_out, LANES), everyone,...  6.83 us
    all_to_all x1, starting transfers between devices, body(): lax.all_to_all(messages(tile, turned, diagonal_part(features), n_param),...  5.99 us
    all_to_all x1, waiting for transfers between devices, body(): lax.all_to_all(messages(tile, turned, diagonal_part(features), n_param),...  5.86 us
  transfers between devices with their start and end apart: 16, of which 8 were waited for; matrix products, arithmetic and copies ran while one was open for 3% of the time, Pallas kernels for 24%

profile of v9, /device:TPU:1, one launch (start us, length us, event | category | flops | bytes accessed | tf_op | source)
XLA Modules:
  0.0 162.1 jit_solution(3850243106782209635)
XLA Ops:
  0.6 0.0 copy-start
  0.6 20.8 %make_table.1.table_ref = f32[32768,128]{1,0:T(8,128)S(1)} custom-call(bf16[64,128,1024]{2,1,0:T(8,128)(2,1)} %acts_ref.1, bf16[64,64,128]{2,1,0:T(8,128)(2,1)} %bitcast.29, s32[64,128]{1,0:T(8,128)} %refs_1_.1, s32[64,1024]{1,0:T(8,128)} %refs_2_.1, bf16[256,256]{1,0:T(8,128)(2,1)} %constant.24.clone.refs_3_), custom_call_target="tpu_custom_call" | custom-call | flops 9999999827968 | bytes 33554432 | tf_op jit(solution)/shard_map/make_table/pallas_call | solution.py:142
  21.5 0.0 copy-done
  21.5 0.1 make_index.1
  21.6 4.6 %gather_rows.8.refs_0_ = f32[32,64,128]{2,1,0:T(8,128)S(1)} custom-call(s32[4096]{0:T(1024)S(1)} %bitcast.28, f32[32768,128]{1,0:T(8,128)S(1)} %make_table.1.table_ref, s32[256,128]{1,0:T(8,128)S(1)} %get-tuple-element.15.half_ref, f32[256,128]{1,0:T(8,128)S(1)} %get-tuple-element.16.sign_ref), custom_call_target="tpu_custom_call" | custom-call | flops 40960000000 | bytes 16777216 | tf_op jit(solution)/shard_map/gather_rows/pallas_call | solution.py:173
  26.2 1.5 collective-permute-start
  27.7 4.6 %gather_rows.9 = f32[32,64,128]{2,1,0:T(8,128)S(1)} custom-call(s32[4096]{0:T(1024)S(1)} %bitcast.27, f32[32768,128]{1,0:T(8,128)S(1)} %make_table.1.table_ref, s32[256,128]{1,0:T(8,128)S(1)} %get-tuple-element.15.half_ref, f32[256,128]{1,0:T(8,128)S(1)} %get-tuple-element.16.sign_ref, f32[32,64,128]{2,1,0:T(8,128)S(1)} %gather_rows.8.refs_0_), custom_call_target="tpu_custom_call" | custom-call | flops 40960000000 | bytes 16777216 | tf_op jit(solution)/shard_map/gather_rows/pallas_call | solution.py:173
  32.3 0.0 collective-permute-done
  32.3 1.1 add.19.refs_0_
  33.5 3.0 %collective-permute-start.4 = (f32[32,64,128]{2,1,0:T(8,128)}, f32[32,64,128]{2,1,0:T(8,128)}, u32[]{:S(2)}, u32[]{:S(2)}) collective-permute-start(f32[32,64,128]{2,1,0:T(8,128)} %add.19.refs_0_), channel_id=1, source_target_pairs={{0,64},{16,80},{32,96},{48,112},{64,0},{80,16},{96,32},{112,48},{1... | collective-permute-start | bytes 3145736 | tf_op jit(solution)/shard_map/ppermute | solution.py:428
  36.5 4.6 %gather_rows.10.refs_0_ = f32[32,64,128]{2,1,0:T(8,128)S(1)} custom-call(s32[4096]{0:T(1024)S(1)} %bitcast.26, f32[32768,128]{1,0:T(8,128)S(1)} %make_table.1.table_ref, s32[256,128]{1,0:T(8,128)S(1)} %get-tuple-element.15.half_ref, f32[256,128]{1,0:T(8,128)S(1)} %get-tuple-element.16.sign_ref, f32[32,64,128]{2,1,0:T(8,128)} %add.19.refs_0_), custom_call_target="tpu_custom_call" | custom-call | flops 40960000000 | bytes 16777216 | tf_op jit(solution)/shard_map/gather_rows/pallas_call | solution.py:173
  41.1 0.4 collective-permute-start.1
  41.4 4.6 %gather_rows.11 = f32[32,64,128]{2,1,0:T(8,128)S(1)} custom-call(s32[4096]{0:T(1024)S(1)} %bitcast.25, f32[32768,128]{1,0:T(8,128)S(1)} %make_table.1.table_ref, s32[256,128]{1,0:T(8,128)S(1)} %get-tuple-element.15.half_ref, f32[256,128]{1,0:T(8,128)S(1)} %get-tuple-element.16.sign_ref, f32[32,64,128]{2,1,0:T(8,128)S(1)} %gather_rows.10.refs_0_), custom_call_target="tpu_custom_call" | custom-call | flops 40960000000 | bytes 16777216 | tf_op jit(solution)/shard_map/gather_rows/pallas_call | solution.py:173
  46.1 0.0 collective-permute-done.1
  46.1 1.1 slice_add_fusion.2
  47.2 0.8 collective-permute-start.6
  48.0 0.7 collective-permute-start.5
  48.7 4.6 %gather_rows.12.refs_0_ = f32[32,64,128]{2,1,0:T(8,128)S(1)} custom-call(s32[4096]{0:T(1024)S(1)} %bitcast.24, f32[32768,128]{1,0:T(8,128)S(1)} %make_table.1.table_ref, s32[256,128]{1,0:T(8,128)S(1)} %get-tuple-element.15.half_ref, f32[256,128]{1,0:T(8,128)S(1)} %get-tuple-element.16.sign_ref, f32[16,64,128]{2,1,0:T(8,128)} %get-tuple-element.29.refs_0_, ...), custom_call_target="tpu_custom_call" | custom-call | flops 40960000000 | bytes 16777216 | tf_op jit(solution)/shard_map/gather_rows/pallas_call | solution.py:173
  53.3 0.9 collective-permute-start.2
  54.2 4.6 %gather_rows.13 = f32[32,64,128]{2,1,0:T(8,128)S(1)} custom-call(s32[4096]{0:T(1024)S(1)} %bitcast.23, f32[32768,128]{1,0:T(8,128)S(1)} %make_table.1.table_ref, s32[256,128]{1,0:T(8,128)S(1)} %get-tuple-element.15.half_ref, f32[256,128]{1,0:T(8,128)S(1)} %get-tuple-element.16.sign_ref, f32[32,64,128]{2,1,0:T(8,128)S(1)} %gather_rows.12.refs_0_), custom_call_target="tpu_custom_call" | custom-call | flops 40960000000 | bytes 16777216 | tf_op jit(solution)/shard_map/gather_rows/pallas_call | solution.py:173
  58.8 0.0 collective-permute-done.2
  58.8 1.2 slice_add_fusion
  59.9 2.0 %collective-permute-start.8 = (f32[16,64,128]{2,1,0:T(8,128)}, f32[16,64,128]{2,1,0:T(8,128)S(1)}, u32[]{:S(2)}, u32[]{:S(2)}) collective-permute-start(f32[16,64,128]{2,1,0:T(8,128)} %get-tuple-element.26.refs_1_), channel_id=1, source_target_pairs={{0,96},{16,112},{32,0},{48,16},{64,32},{80,48},{96,64},{112,80},{1... | collective-permute-start | bytes 1572872 | tf_op jit(solution)/shard_map/ppermute | solution.py:436
  62.0 0.0 collective-permute-start.7
  62.0 4.6 %gather_rows.14.refs_0_ = f32[32,64,128]{2,1,0:T(8,128)S(1)} custom-call(s32[4096]{0:T(1024)S(1)} %bitcast.22, f32[32768,128]{1,0:T(8,128)S(1)} %make_table.1.table_ref, s32[256,128]{1,0:T(8,128)S(1)} %get-tuple-element.15.half_ref, f32[256,128]{1,0:T(8,128)S(1)} %get-tuple-element.16.sign_ref, f32[16,64,128]{2,1,0:T(8,128)} %get-tuple-element.27.refs_0_, ...), custom_call_target="tpu_custom_call" | custom-call | flops 40960000000 | bytes 16777216 | tf_op jit(solution)/shard_map/gather_rows/pallas_call | solution.py:173
  66.6 0.0 collective-permute-done.4.refs_2_
  66.6 0.4 collective-permute-start.3
  67.0 4.6 %gather_rows.15.refs_0_ = f32[32,64,128]{2,1,0:T(8,128)S(1)} custom-call(s32[4096]{0:T(1024)S(1)} %bitcast.21, f32[32768,128]{1,0:T(8,128)S(1)} %make_table.1.table_ref, s32[256,128]{1,0:T(8,128)S(1)} %get-tuple-element.15.half_ref, f32[256,128]{1,0:T(8,128)S(1)} %get-tuple-element.16.sign_ref, f32[32,64,128]{2,1,0:T(8,128)S(1)} %gather_rows.14.refs_0_), custom_call_target="tpu_custom_call" | custom-call | flops 40960000000 | bytes 16777216 | tf_op jit(solution)/shard_map/gather_rows/pallas_call | solution.py:173
  71.6 0.2 collective-permute-done.6.refs_4_
  71.8 0.0 collective-permute-done.5.refs_3_
  71.8 0.0 collective-permute-done.3.refs_1_
  71.8 2.5 %join.2.refs_5_.refs_0_ = f32[16,64,128]{2,1,0:T(8,128)} custom-call(f32[32,64,128]{2,1,0:T(8,128)S(1)} %gather_rows.15.refs_0_, f32[32,64,128]{2,1,0:T(8,128)S(1)} %collective-permute-done.3.refs_1_, f32[32,64,128]{2,1,0:T(8,128)} %collective-permute-done.4.refs_2_, f32[16,64,128]{2,1,0:T(8,128)} %collective-permute-done.5.refs_3_, ...), custom_call_target="tpu_custom_call" | custom-call | tf_op jit(solution)/shard_map/join/pallas_call | solution.py:401
  74.3 7.6 %all-to-all-start = ((f32[16,64,128]{2,1,0:T(8,128)}), f32[16,64,128]{2,1,0:T(8,128)S(1)}, u32[]{:S(2)}, u32[]{:S(2)}) async-start(f32[16,64,128]{2,1,0:T(8,128)} %join.2.refs_5_.refs_0_), calls=%async_computation | async-start | bytes 1048576 | tf_op jit(solution)/shard_map/all_to_all | solution.py:444
  81.9 1.1 collective-permute-done.8.refs_4_
  83.0 0.0 collective-permute-done.7.refs_3_
  83.0 2.4 %join.3.refs_1_ = f32[16,64,128]{2,1,0:T(8,128)} custom-call(f32[32,64,128]{2,1,0:T(8,128)S(1)} %gather_rows.15.refs_0_, f32[32,64,128]{2,1,0:T(8,128)S(1)} %collective-permute-done.3.refs_1_, f32[32,64,128]{2,1,0:T(8,128)} %collective-permute-done.4.refs_2_, f32[16,64,128]{2,1,0:T(8,128)} %collective-permute-done.7.refs_3_, ...), custom_call_target="tpu_custom_call" | custom-call | tf_op jit(solution)/shard_map/join/pallas_call | solution.py:401
  85.3 6.7 %all-to-all-done.refs_0_ = f32[16,64,128]{2,1,0:T(8,128)S(1)} async-done(((f32[16,64,128]{2,1,0:T(8,128)}), f32[16,64,128]{2,1,0:T(8,128)S(1)}, u32[]{:S(2)}, u32[]{:S(2)}) %all-to-all-start) | async-done | bytes 524320 | tf_op jit(solution)/shard_map/all_to_all | solution.py:444
  92.0 3.6 %all-to-all-start.1 = ((f32[16,64,128]{2,1,0:T(8,128)}), f32[16,64,128]{2,1,0:T(8,128)S(1)}, u32[]{:S(2)}, u32[]{:S(2)}) async-start(f32[16,64,128]{2,1,0:T(8,128)} %join.3.refs_1_), calls=%async_computation.1 | async-start | bytes 1048576 | tf_op jit(solution)/shard_map/all_to_all | solution.py:444
  95.6 2.4 %collective-permute-start.9 = (f32[16,64,128]{2,1,0:T(8,128)S(1)}, f32[16,64,128]{2,1,0:T(8,128)S(1)}, u32[]{:S(2)}, u32[]{:S(2)}) collective-permute-start(f32[16,64,128]{2,1,0:T(8,128)S(1)} %all-to-all-done.refs_0_), channel_id=1, source_target_pairs={{0,16},{16,0},{32,48},{48,32},{64,80},{80,64},{96,112},{112,96},{1... | collective-permute-start | bytes 1572872 | tf_op jit(solution)/shard_map/ppermute | solution.py:445
  98.0 6.9 %all-to-all-done.1.refs_1_ = f32[16,64,128]{2,1,0:T(8,128)S(1)} async-done(((f32[16,64,128]{2,1,0:T(8,128)}), f32[16,64,128]{2,1,0:T(8,128)S(1)}, u32[]{:S(2)}, u32[]{:S(2)}) %all-to-all-start.1) | async-done | bytes 524320 | tf_op jit(solution)/shard_map/all_to_all | solution.py:444
  104.9 3.2 %collective-permute-start.10 = (f32[16,64,128]{2,1,0:T(8,128)S(1)}, f32[16,64,128]{2,1,0:T(8,128)S(1)}, u32[]{:S(2)}, u32[]{:S(2)}) collective-permute-start(f32[16,64,128]{2,1,0:T(8,128)S(1)} %all-to-all-done.1.refs_1_), channel_id=1, source_target_pairs={{0,16},{16,0},{32,48},{48,32},{64,80},{80,64},{96,112},{112,96},{1... | collective-permute-start | bytes 1572872 | tf_op jit(solution)/shard_map/ppermute | solution.py:445
  108.1 0.0 collective-permute-done.9.refs_2_
  108.1 1.5 collective-permute-done.10.refs_3_
  109.6 5.0 %partial_gram.1 = f32[4,16,32,128]{3,2,1,0:T(8,128)} custom-call(s32[1]{0:T(128)} %bitcast.13.core_ref, f32[16,64,128]{2,1,0:T(8,128)S(1)} %all-to-all-done.refs_0_, f32[16,64,128]{2,1,0:T(8,128)S(1)} %all-to-all-done.1.refs_1_, f32[16,64,128]{2,1,0:T(8,128)S(1)} %collective-permute-done.9.refs_2_, f32[16,64,128]{2,1,0:T(8,128)S(1)} %collective-permute-done.10.refs_3_), custom_call_target="tpu_custom_call" | custom-call | tf_op jit(solution)/shard_map/partial_gram/pallas_call | solution.py:273
  114.6 6.8 %all-to-all-start.2 = ((f32[64,32,128]{2,1,0:T(8,128)}), f32[64,32,128]{2,1,0:T(8,128)S(1)}, u32[]{:S(2)}, u32[]{:S(2)}) async-start(f32[64,32,128]{2,1,0:T(8,128)} %bitcast.14), calls=%async_computation.2 | async-start | bytes 2097152 | tf_op jit(solution)/shard_map/all_to_all | solution.py:454
  121.4 18.1 %all-to-all-done.2.x_ref = f32[64,32,128]{2,1,0:T(8,128)S(1)} async-done(((f32[64,32,128]{2,1,0:T(8,128)}), f32[64,32,128]{2,1,0:T(8,128)S(1)}, u32[]{:S(2)}, u32[]{:S(2)}) %all-to-all-start.2) | async-done | bytes 1048608 | tf_op jit(solution)/shard_map/all_to_all | solution.py:454
  139.6 0.2 sum_tiles.1
  139.8 1.4 collective-permute-start.11
  141.2 1.8 %diagonal_part.1.part_ref = f32[32,128]{1,0:T(8,128)S(1)} custom-call(f32[16,64,128]{2,1,0:T(8,128)} %join.2.refs_5_.refs_0_, f32[16,64,128]{2,1,0:T(8,128)} %join.3.refs_1_), custom_call_target="tpu_custom_call" | custom-call | flops 4000000000 | bytes 1048576 | tf_op jit(solution)/shard_map/diagonal_part/pallas_call | solution.py:311
  142.9 3.3 %collective-permute-done.11.turned_ref = f32[64,64]{1,0:T(8,128)S(1)} collective-permute-done((f32[64,64]{1,0:T(8,128)S(1)}, f32[64,64]{1,0:T(8,128)S(1)}, u32[]{:S(2)}, u32[]{:S(2)}) %collective-permute-start.11) | collective-permute-done | bytes 16416 | tf_op jit(solution)/shard_map/ppermute | solution.py:465
  146.2 0.8 messages.1
  147.0 6.0 %all-to-all-start.3 = ((f32[8,96,128]{2,1,0:T(8,128)}), f32[8,96,128]{2,1,0:T(8,128)S(1)}, u32[]{:S(2)}, u32[]{:S(2)}) async-start(f32[8,96,128]{2,1,0:T(8,128)} %messages.1), calls=%async_computation.3 | async-start | bytes 786432 | tf_op jit(solution)/shard_map/all_to_all | solution.py:466
  153.0 2.2 %copy_bitcast_fusion = f32[64,4096]{1,0:T(8,128)} fusion(f32[16,64,128]{2,1,0:T(8,128)} %join.3.refs_1_, f32[16,64,128]{2,1,0:T(8,128)} %join.2.refs_5_.refs_0_), kind=kLoop, calls=%fused_computation | loop fusion | flops 262144 | bytes 2097152 | tf_op jit(solution)/shard_map/reshape | solution.py:446
  155.3 5.9 %all-to-all-done.3.x_ref = f32[8,96,128]{2,1,0:T(8,128)S(1)} async-done(((f32[8,96,128]{2,1,0:T(8,128)}), f32[8,96,128]{2,1,0:T(8,128)S(1)}, u32[]{:S(2)}, u32[]{:S(2)}) %all-to-all-start.3) | async-done | bytes 393248 | tf_op jit(solution)/shard_map/all_to_all | solution.py:466
  161.1 0.9 place_tiles.1
Async XLA Ops:
  0.6 20.8 %copy-start = (s32[32768]{0:T(1024)S(1)}, s32[32768]{0:T(1024)}, u32[]{:S(2)}) copy-start(s32[32768]{0:T(1024)} %param.10) | copy-start | bytes 393220
  26.2 6.1 %collective-permute-start = (f32[32,64,128]{2,1,0:T(8,128)S(1)}, f32[32,64,128]{2,1,0:T(8,128)S(1)}, u32[]{:S(2)}, u32[]{:S(2)}) collective-permute-start(f32[32,64,128]{2,1,0:T(8,128)S(1)} %gather_rows.8.refs_0_), channel_id=1, source_target_pairs={{0,16},{16,0},{32,48},{48,32},{64,80},{80,64},{96,112},{112,96},{1... | collective-permute-start | bytes 3145736 | tf_op jit(solution)/shard_map/ppermute | solution.py:426
  33.5 33.1 %collective-permute-start.4 = (f32[32,64,128]{2,1,0:T(8,128)}, f32[32,64,128]{2,1,0:T(8,128)}, u32[]{:S(2)}, u32[]{:S(2)}) collective-permute-start(f32[32,64,128]{2,1,0:T(8,128)} %add.19.refs_0_), channel_id=1, source_target_pairs={{0,64},{16,80},{32,96},{48,112},{64,0},{80,16},{96,32},{112,48},{1... | collective-permute-start | bytes 3145736 | tf_op jit(solution)/shard_map/ppermute | solution.py:428
  41.1 5.0 %collective-permute-start.1 = (f32[32,64,128]{2,1,0:T(8,128)S(1)}, f32[32,64,128]{2,1,0:T(8,128)S(1)}, u32[]{:S(2)}, u32[]{:S(2)}) collective-permute-start(f32[32,64,128]{2,1,0:T(8,128)S(1)} %gather_rows.10.refs_0_), channel_id=1, source_target_pairs={{0,16},{16,0},{32,48},{48,32},{64,80},{80,64},{96,112},{112,96},{1... | collective-permute-start | bytes 3145736 | tf_op jit(solution)/shard_map/ppermute | solution.py:432
  47.2 24.5 %collective-permute-start.6 = (f32[16,64,128]{2,1,0:T(8,128)}, f32[16,64,128]{2,1,0:T(8,128)}, u32[]{:S(2)}, u32[]{:S(2)}) collective-permute-start(f32[16,64,128]{2,1,0:T(8,128)} %get-tuple-element.28.refs_1_), channel_id=1, source_target_pairs={{0,96},{16,112},{32,0},{48,16},{64,32},{80,48},{96,64},{112,80},{1... | collective-permute-start | bytes 1572872 | tf_op jit(solution)/shard_map/ppermute | solution.py:436
  48.0 23.7 %collective-permute-start.5 = (f32[16,64,128]{2,1,0:T(8,128)}, f32[16,64,128]{2,1,0:T(8,128)}, u32[]{:S(2)}, u32[]{:S(2)}) collective-permute-start(f32[16,64,128]{2,1,0:T(8,128)} %get-tuple-element.29.refs_0_), channel_id=1, source_target_pairs={{0,32},{16,48},{32,64},{48,80},{64,96},{80,112},{96,0},{112,16},{1... | collective-permute-start | bytes 1572872 | tf_op jit(solution)/shard_map/ppermute | solution.py:436
  53.3 5.5 %collective-permute-start.2 = (f32[32,64,128]{2,1,0:T(8,128)S(1)}, f32[32,64,128]{2,1,0:T(8,128)S(1)}, u32[]{:S(2)}, u32[]{:S(2)}) collective-permute-start(f32[32,64,128]{2,1,0:T(8,128)S(1)} %gather_rows.12.refs_0_), channel_id=1, source_target_pairs={{0,16},{16,0},{32,48},{48,32},{64,80},{80,64},{96,112},{112,96},{1... | collective-permute-start | bytes 3145736 | tf_op jit(solution)/shard_map/ppermute | solution.py:432
  59.9 23.0 %collective-permute-start.8 = (f32[16,64,128]{2,1,0:T(8,128)}, f32[16,64,128]{2,1,0:T(8,128)S(1)}, u32[]{:S(2)}, u32[]{:S(2)}) collective-permute-start(f32[16,64,128]{2,1,0:T(8,128)} %get-tuple-element.26.refs_1_), channel_id=1, source_target_pairs={{0,96},{16,112},{32,0},{48,16},{64,32},{80,48},{96,64},{112,80},{1... | collective-permute-start | bytes 1572872 | tf_op jit(solution)/shard_map/ppermute | solution.py:436
  62.0 21.0 %collective-permute-start.7 = (f32[16,64,128]{2,1,0:T(8,128)}, f32[16,64,128]{2,1,0:T(8,128)}, u32[]{:S(2)}, u32[]{:S(2)}) collective-permute-start(f32[16,64,128]{2,1,0:T(8,128)} %get-tuple-element.27.refs_0_), channel_id=1, source_target_pairs={{0,32},{16,48},{32,64},{48,80},{64,96},{80,112},{96,0},{112,16},{1... | collective-permute-start | bytes 1572872 | tf_op jit(solution)/shard_map/ppermute | solution.py:436
  66.6 5.2 %collective-permute-start.3 = (f32[32,64,128]{2,1,0:T(8,128)S(1)}, f32[32,64,128]{2,1,0:T(8,128)S(1)}, u32[]{:S(2)}, u32[]{:S(2)}) collective-permute-start(f32[32,64,128]{2,1,0:T(8,128)S(1)} %gather_rows.14.refs_0_), channel_id=1, source_target_pairs={{0,16},{16,0},{32,48},{48,32},{64,80},{80,64},{96,112},{112,96},{1... | collective-permute-start | bytes 3145736 | tf_op jit(solution)/shard_map/ppermute | solution.py:439
  74.3 17.8 %all-to-all-start = ((f32[16,64,128]{2,1,0:T(8,128)}), f32[16,64,128]{2,1,0:T(8,128)S(1)}, u32[]{:S(2)}, u32[]{:S(2)}) async-start(f32[16,64,128]{2,1,0:T(8,128)} %join.2.refs_5_.refs_0_), calls=%async_computation | async-start | bytes 1048576 | tf_op jit(solution)/shard_map/all_to_all | solution.py:444
  92.0 12.9 %all-to-all-start.1 = ((f32[16,64,128]{2,1,0:T(8,128)}), f32[16,64,128]{2,1,0:T(8,128)S(1)}, u32[]{:S(2)}, u32[]{:S(2)}) async-start(f32[16,64,128]{2,1,0:T(8,128)} %join.3.refs_1_), calls=%async_computation.1 | async-start | bytes 1048576 | tf_op jit(solution)/shard_map/all_to_all | solution.py:444
  95.6 12.5 %collective-permute-start.9 = (f32[16,64,128]{2,1,0:T(8,128)S(1)}, f32[16,64,128]{2,1,0:T(8,128)S(1)}, u32[]{:S(2)}, u32[]{:S(2)}) collective-permute-start(f32[16,64,128]{2,1,0:T(8,128)S(1)} %all-to-all-done.refs_0_), channel_id=1, source_target_pairs={{0,16},{16,0},{32,48},{48,32},{64,80},{80,64},{96,112},{112,96},{1... | collective-permute-start | bytes 1572872 | tf_op jit(solution)/shard_map/ppermute | solution.py:445
  104.9 4.7 %collective-permute-start.10 = (f32[16,64,128]{2,1,0:T(8,128)S(1)}, f32[16,64,128]{2,1,0:T(8,128)S(1)}, u32[]{:S(2)}, u32[]{:S(2)}) collective-permute-start(f32[16,64,128]{2,1,0:T(8,128)S(1)} %all-to-all-done.1.refs_1_), channel_id=1, source_target_pairs={{0,16},{16,0},{32,48},{48,32},{64,80},{80,64},{96,112},{112,96},{1... | collective-permute-start | bytes 1572872 | tf_op jit(solution)/shard_map/ppermute | solution.py:445
  114.6 24.9 %all-to-all-start.2 = ((f32[64,32,128]{2,1,0:T(8,128)}), f32[64,32,128]{2,1,0:T(8,128)S(1)}, u32[]{:S(2)}, u32[]{:S(2)}) async-start(f32[64,32,128]{2,1,0:T(8,128)} %bitcast.14), calls=%async_computation.2 | async-start | bytes 2097152 | tf_op jit(solution)/shard_map/all_to_all | solution.py:454
  139.8 6.4 %collective-permute-start.11 = (f32[64,64]{1,0:T(8,128)S(1)}, f32[64,64]{1,0:T(8,128)S(1)}, u32[]{:S(2)}, u32[]{:S(2)}) collective-permute-start(f32[64,64]{1,0:T(8,128)S(1)} %get-tuple-element.25), channel_id=1, source_target_pairs={{0,1},{1,2},{2,3},{3,4},{4,5},{5,6},{6,7},{7,8},{8,9},{9,10},{10,1... | collective-permute-start | bytes 49160 | tf_op jit(solution)/shard_map/ppermute | solution.py:465
  147.0 14.1 %all-to-all-start.3 = ((f32[8,96,128]{2,1,0:T(8,128)}), f32[8,96,128]{2,1,0:T(8,128)S(1)}, u32[]{:S(2)}, u32[]{:S(2)}) async-start(f32[8,96,128]{2,1,0:T(8,128)} %messages.1), calls=%async_computation.3 | async-start | bytes 786432 | tf_op jit(solution)/shard_map/all_to_all | solution.py:466

commit v10 on v7

--- a/solution.py
+++ b/solution.py
@@ -243,7 +243,8 @@
 
 
 def gram_kernel(n_ex, core_ref, *refs):
-    x_refs, out_ref, high_ref, low_ref, part_ref = refs[:-4], refs[-4], refs[-3], refs[-2], refs[-1]
+    x_refs = refs[:-5]
+    out_ref, high_ref, low_ref, part_ref = refs[-4:]
     core = core_ref[0]
     blocks = x_refs[0].shape[0]
     half = LANES // 2
@@ -280,20 +281,21 @@
                 out_ref[m, row_block] = jnp.where(left, top, low)
 
 
-def partial_gram(shares, core):
+def partial_gram(shares, core, after):
     blocks, n_ex, _ = shares[0].shape
     width = len(shares) * LANES
     vmem = pl.BlockSpec(memory_space=pltpu.VMEM)
     return pl.pallas_call(
         functools.partial(gram_kernel, n_ex),
         out_shape=jax.ShapeDtypeStruct((4, blocks, n_ex // 2, LANES), jnp.float32),
-        in_specs=[pl.BlockSpec(memory_space=pltpu.SMEM)] + [vmem] * len(shares),
+        in_specs=[pl.BlockSpec(memory_space=pltpu.SMEM)] + [vmem] * len(shares)
+        + [pl.BlockSpec(memory_space=pl.ANY)],
         out_specs=vmem,
         scratch_shapes=[pltpu.VMEM(((blocks + 8) * n_ex, width), jnp.bfloat16)] * 2
         + [pltpu.VMEM((12 * n_ex, 4 * n_ex), jnp.float32)],
         compiler_params=pltpu.CompilerParams(vmem_limit_bytes=16 * 1024 * 1024),
         name="partial_gram",
-    )(core.reshape(1), *shares)
+    )(core.reshape(1), *shares, after)
 
 
 def halves_side_by_side(tile):
@@ -438,7 +440,8 @@
     shares += [lax.ppermute(x, "param", swap) for x in shares]
     whole_features = jnp.swapaxes(jnp.concatenate(features, axis=0), 0, 1).reshape(n_ex, -1)
 
-    partial = partial_gram(shares, me % 2)
+    own_part = diagonal_part(features)
+    partial = partial_gram(shares, me % 2, own_part)
     rows_out = partial.shape[2]
     everyone = ("param", "ex")
     alike = [
@@ -457,7 +460,7 @@
     ]
     turned = lax.ppermute(turned, everyone, onward)
     spread = lax.all_to_all(
-        messages(tile, turned, diagonal_part(features), n_param), "param", split_axis=0, concat_axis=0
+        messages(tile, turned, own_part, n_param), "param", split_axis=0, concat_axis=0
     )
     gram = place_tiles(spread, lax.axis_index("ex"), n_ex, n_group)
     return (whole_features, gram)

time: 161 us -> 160 us (level)
  blocking collectives: 0 us -> 23.4 us
  waiting for transfers between devices: 43.9 us -> 26.3 us
  starting transfers between devices: 42.2 us -> 36.4 us
    all_to_all x0 -> x1, blocking collectives: none -> 23.4 us  [body(): lax.all_to_all(partial.reshape(n_y * n_group, rows_out, LANES), everyone,...]
    all_to_all x2 -> x1, waiting for transfers between devices: 24 us -> 5.86 us  [body(): lax.all_to_all(messages(tile, turned, own_part, n_param), 'param', split_...]
    all_to_all x2 -> x1, starting transfers between devices: 11.2 us -> 5.67 us  [body(): lax.all_to_all(messages(tile, turned, own_part, n_param), 'param', split_...]
    ppermute x1, waiting for transfers between devices: 3.28 us -> 5.25 us  [body(): turned = lax.ppermute(turned, everyone, onward)]
  transfers between devices with their start and end apart: 17 -> 16, of which waited for: 8 -> 6; matrix products, arithmetic and copies ran while one was open for 4% -> 4% of each run, Pallas kernels for 21% -> 22%
where the time goes in v10:
time: 160 us
  Pallas kernels  65.9 us (41%)
  starting transfers between devices  36.4 us (23%)
  waiting for transfers between devices  26.3 us (16%)
  blocking collectives  23.4 us (15%)
  other arithmetic  6.64 us (4%)
    pallas_call x8, Pallas kernels, gather_rows(): pl.pallas_call(kernel, out_shape=jax.ShapeDtypeStruct((n_block, LANES //...  37.2 us
    all_to_all x1, blocking collectives, body(): lax.all_to_all(partial.reshape(n_y * n_group, rows_out, LANES), everyone,...  23.4 us
    pallas_call x1, Pallas kernels, make_table(): pl.pallas_call(functools.partial(table_kernel, n_ex, width), out_shape=pl...  20.8 us
    all_to_all x2, starting transfers between devices, body(): lax.all_to_all(x, 'ex', split_axis=0, concat_axis=0)  11.2 us
    all_to_all x2, waiting for transfers between devices, body(): lax.all_to_all(x, 'ex', split_axis=0, concat_axis=0)  10.4 us
    ppermute x3, starting transfers between devices, body(): lax.ppermute(outward[1], 'param', along(-1))  8.59 us
    ppermute x2, starting transfers between devices, body(): shares += [lax.ppermute(x, 'param', swap) for x in shares]  7.3 us
    all_to_all x1, waiting for transfers between devices, body(): lax.all_to_all(messages(tile, turned, own_part, n_param), 'param', split_...  5.86 us
  transfers between devices with their start and end apart: 16, of which 6 were waited for; matrix products, arithmetic and copies ran while one was open for 4% of the time, Pallas kernels for 22%

profile of v10, /device:TPU:1, one launch (start us, length us, event | category | flops | bytes accessed | tf_op | source)
XLA Modules:
  0.0 159.5 jit_solution(977211562755789377)
XLA Ops:
  0.6 0.0 copy-start
  0.6 20.8 %make_table.1.table_ref.refs_1_ = f32[32768,128]{1,0:T(8,128)S(1)} custom-call(bf16[64,128,1024]{2,1,0:T(8,128)(2,1)} %acts_ref.1, bf16[64,64,128]{2,1,0:T(8,128)(2,1)} %bitcast.30, s32[64,128]{1,0:T(8,128)} %refs_1_.1, s32[64,1024]{1,0:T(8,128)} %refs_2_.1, bf16[256,256]{1,0:T(8,128)(2,1)} %constant.24.clone.refs_3_), custom_call_target="tpu_custom_call" | custom-call | flops 9999999827968 | bytes 33554432 | tf_op jit(solution)/shard_map/make_table/pallas_call | solution.py:144
  21.5 0.0 copy-done
  21.5 0.1 make_index.1
  21.6 4.6 %gather_rows.8.refs_4_ = f32[32,64,128]{2,1,0:T(8,128)S(1)} custom-call(s32[4096]{0:T(1024)S(1)} %bitcast.29, f32[32768,128]{1,0:T(8,128)S(1)} %make_table.1.table_ref.refs_1_, s32[256,128]{1,0:T(8,128)S(1)} %get-tuple-element.18.refs_2_, f32[256,128]{1,0:T(8,128)S(1)} %get-tuple-element.19.refs_3_), custom_call_target="tpu_custom_call" | custom-call | flops 40960000000 | bytes 16777216 | tf_op jit(solution)/shard_map/gather_rows/pallas_call | solution.py:188
  26.2 1.5 collective-permute-start
  27.7 4.6 %gather_rows.9 = f32[32,64,128]{2,1,0:T(8,128)S(1)} custom-call(s32[4096]{0:T(1024)S(1)} %bitcast.28, f32[32768,128]{1,0:T(8,128)S(1)} %make_table.1.table_ref.refs_1_, s32[256,128]{1,0:T(8,128)S(1)} %get-tuple-element.18.refs_2_, f32[256,128]{1,0:T(8,128)S(1)} %get-tuple-element.19.refs_3_, f32[32,64,128]{2,1,0:T(8,128)S(1)} %gather_rows.8.refs_4_), custom_call_target="tpu_custom_call" | custom-call | flops 40960000000 | bytes 16777216 | tf_op jit(solution)/shard_map/gather_rows/pallas_call | solution.py:188
  32.3 0.0 collective-permute-done
  32.4 1.0 slice_add_fusion.6
  33.3 2.8 %collective-permute-start.1 = (f32[16,64,128]{2,1,0:T(8,128)}, f32[16,64,128]{2,1,0:T(8,128)}, u32[]{:S(2)}, u32[]{:S(2)}) collective-permute-start(f32[16,64,128]{2,1,0:T(8,128)} %get-tuple-element.36.refs_5_), channel_id=1, source_target_pairs={{0,96},{16,112},{32,0},{48,16},{64,32},{80,48},{96,64},{112,80},{1... | collective-permute-start | bytes 1572872 | tf_op jit(solution)/shard_map/ppermute | solution.py:421
  36.1 0.0 collective-permute-start.2
  36.1 4.6 %gather_rows.10.refs_4_ = f32[32,64,128]{2,1,0:T(8,128)S(1)} custom-call(s32[4096]{0:T(1024)S(1)} %bitcast.27, f32[32768,128]{1,0:T(8,128)S(1)} %make_table.1.table_ref.refs_1_, s32[256,128]{1,0:T(8,128)S(1)} %get-tuple-element.18.refs_2_, f32[256,128]{1,0:T(8,128)S(1)} %get-tuple-element.19.refs_3_, f32[16,64,128]{2,1,0:T(8,128)S(1)} %get-tuple-element.37.refs_4_, ...), custom_call_target="tpu_custom_call" | custom-call | flops 40960000000 | bytes 16777216 | tf_op jit(solution)/shard_map/gather_rows/pallas_call | solution.py:188
  40.7 0.4 collective-permute-start.3
  41.1 4.6 %gather_rows.11.refs_4_ = f32[32,64,128]{2,1,0:T(8,128)S(1)} custom-call(s32[4096]{0:T(1024)S(1)} %bitcast.26, f32[32768,128]{1,0:T(8,128)S(1)} %make_table.1.table_ref.refs_1_, s32[256,128]{1,0:T(8,128)S(1)} %get-tuple-element.18.refs_2_, f32[256,128]{1,0:T(8,128)S(1)} %get-tuple-element.19.refs_3_, f32[32,64,128]{2,1,0:T(8,128)S(1)} %gather_rows.10.refs_4_), custom_call_target="tpu_custom_call" | custom-call | flops 40960000000 | bytes 16777216 | tf_op jit(solution)/shard_map/gather_rows/pallas_call | solution.py:188
  45.7 0.3 collective-permute-start.4
  46.0 4.6 %gather_rows.12.refs_5_ = f32[32,64,128]{2,1,0:T(8,128)S(1)} custom-call(s32[4096]{0:T(1024)S(1)} %bitcast.25, f32[32768,128]{1,0:T(8,128)S(1)} %make_table.1.table_ref.refs_1_, s32[256,128]{1,0:T(8,128)S(1)} %get-tuple-element.18.refs_2_, f32[256,128]{1,0:T(8,128)S(1)} %get-tuple-element.19.refs_3_, f32[32,64,128]{2,1,0:T(8,128)S(1)} %gather_rows.11.refs_4_), custom_call_target="tpu_custom_call" | custom-call | flops 40960000000 | bytes 16777216 | tf_op jit(solution)/shard_map/gather_rows/pallas_call | solution.py:188
  50.6 0.4 collective-permute-start.5
  51.0 0.0 collective-permute-done.2.refs_4_
  51.0 4.6 %gather_rows.13 = f32[32,64,128]{2,1,0:T(8,128)S(1)} custom-call(s32[4096]{0:T(1024)S(1)} %bitcast.24, f32[32768,128]{1,0:T(8,128)S(1)} %make_table.1.table_ref.refs_1_, s32[256,128]{1,0:T(8,128)S(1)} %get-tuple-element.18.refs_2_, f32[256,128]{1,0:T(8,128)S(1)} %get-tuple-element.19.refs_3_, f32[16,64,128]{2,1,0:T(8,128)S(1)} %collective-permute-done.2.refs_4_, ...), custom_call_target="tpu_custom_call" | custom-call | flops 40960000000 | bytes 16777216 | tf_op jit(solution)/shard_map/gather_rows/pallas_call | solution.py:188
  55.7 0.0 collective-permute-done.3
  55.7 0.2 slice_add_fusion.3
  55.9 3.0 %collective-permute-start.7 = (f32[16,64,128]{2,1,0:T(8,128)S(1)}, f32[16,64,128]{2,1,0:T(8,128)S(1)}, u32[]{:S(2)}, u32[]{:S(2)}) collective-permute-start(f32[16,64,128]{2,1,0:T(8,128)S(1)} %get-tuple-element.34.refs_6_), channel_id=1, source_target_pairs={{0,96},{16,112},{32,0},{48,16},{64,32},{80,48},{96,64},{112,80},{1... | collective-permute-start | bytes 1572872 | tf_op jit(solution)/shard_map/ppermute | solution.py:430
  58.9 0.0 collective-permute-start.6
  58.9 0.0 collective-permute-done.1.refs_4_
  58.9 4.9 %gather_rows.14 = f32[32,64,128]{2,1,0:T(8,128)S(1)} custom-call(s32[4096]{0:T(1024)S(1)} %bitcast.23, f32[32768,128]{1,0:T(8,128)S(1)} %make_table.1.table_ref.refs_1_, s32[256,128]{1,0:T(8,128)S(1)} %get-tuple-element.18.refs_2_, f32[256,128]{1,0:T(8,128)S(1)} %get-tuple-element.19.refs_3_, f32[16,64,128]{2,1,0:T(8,128)} %collective-permute-done.1.refs_4_, ...), custom_call_target="tpu_custom_call" | custom-call | flops 40960000000 | bytes 16777216 | tf_op jit(solution)/shard_map/gather_rows/pallas_call | solution.py:188
  63.8 0.0 collective-permute-done.4
  63.8 0.2 slice_add_fusion.2
  64.0 2.7 %collective-permute-start.9 = (f32[16,64,128]{2,1,0:T(8,128)S(1)}, f32[16,64,128]{2,1,0:T(8,128)S(1)}, u32[]{:S(2)}, u32[]{:S(2)}) collective-permute-start(f32[16,64,128]{2,1,0:T(8,128)S(1)} %get-tuple-element.33.refs_5_), channel_id=1, source_target_pairs={{0,96},{16,112},{32,0},{48,16},{64,32},{80,48},{96,64},{112,80},{1... | collective-permute-start | bytes 1572872 | tf_op jit(solution)/shard_map/ppermute | solution.py:433
  66.7 0.0 collective-permute-start.8
  66.7 4.6 %gather_rows.15 = f32[32,64,128]{2,1,0:T(8,128)S(1)} custom-call(s32[4096]{0:T(1024)S(1)} %bitcast.22, f32[32768,128]{1,0:T(8,128)S(1)} %make_table.1.table_ref.refs_1_, s32[256,128]{1,0:T(8,128)S(1)} %get-tuple-element.18.refs_2_, f32[256,128]{1,0:T(8,128)S(1)} %get-tuple-element.19.refs_3_, f32[16,64,128]{2,1,0:T(8,128)S(1)} %get-tuple-element.32.refs_4_, ...), custom_call_target="tpu_custom_call" | custom-call | flops 40960000000 | bytes 16777216 | tf_op jit(solution)/shard_map/gather_rows/pallas_call | solution.py:188
  71.3 0.0 collective-permute-done.5
  71.4 0.0 copy-start.1
  71.4 0.0 collective-permute-done.7
  71.4 1.9 %collective-permute-done.6 = f32[16,64,128]{2,1,0:T(8,128)S(1)} collective-permute-done((f32[16,64,128]{2,1,0:T(8,128)S(1)}, f32[16,64,128]{2,1,0:T(8,128)S(1)}, u32[]{:S(2)}, u32[]{:S(2)}) %collective-permute-start.6) | collective-permute-done | bytes 524320 | tf_op jit(solution)/shard_map/ppermute | solution.py:430
  73.3 0.0 copy-done.1
  73.3 0.9 fusion.1.refs_0_
  74.3 7.6 %all-to-all-start = ((f32[16,64,128]{2,1,0:T(8,128)}), f32[16,64,128]{2,1,0:T(8,128)S(1)}, u32[]{:S(2)}, u32[]{:S(2)}) async-start(f32[16,64,128]{2,1,0:T(8,128)} %fusion.1.refs_0_), calls=%async_computation | async-start | bytes 1048576 | tf_op jit(solution)/shard_map/all_to_all | solution.py:439
  81.9 0.0 collective-permute-done.9
  81.9 2.8 %collective-permute-done.8 = f32[16,64,128]{2,1,0:T(8,128)} collective-permute-done((f32[16,64,128]{2,1,0:T(8,128)S(1)}, f32[16,64,128]{2,1,0:T(8,128)}, u32[]{:S(2)}, u32[]{:S(2)}) %collective-permute-start.8) | collective-permute-done | bytes 524320 | tf_op jit(solution)/shard_map/ppermute | solution.py:433
  84.7 2.1 %add_add_fusion.refs_1_ = f32[16,64,128]{2,1,0:T(8,128)} fusion(f32[16,64,128]{2,1,0:T(8,128)S(1)} %collective-permute-done.9, f32[16,64,128]{2,1,0:T(8,128)} %collective-permute-done.8, f32[32,64,128]{2,1,0:T(8,128)} %copy-done.1, f32[32,64,128]{2,1,0:T(8,128)S(1)} %gather_rows.15), kind=kLoop, calls=%fused_computation.11 | loop fusion | flops 393216 | bytes 2621440 | tf_op jit(solution)/shard_map/add | solution.py:437
  86.8 4.6 %all-to-all-done.refs_0_ = f32[16,64,128]{2,1,0:T(8,128)S(1)} async-done(((f32[16,64,128]{2,1,0:T(8,128)}), f32[16,64,128]{2,1,0:T(8,128)S(1)}, u32[]{:S(2)}, u32[]{:S(2)}) %all-to-all-start) | async-done | bytes 524320 | tf_op jit(solution)/shard_map/all_to_all | solution.py:439
  91.4 3.6 %all-to-all-start.1 = ((f32[16,64,128]{2,1,0:T(8,128)}), f32[16,64,128]{2,1,0:T(8,128)S(1)}, u32[]{:S(2)}, u32[]{:S(2)}) async-start(f32[16,64,128]{2,1,0:T(8,128)} %add_add_fusion.refs_1_), calls=%async_computation.1 | async-start | bytes 1048576 | tf_op jit(solution)/shard_map/all_to_all | solution.py:439
  95.0 3.1 %collective-permute-start.10 = (f32[16,64,128]{2,1,0:T(8,128)S(1)}, f32[16,64,128]{2,1,0:T(8,128)S(1)}, u32[]{:S(2)}, u32[]{:S(2)}) collective-permute-start(f32[16,64,128]{2,1,0:T(8,128)S(1)} %all-to-all-done.refs_0_), channel_id=1, source_target_pairs={{0,16},{16,0},{32,48},{48,32},{64,80},{80,64},{96,112},{112,96},{1... | collective-permute-start | bytes 1572872 | tf_op jit(solution)/shard_map/ppermute | solution.py:440
  98.1 5.8 %all-to-all-done.1.refs_1_ = f32[16,64,128]{2,1,0:T(8,128)S(1)} async-done(((f32[16,64,128]{2,1,0:T(8,128)}), f32[16,64,128]{2,1,0:T(8,128)S(1)}, u32[]{:S(2)}, u32[]{:S(2)}) %all-to-all-start.1) | async-done | bytes 524320 | tf_op jit(solution)/shard_map/all_to_all | solution.py:439
  103.9 4.2 %collective-permute-start.11 = (f32[16,64,128]{2,1,0:T(8,128)S(1)}, f32[16,64,128]{2,1,0:T(8,128)S(1)}, u32[]{:S(2)}, u32[]{:S(2)}) collective-permute-start(f32[16,64,128]{2,1,0:T(8,128)S(1)} %all-to-all-done.1.refs_1_), channel_id=1, source_target_pairs={{0,16},{16,0},{32,48},{48,32},{64,80},{80,64},{96,112},{112,96},{1... | collective-permute-start | bytes 1572872 | tf_op jit(solution)/shard_map/ppermute | solution.py:440
  108.1 1.8 %diagonal_part.1.refs_4_.part_ref = f32[32,128]{1,0:T(8,128)S(1)} custom-call(f32[16,64,128]{2,1,0:T(8,128)} %fusion.1.refs_0_, f32[16,64,128]{2,1,0:T(8,128)} %add_add_fusion.refs_1_), custom_call_target="tpu_custom_call" | custom-call | flops 4000000000 | bytes 1048576 | tf_op jit(solution)/shard_map/diagonal_part/pallas_call | solution.py:327
  109.9 0.0 collective-permute-done.10.refs_2_
  109.9 0.0 collective-permute-done.11.refs_3_
  109.9 4.0 %partial_gram.1 = f32[4,16,32,128]{3,2,1,0:T(8,128)S(1)} custom-call(s32[1]{0:T(128)} %bitcast.13.core_ref, f32[16,64,128]{2,1,0:T(8,128)S(1)} %all-to-all-done.refs_0_, f32[16,64,128]{2,1,0:T(8,128)S(1)} %all-to-all-done.1.refs_1_, f32[16,64,128]{2,1,0:T(8,128)S(1)} %collective-permute-done.10.refs_2_, f32[16,64,128]{2,1,0:T(8,128)S(1)} %collective-permute-done.11.refs_3_, ...), custom_call_target="tpu_custom_call" | custom-call | tf_op jit(solution)/shard_map/partial_gram/pallas_call | solution.py:288
  113.9 23.4 %all_to_all.20.x_ref = f32[64,32,128]{2,1,0:T(8,128)S(1)} all-to-all(f32[64,32,128]{2,1,0:T(8,128)S(1)} %bitcast.20), channel_id=1, replica_groups={{0,1,2,3,4,5,6,7,8,9,10,11,12,13,14,15,32,33,34,35,36,37,38,39,40,41,42..., dimensions={0} | all-to-all | bytes 2097152 | tf_op jit(solution)/shard_map/all_to_all | solution.py:450
  137.3 0.2 sum_tiles.1
  137.6 1.2 collective-permute-start.12
  138.7 5.3 %collective-permute-done.12.turned_ref = f32[64,64]{1,0:T(8,128)S(1)} collective-permute-done((f32[64,64]{1,0:T(8,128)S(1)}, f32[64,64]{1,0:T(8,128)S(1)}, u32[]{:S(2)}, u32[]{:S(2)}) %collective-permute-start.12) | collective-permute-done | bytes 16416 | tf_op jit(solution)/shard_map/ppermute | solution.py:461
  144.0 0.8 messages.1
  144.8 5.7 %all-to-all-start.3 = ((f32[8,96,128]{2,1,0:T(8,128)}), f32[8,96,128]{2,1,0:T(8,128)S(1)}, u32[]{:S(2)}, u32[]{:S(2)}) async-start(f32[8,96,128]{2,1,0:T(8,128)} %messages.1), calls=%async_computation.3 | async-start | bytes 786432 | tf_op jit(solution)/shard_map/all_to_all | solution.py:462
  150.5 2.2 %copy_bitcast_fusion = f32[64,4096]{1,0:T(8,128)} fusion(f32[16,64,128]{2,1,0:T(8,128)} %add_add_fusion.refs_1_, f32[16,64,128]{2,1,0:T(8,128)} %fusion.1.refs_0_), kind=kLoop, calls=%fused_computation | loop fusion | flops 262144 | bytes 2097152 | tf_op jit(solution)/shard_map/reshape | solution.py:441
  152.7 5.9 %all-to-all-done.3.x_ref = f32[8,96,128]{2,1,0:T(8,128)S(1)} async-done(((f32[8,96,128]{2,1,0:T(8,128)}), f32[8,96,128]{2,1,0:T(8,128)S(1)}, u32[]{:S(2)}, u32[]{:S(2)}) %all-to-all-start.3) | async-done | bytes 393248 | tf_op jit(solution)/shard_map/all_to_all | solution.py:462
  158.6 0.9 place_tiles.1
Async XLA Ops:
  0.6 20.8 %copy-start = (s32[32768]{0:T(1024)S(1)}, s32[32768]{0:T(1024)}, u32[]{:S(2)}) copy-start(s32[32768]{0:T(1024)} %param.10) | copy-start | bytes 393220
  26.2 6.1 %collective-permute-start = (f32[32,64,128]{2,1,0:T(8,128)S(1)}, f32[32,64,128]{2,1,0:T(8,128)S(1)}, u32[]{:S(2)}, u32[]{:S(2)}) collective-permute-start(f32[32,64,128]{2,1,0:T(8,128)S(1)} %gather_rows.8.refs_4_), channel_id=1, source_target_pairs={{0,16},{16,0},{32,48},{48,32},{64,80},{80,64},{96,112},{112,96},{1... | collective-permute-start | bytes 3145736 | tf_op jit(solution)/shard_map/ppermute | solution.py:418
  33.3 25.6 %collective-permute-start.1 = (f32[16,64,128]{2,1,0:T(8,128)}, f32[16,64,128]{2,1,0:T(8,128)}, u32[]{:S(2)}, u32[]{:S(2)}) collective-permute-start(f32[16,64,128]{2,1,0:T(8,128)} %get-tuple-element.36.refs_5_), channel_id=1, source_target_pairs={{0,96},{16,112},{32,0},{48,16},{64,32},{80,48},{96,64},{112,80},{1... | collective-permute-start | bytes 1572872 | tf_op jit(solution)/shard_map/ppermute | solution.py:421
  36.1 14.9 %collective-permute-start.2 = (f32[16,64,128]{2,1,0:T(8,128)S(1)}, f32[16,64,128]{2,1,0:T(8,128)S(1)}, u32[]{:S(2)}, u32[]{:S(2)}) collective-permute-start(f32[16,64,128]{2,1,0:T(8,128)S(1)} %get-tuple-element.37.refs_4_), channel_id=1, source_target_pairs={{0,32},{16,48},{32,64},{48,80},{64,96},{80,112},{96,0},{112,16},{1... | collective-permute-start | bytes 1572872 | tf_op jit(solution)/shard_map/ppermute | solution.py:421
  40.7 14.9 %collective-permute-start.3 = (f32[32,64,128]{2,1,0:T(8,128)S(1)}, f32[32,64,128]{2,1,0:T(8,128)S(1)}, u32[]{:S(2)}, u32[]{:S(2)}) collective-permute-start(f32[32,64,128]{2,1,0:T(8,128)S(1)} %gather_rows.10.refs_4_), channel_id=1, source_target_pairs={{0,16},{16,0},{32,48},{48,32},{64,80},{80,64},{96,112},{112,96},{1... | collective-permute-start | bytes 3145736 | tf_op jit(solution)/shard_map/ppermute | solution.py:423
  45.7 18.1 %collective-permute-start.4 = (f32[32,64,128]{2,1,0:T(8,128)S(1)}, f32[32,64,128]{2,1,0:T(8,128)S(1)}, u32[]{:S(2)}, u32[]{:S(2)}) collective-permute-start(f32[32,64,128]{2,1,0:T(8,128)S(1)} %gather_rows.11.refs_4_), channel_id=1, source_target_pairs={{0,16},{16,0},{32,48},{48,32},{64,80},{80,64},{96,112},{112,96},{1... | collective-permute-start | bytes 3145736 | tf_op jit(solution)/shard_map/ppermute | solution.py:425
  50.6 20.7 %collective-permute-start.5 = (f32[32,64,128]{2,1,0:T(8,128)S(1)}, f32[32,64,128]{2,1,0:T(8,128)S(1)}, u32[]{:S(2)}, u32[]{:S(2)}) collective-permute-start(f32[32,64,128]{2,1,0:T(8,128)S(1)} %gather_rows.12.refs_5_), channel_id=1, source_target_pairs={{0,16},{16,0},{32,48},{48,32},{64,80},{80,64},{96,112},{112,96},{1... | collective-permute-start | bytes 3145736 | tf_op jit(solution)/shard_map/ppermute | solution.py:427
  55.9 15.5 %collective-permute-start.7 = (f32[16,64,128]{2,1,0:T(8,128)S(1)}, f32[16,64,128]{2,1,0:T(8,128)S(1)}, u32[]{:S(2)}, u32[]{:S(2)}) collective-permute-start(f32[16,64,128]{2,1,0:T(8,128)S(1)} %get-tuple-element.34.refs_6_), channel_id=1, source_target_pairs={{0,96},{16,112},{32,0},{48,16},{64,32},{80,48},{96,64},{112,80},{1... | collective-permute-start | bytes 1572872 | tf_op jit(solution)/shard_map/ppermute | solution.py:430
  58.9 14.4 %collective-permute-start.6 = (f32[16,64,128]{2,1,0:T(8,128)S(1)}, f32[16,64,128]{2,1,0:T(8,128)S(1)}, u32[]{:S(2)}, u32[]{:S(2)}) collective-permute-start(f32[16,64,128]{2,1,0:T(8,128)S(1)} %get-tuple-element.35.refs_5_), channel_id=1, source_target_pairs={{0,32},{16,48},{32,64},{48,80},{64,96},{80,112},{96,0},{112,16},{1... | collective-permute-start | bytes 1572872 | tf_op jit(solution)/shard_map/ppermute | solution.py:430
  64.0 17.9 %collective-permute-start.9 = (f32[16,64,128]{2,1,0:T(8,128)S(1)}, f32[16,64,128]{2,1,0:T(8,128)S(1)}, u32[]{:S(2)}, u32[]{:S(2)}) collective-permute-start(f32[16,64,128]{2,1,0:T(8,128)S(1)} %get-tuple-element.33.refs_5_), channel_id=1, source_target_pairs={{0,96},{16,112},{32,0},{48,16},{64,32},{80,48},{96,64},{112,80},{1... | collective-permute-start | bytes 1572872 | tf_op jit(solution)/shard_map/ppermute | solution.py:433
  66.7 17.9 %collective-permute-start.8 = (f32[16,64,128]{2,1,0:T(8,128)S(1)}, f32[16,64,128]{2,1,0:T(8,128)}, u32[]{:S(2)}, u32[]{:S(2)}) collective-permute-start(f32[16,64,128]{2,1,0:T(8,128)S(1)} %get-tuple-element.32.refs_4_), channel_id=1, source_target_pairs={{0,32},{16,48},{32,64},{48,80},{64,96},{80,112},{96,0},{112,16},{1... | collective-permute-start | bytes 1572872 | tf_op jit(solution)/shard_map/ppermute | solution.py:433
  71.4 2.0 %copy-start.1 = (f32[32,64,128]{2,1,0:T(8,128)}, f32[32,64,128]{2,1,0:T(8,128)S(1)}, u32[]{:S(2)}) copy-start(f32[32,64,128]{2,1,0:T(8,128)S(1)} %collective-permute-done.5) | copy-start | bytes 3145732
  74.3 17.1 %all-to-all-start = ((f32[16,64,128]{2,1,0:T(8,128)}), f32[16,64,128]{2,1,0:T(8,128)S(1)}, u32[]{:S(2)}, u32[]{:S(2)}) async-start(f32[16,64,128]{2,1,0:T(8,128)} %fusion.1.refs_0_), calls=%async_computation | async-start | bytes 1048576 | tf_op jit(solution)/shard_map/all_to_all | solution.py:439
  91.4 12.5 %all-to-all-start.1 = ((f32[16,64,128]{2,1,0:T(8,128)}), f32[16,64,128]{2,1,0:T(8,128)S(1)}, u32[]{:S(2)}, u32[]{:S(2)}) async-start(f32[16,64,128]{2,1,0:T(8,128)} %add_add_fusion.refs_1_), calls=%async_computation.1 | async-start | bytes 1048576 | tf_op jit(solution)/shard_map/all_to_all | solution.py:439
  95.0 14.9 %collective-permute-start.10 = (f32[16,64,128]{2,1,0:T(8,128)S(1)}, f32[16,64,128]{2,1,0:T(8,128)S(1)}, u32[]{:S(2)}, u32[]{:S(2)}) collective-permute-start(f32[16,64,128]{2,1,0:T(8,128)S(1)} %all-to-all-done.refs_0_), channel_id=1, source_target_pairs={{0,16},{16,0},{32,48},{48,32},{64,80},{80,64},{96,112},{112,96},{1... | collective-permute-start | bytes 1572872 | tf_op jit(solution)/shard_map/ppermute | solution.py:440
  103.9 6.0 %collective-permute-start.11 = (f32[16,64,128]{2,1,0:T(8,128)S(1)}, f32[16,64,128]{2,1,0:T(8,128)S(1)}, u32[]{:S(2)}, u32[]{:S(2)}) collective-permute-start(f32[16,64,128]{2,1,0:T(8,128)S(1)} %all-to-all-done.1.refs_1_), channel_id=1, source_target_pairs={{0,16},{16,0},{32,48},{48,32},{64,80},{80,64},{96,112},{112,96},{1... | collective-permute-start | bytes 1572872 | tf_op jit(solution)/shard_map/ppermute | solution.py:440
  137.6 6.4 %collective-permute-start.12 = (f32[64,64]{1,0:T(8,128)S(1)}, f32[64,64]{1,0:T(8,128)S(1)}, u32[]{:S(2)}, u32[]{:S(2)}) collective-permute-start(f32[64,64]{1,0:T(8,128)S(1)} %get-tuple-element.31), channel_id=1, source_target_pairs={{0,1},{1,2},{2,3},{3,4},{4,5},{5,6},{6,7},{7,8},{8,9},{9,10},{10,1... | collective-permute-start | bytes 49160 | tf_op jit(solution)/shard_map/ppermute | solution.py:461
  144.8 13.8 %all-to-all-start.3 = ((f32[8,96,128]{2,1,0:T(8,128)}), f32[8,96,128]{2,1,0:T(8,128)S(1)}, u32[]{:S(2)}, u32[]{:S(2)}) async-start(f32[8,96,128]{2,1,0:T(8,128)} %messages.1), calls=%async_computation.3 | async-start | bytes 786432 | tf_op jit(solution)/shard_map/all_to_all | solution.py:462
